TPU v7x, 32 devices: a whole 2x2x4 slice. The times are simulated.
32 devices in a mesh: node: 16 (over z, y, core), local: 2 (over x).
Axes of the slice: x: 2, y: 2, z: 4, core: 2. Of those that a mesh axis runs over, the one named last changes fastest.
Arguments:
- block_input: bfloat16 [12544, 512], P(('node', 'local')), may hold values from 0 to 2
- conv_weight: bfloat16 [512, 2048], replicated, may hold values from -0.25 to 0.25
- bn_gain: float32 [2048], replicated, may hold values from 0.1 to 1.9
- out_cotangent: bfloat16 [12544, 2048], P(('node', 'local')), may hold values from -0.109375 to 0.109375
- master_weight: float32 [2048, 512], P('node'), may hold values from -0.25 to 0.25
- velocity: float32 [2048, 512], P('node'), may hold values from -6 to 6
Outputs:
- new_velocity: float32 [2048, 512], P('node')
- new_weight: float32 [2048, 512], P('node')
All inputs are finite; a program needn't handle non-finite values.
Results may differ from a plain program's by a relative error of at most 0.0095.
Values may be sent and summed in bfloat16 or wider, within the bound.
No kernel may reach another device: no remote copies, remote signals or barrier semaphores. Data moves between devices by JAX's collectives and lax.ppermute only.
A program may use at most 64 MiB of HBM per device.

v0:
```python
import jax
import jax.numpy as jnp
from jax import lax
from jax.sharding import PartitionSpec as P

BUCKETS = 4


EPS = 1e-05
MOMENTUM = 0.9
RATE = 0.1
DECAY = 5e-05


def normalize_backward(block_input, conv_weight, bn_gain, out_cotangent):
    row_count = block_input.shape[0]
    convolved = jnp.dot(block_input, conv_weight, preferred_element_type=jnp.float32)
    center = jnp.mean(convolved, axis=0)
    spread = convolved - center
    inverse = lax.rsqrt(jnp.mean(spread * spread, axis=0) + EPS)
    normed = spread * inverse
    upstream = out_cotangent.astype(jnp.float32)
    shift_grad = jnp.sum(upstream, axis=0)
    gain_grad = jnp.sum(upstream * normed, axis=0)
    return (
        bn_gain * inverse / row_count * (row_count * upstream - shift_grad - normed * gain_grad)
    ).astype(jnp.bfloat16)


def reduce_shards(contribution):
    summed = lax.psum(contribution.astype(jnp.bfloat16), "local").astype(jnp.float32)
    return lax.psum_scatter(summed, "node", scatter_dimension=1, tiled=True)


def local(block_input, conv_weight, bn_gain, out_cotangent, master_weight, velocity):
    conv_grad = normalize_backward(block_input, conv_weight, bn_gain, out_cotangent)
    row_count = conv_grad.shape[0]
    width_out = conv_grad.shape[1]
    width_in = block_input.shape[1]
    node_count = lax.axis_size("node")
    node_rows = width_out // node_count
    bucket_rows = node_rows // BUCKETS
    ordered = conv_grad.reshape(row_count, node_count, BUCKETS, bucket_rows).transpose(0, 2, 1, 3)
    contract = (((0,), (0,)), ((), ()))
    pieces = []
    for bucket in range(BUCKETS):
        columns = ordered[:, bucket].reshape(row_count, node_count * bucket_rows)
        contribution = lax.dot_general(
            columns, block_input, contract, preferred_element_type=jnp.float32
        )
        pieces.append(reduce_shards(contribution.reshape(1, node_count, bucket_rows, width_in)))
    reduced = jnp.concatenate(pieces, axis=0)
    gradient = reduced.reshape(node_rows, width_in)
    new_velocity = MOMENTUM * velocity + gradient + DECAY * master_weight
    new_weight = master_weight - RATE * new_velocity
    return (new_velocity, new_weight)


def solution(mesh):
    in_specs = (
        P(("node", "local"), None),
        P(),
        P(),
        P(("node", "local"), None),
        P("node", None),
        P("node", None),
    )
    out_specs = (P("node", None), P("node", None))
    return jax.shard_map(local, mesh=mesh, in_specs=in_specs, out_specs=out_specs, check_vma=False)
```

profile of v0, /device:TPU:0, one launch (start us, length us, event | category | flops | bytes accessed | tf_op | source)
XLA Modules:
  0.0 344.5 jit_solution(8065104903388180618)
XLA Ops:
  7.2 0.0 copy-start
  7.2 0.0 all-reduce.3.cloned.1.call-start
  7.2 1.5 copy-done
  8.8 2.0 fusion.15
  10.8 0.0 copy-start.7
  10.8 0.0 copy-start.1
  10.8 0.4 multiply_reduce_fusion
  11.2 0.3 copy-done.7
  11.5 0.7 copy-done.1
  12.2 0.7 convert_reduce_fusion
  12.9 2.0 fusion.3
  15.0 0.0 copy-start.2
  15.0 3.8 %copy.12 = bf16[392,2048]{0,1:T(8,128)(2,1)} copy(bf16[392,2048]{1,0:T(8,128)(2,1)} %fusion.3) | data formatting | bytes 3211264 | tf_op jit(solution)/shard_map/convert_element_type | solution.py:27
  18.7 0.0 copy-done.2
  18.7 2.3 fusion.8
  21.0 2.3 fusion.7
  23.3 2.3 fusion.6
  25.6 2.3 fusion.5
  27.9 0.0 all-reduce.3.cloned.1.call-update
  27.9 0.0 reduce-scatter.11.cloned.1.call-start
  28.0 66.3 %all-reduce.3.cloned.1.call-done = (bf16[1,16,32,512]{3,2,1,0:T(8,128)(2,1)}, bf16[1,16,32,512]{3,2,1,0:T(8,128)(2,1)}, bf16[1,16,32,512]{3,2,1,0:T(8,128)(2,1)}, bf16[1,16,32,512]{3,2,1,0:T(8,128)(2,1)}) async-done(((bf16[1,16,32,512]{3,2,1,0:T(8,128)(2,1)}, bf16[1,16,32,512]{3,2,1,0:T(8,128)(2,1)}, bf16[1,16,32,512]{3,2,1,0:T(8,128)(2,1)}, bf16[1,16,32,512]{3,2,1,0:T(8,128)(2,1)}), ...) | async-done | bytes 2097168 | tf_op jit(solution)/shard_map/psum | solution.py:31
  94.2 0.0 copy-start.4
  94.2 2.2 convert_element_type.55
  96.4 0.0 copy-start.3
  96.4 0.0 reduce-scatter.11.cloned.1.call-update
  96.5 0.0 reduce-scatter.9.cloned.1.call-start
  96.5 2.2 convert_element_type.52
  98.8 0.0 copy-start.5
  98.8 0.0 reduce-scatter.9.cloned.1.call-update
  98.8 0.0 reduce-scatter.7.cloned.1.call-start
  98.8 0.0 copy-done.4
  98.8 1.1 convert_element_type.49
  100.0 0.0 copy-start.6
  100.0 0.0 reduce-scatter.7.cloned.1.call-update
  100.0 0.0 reduce-scatter.5.cloned.1.call-start
  100.1 0.0 copy-done.3
  100.1 1.1 convert_element_type.46
  101.2 0.0 reduce-scatter.5.cloned.1.call-update
  101.2 54.6 %reduce-scatter.11.cloned.1.call-done = f32[1,1,32,512]{3,2,1,0:T(8,128)} async-done(((f32[1,16,32,512]{3,2,1,0:T(8,128)}), f32[1,1,32,512]{3,2,1,0:T(8,128)}) %reduce-scatter.11.cloned.1.call-update) | async-done | bytes 65552 | tf_op jit(solution)/shard_map/reduce_scatter | solution.py:32
  155.8 60.0 %reduce-scatter.9.cloned.1.call-done = f32[1,1,32,512]{3,2,1,0:T(8,128)} async-done(((f32[1,16,32,512]{3,2,1,0:T(8,128)}), f32[1,1,32,512]{3,2,1,0:T(8,128)}) %reduce-scatter.9.cloned.1.call-update) | async-done | bytes 65552 | tf_op jit(solution)/shard_map/reduce_scatter | solution.py:32
  215.8 60.4 %reduce-scatter.7.cloned.1.call-done = f32[1,1,32,512]{3,2,1,0:T(8,128)} async-done(((f32[1,16,32,512]{3,2,1,0:T(8,128)}), f32[1,1,32,512]{3,2,1,0:T(8,128)}) %reduce-scatter.7.cloned.1.call-update) | async-done | bytes 65552 | tf_op jit(solution)/shard_map/reduce_scatter | solution.py:32
  276.2 60.0 %reduce-scatter.5.cloned.1.call-done = f32[1,1,32,512]{3,2,1,0:T(8,128)} async-done(((f32[1,16,32,512]{3,2,1,0:T(8,128)}), f32[1,1,32,512]{3,2,1,0:T(8,128)}) %reduce-scatter.5.cloned.1.call-update) | async-done | bytes 65552 | tf_op jit(solution)/shard_map/reduce_scatter | solution.py:32
  336.1 1.0 pad_maximum_fusion
  337.1 0.0 copy-done.5
  337.1 0.0 copy-done.6
  337.1 0.9 multiply_subtract_fusion
  (2 shorter events, 0.0 us)
Async XLA Ops:
  7.2 1.6 copy-start
  7.2 87.1 %all-reduce.3.cloned.1.call-start = ((), (), s32[]{:S(2)}) async-start(), calls=%async_computation.8 | async-start | bytes 4194304 | tf_op jit(solution)/shard_map/psum | solution.py:31
  10.8 0.7 copy-start.7
  10.8 1.4 copy-start.1
  15.0 3.8 %copy-start.2 = (bf16[392,512]{1,0:T(8,128)(2,1)S(1)}, bf16[392,512]{1,0:T(8,128)(2,1)}, u32[]{:S(2)}) copy-start(bf16[392,512]{1,0:T(8,128)(2,1)} %param.6) | copy-start | bytes 1204228
  27.9 127.9 %reduce-scatter.11.cloned.1.call-start = ((), (), s32[]{:S(2)}) async-start(), calls=%async_computation.7 | async-start | bytes 1114112 | tf_op jit(solution)/shard_map/reduce_scatter | solution.py:32
  94.2 4.6 %copy-start.4 = (bf16[1,16,32,512]{3,2,1,0:T(8,128)(2,1)S(1)}, bf16[1,16,32,512]{3,2,1,0:T(8,128)(2,1)}, u32[]{:S(2)}) copy-start(bf16[1,16,32,512]{3,2,1,0:T(8,128)(2,1)} %get-tuple-element.6) | copy-start | bytes 1572868
  96.4 3.6 %copy-start.3 = (bf16[1,16,32,512]{3,2,1,0:T(8,128)(2,1)S(1)}, bf16[1,16,32,512]{3,2,1,0:T(8,128)(2,1)}, u32[]{:S(2)}) copy-start(bf16[1,16,32,512]{3,2,1,0:T(8,128)(2,1)} %get-tuple-element.7) | copy-start | bytes 1572868
  96.5 119.3 %reduce-scatter.9.cloned.1.call-start = ((), (), s32[]{:S(2)}) async-start(), calls=%async_computation.6 | async-start | bytes 1114112 | tf_op jit(solution)/shard_map/reduce_scatter | solution.py:32
  98.8 238.3 %copy-start.5 = (f32[128,512]{1,0:T(8,128)S(1)}, f32[128,512]{1,0:T(8,128)}, u32[]{:S(2)}) copy-start(f32[128,512]{1,0:T(8,128)} %param.10) | copy-start | bytes 786436
  98.8 177.4 %reduce-scatter.7.cloned.1.call-start = ((), (), s32[]{:S(2)}) async-start(), calls=%async_computation.5 | async-start | bytes 1114112 | tf_op jit(solution)/shard_map/reduce_scatter | solution.py:32
  100.0 237.1 %copy-start.6 = (f32[128,512]{1,0:T(8,128)S(1)}, f32[128,512]{1,0:T(8,128)}, u32[]{:S(2)}) copy-start(f32[128,512]{1,0:T(8,128)} %param.11) | copy-start | bytes 786436
  100.0 236.1 %reduce-scatter.5.cloned.1.call-start = ((), (), s32[]{:S(2)}) async-start(), calls=%async_computation.4 | async-start | bytes 1114112 | tf_op jit(solution)/shard_map/reduce_scatter | solution.py:32
Sparse Core Ops, SparseCore 0:
  28.0 66.1 all-reduce.2
  98.3 57.4 reduce-scatter.10
  159.4 56.3 reduce-scatter.8
  219.7 56.4 reduce-scatter.6
  279.6 56.4 reduce-scatter.4
where the time goes:
time: 345 us
  waiting for transfers between devices  301 us (87%)
  between operations  13.9 us (4%)
  other arithmetic  11.6 us (3%)
  matrix products  11.1 us (3%)
  local copies, waits for them, and re-layouts  6.37 us (2%)
    reduce_scatter x4, waiting for transfers between devices, reduce_shards(): return lax.psum_scatter(summed, 'node', scatter_dimension=1, tiled=True)  235 us
    psum x1, waiting for transfers between devices, reduce_shards(): lax.psum(contribution.astype(jnp.bfloat16), 'local').astype(jnp.float32)  66.3 us
    dot_general x4, matrix products, local(): lax.dot_general(columns, block_input, contract, preferred_element_type=jn...  9.14 us
  transfers between devices with their start and end apart: 5, of which 5 were waited for; matrix products, arithmetic and copies ran while one was open for 1% of the time, Pallas kernels for 0%

commit v1 on v0

v1 whole, which is shorter than its diff:
```python
import functools

import jax
import jax.numpy as jnp
from jax import lax
from jax.experimental import pallas as pl
from jax.experimental.pallas import tpu as pltpu
from jax.sharding import PartitionSpec as P

EPS = 1e-05
MOMENTUM = 0.9
RATE = 0.1
DECAY = 5e-05

BLOCK = 256
CHUNKS = 2
NODE = "node"
LOCAL = "local"


def term_kernel(run, core_ref, x_ref, w_ref, gain_ref, u_ref, mine_ref, other_ref, term_ref):
    core = core_ref[0]
    rows = x_ref.shape[0]
    x = x_ref[...]
    conv = jnp.dot(x, w_ref[...], preferred_element_type=jnp.float32)
    center = jnp.sum(conv, axis=0, keepdims=True) * (1.0 / rows)
    spread = conv - center
    upstream = u_ref[...].astype(jnp.float32)
    inverse = lax.rsqrt(jnp.sum(spread * spread, axis=0, keepdims=True) * (1.0 / rows) + EPS)
    shift_grad = jnp.sum(upstream, axis=0, keepdims=True)
    gain_grad = jnp.sum(upstream * spread, axis=0, keepdims=True) * inverse
    scale = gain_ref[...] * inverse
    step = scale * (1.0 / rows)
    grad = scale * upstream - (step * shift_grad + spread * (step * inverse * gain_grad))
    term_ref[...] = lax.dot_general(
        grad.astype(jnp.bfloat16), x, (((0,), (0,)), ((), ())), preferred_element_type=jnp.float32
    )
    for pair in range(term_ref.shape[0] // (2 * run)):
        own = pl.multiple_of(pair * 2 * run + core * run, run)
        far = pl.multiple_of(pair * 2 * run + (1 - core) * run, run)
        mine_ref[pl.ds(pair * run, run), :] = term_ref[pl.ds(own, run), :].astype(jnp.bfloat16)
        other_ref[pl.ds(pair * run, run), :] = term_ref[pl.ds(far, run), :].astype(jnp.bfloat16)


def term_chunk(chunk, run, core, block_input, conv_weight, gain, out_cotangent):
    rows, width_in = block_input.shape
    width_out = conv_weight.shape[1]
    channels = width_out // CHUNKS
    steps = channels // BLOCK
    first = chunk * steps
    out = jax.ShapeDtypeStruct((channels // 2, width_in), jnp.bfloat16)
    return pl.pallas_call(
        functools.partial(term_kernel, run),
        grid=(steps,),
        out_shape=(out, out),
        in_specs=[
            pl.BlockSpec(memory_space=pltpu.SMEM),
            pl.BlockSpec((rows, width_in), lambda i: (0, 0)),
            pl.BlockSpec((width_in, BLOCK), lambda i: (0, first + i)),
            pl.BlockSpec((1, BLOCK), lambda i: (0, first + i)),
            pl.BlockSpec((rows, BLOCK), lambda i: (0, first + i)),
        ],
        out_specs=(
            pl.BlockSpec((BLOCK // 2, width_in), lambda i: (i, 0)),
            pl.BlockSpec((BLOCK // 2, width_in), lambda i: (i, 0)),
        ),
        scratch_shapes=[pltpu.VMEM((BLOCK, width_in), jnp.float32)],
        cost_estimate=pl.CostEstimate(
            flops=4 * rows * channels * width_in,
            bytes_accessed=2 * (rows * channels + channels * width_in * 2 + rows * width_in),
            transcendentals=channels,
        ),
        compiler_params=pltpu.CompilerParams(vmem_limit_bytes=24 * 2**20),
        name="term_chunk",
    )(core, block_input, conv_weight, gain, out_cotangent)


def pick(array, index, axis):
    return lax.dynamic_index_in_dim(array, index, axis, keepdims=False)


def shift_pairs(size, shift):
    return [(i, (i + shift) % size) for i in range(size)]


def flip_pairs(size, bit):
    return [(i, i ^ bit) for i in range(size)]


def local_fn(block_input, conv_weight, bn_gain, out_cotangent, master_weight, velocity):
    f32, bf16 = jnp.float32, jnp.bfloat16
    nodes = lax.axis_size(NODE)
    locals_ = lax.axis_size(LOCAL)
    width_in = block_input.shape[1]
    width_out = conv_weight.shape[1]
    run = width_out // nodes
    part = run // locals_
    node = lax.axis_index(NODE)
    lane = lax.axis_index(LOCAL)
    core = node % 2
    side = (node // 2) % 2
    deep = node // 4
    depth = nodes // 4
    half = depth // CHUNKS

    gain = bn_gain.reshape(1, width_out)
    core_arg = core.astype(jnp.int32).reshape(1)

    def core_swap(array):
        return lax.ppermute(array, NODE, flip_pairs(nodes, 1))

    def side_swap(array):
        return lax.ppermute(array, NODE, flip_pairs(nodes, 2))

    def lane_reduce(send, keep):
        total = keep
        for shift in range(1, locals_):
            arrived = lax.ppermute(
                send((lane + shift) % locals_), LOCAL, shift_pairs(locals_, shift)
            )
            total = total + arrived.astype(f32)
        return total

    shape = (half, 2, locals_, part, width_in)
    mine, got = [], []
    for chunk in range(CHUNKS):
        a, b = term_chunk(chunk, run, core_arg, block_input, conv_weight, gain, out_cotangent)
        mine.append(a.reshape(shape))
        got.append(core_swap(b).reshape(shape))

    def chip(chunk, side_index, lane_index):
        a, b = mine[chunk], got[chunk]
        if lane_index is not None:
            a, b = pick(a, lane_index, 2), pick(b, lane_index, 2)
        if side_index is not None:
            a, b = pick(a, side_index, 1), pick(b, side_index, 1)
        return a.astype(f32) + b.astype(f32)

    over_x = lane_reduce(lambda l: chip(0, None, l).astype(bf16), chip(0, None, lane))
    arrived = side_swap(chip(1, 1 - side, None).astype(bf16))
    over_y = chip(1, side, None) + arrived.astype(f32)

    arrived = side_swap(pick(over_x, 1 - side, 1).astype(bf16))
    first = pick(over_x, side, 1) + arrived.astype(f32)
    second = lane_reduce(lambda l: pick(over_y, l, 1).astype(bf16), pick(over_y, lane, 1))

    plane = jnp.concatenate([first, second], axis=0)
    total = pick(plane, deep, 0)
    for shift in range(1, depth):
        piece = pick(plane, (deep + shift) % depth, 0).astype(bf16)
        arrived = lax.ppermute(piece, NODE, shift_pairs(nodes, 4 * shift))
        total = total + arrived.astype(f32)

    total = total.astype(bf16)
    pieces = [total]
    for shift in range(1, locals_):
        pieces.append(lax.ppermute(total, LOCAL, shift_pairs(locals_, -shift)))
    gradient = jnp.concatenate(
        [
            functools.reduce(
                lambda other, s: jnp.where((lane + s) % locals_ == l, pieces[s], other),
                range(1, locals_),
                pieces[0],
            )
            for l in range(locals_)
        ],
        axis=0,
    ).astype(f32)
    new_velocity = MOMENTUM * velocity + gradient + DECAY * master_weight
    new_weight = master_weight - RATE * new_velocity
    return (new_velocity, new_weight)


def solution(mesh):
    in_specs = (
        P((NODE, LOCAL), None),
        P(),
        P(),
        P((NODE, LOCAL), None),
        P(NODE, None),
        P(NODE, None),
    )
    out_specs = (P(NODE, None), P(NODE, None))
    return jax.shard_map(local_fn, mesh=mesh, in_specs=in_specs, out_specs=out_specs, check_vma=False)
```

time: 345 us -> 47.8 us (0.14)
  waiting for transfers between devices: 301 us -> 16.1 us
  starting transfers between devices: 0.21 us -> 14.8 us
  between operations: 13.9 us -> 0.9 us
  matrix products: 11.1 us -> 0 us
  other arithmetic: 11.6 us -> 1.41 us
  Pallas kernels: 0 us -> 8.34 us
    reduce_scatter x4 -> x0, waiting for transfers between devices: 235 us -> none  [reduce_shards(): return lax.psum_scatter(summed, 'node', scatter_dimension=1, tiled=True)]
    psum x1 -> x0, waiting for transfers between devices: 66.3 us -> none  [reduce_shards(): lax.psum(contribution.astype(jnp.bfloat16), 'local').astype(jnp.float32)]
    ppermute x0 -> x10, waiting for transfers between devices: none -> 16.1 us  [the longest x2 6.76 us: lane_reduce(): lax.ppermute(send((lane + shift) % locals_), LOCAL, shift_pairs(locals_,...]
    ppermute x0 -> x10, starting transfers between devices: none -> 14.8 us  [the longest x3 4.67 us: local_fn(): arrived = lax.ppermute(piece, NODE, shift_pairs(nodes, 4 * shift))]
    dot_general x5 -> x0, matrix products: 11.1 us -> none  [the longest x4 9.14 us: local(): lax.dot_general(columns, block_input, contract, preferred_element_type=jn...]
    convert_element_type x5 -> x4, other arithmetic: 8.73 us -> 0.27 us  [the longest x1 0.09 us: local_fn(): piece = pick(plane, (deep + shift) % depth, 0).astype(bf16)]
    pallas_call x0 -> x2, Pallas kernels: none -> 8.34 us  [term_chunk(): pl.pallas_call(functools.partial(term_kernel, run), grid=(steps,), out_sh...]
    convert_element_type x1 -> x2, local copies, waits for them, and re-layouts: 3.79 us -> 0.05 us  [the longest x1 0.03 us: local_fn(): arrived = side_swap(pick(over_x, 1 - side, 1).astype(bf16))]
  transfers between devices with their start and end apart: 5 -> 10, of which waited for: 5 -> 7; matrix products, arithmetic and copies ran while one was open for 1% -> 3% of each run, Pallas kernels for 0% -> 9%
where the time goes in v1:
time: 47.8 us; the launch traced here: 47.5 us
  waiting for transfers between devices  16.1 us (34%)
  starting transfers between devices  14.8 us (31%)
  Pallas kernels  8.34 us (17%)
  local copies, waits for them, and re-layouts  5.96 us (12%)
  other arithmetic  1.41 us (3%)
  between operations  0.9 us (2%)
    pallas_call x2, Pallas kernels, term_chunk(): pl.pallas_call(functools.partial(term_kernel, run), grid=(steps,), out_sh...  8.34 us
    ppermute x2, waiting for transfers between devices, lane_reduce(): lax.ppermute(send((lane + shift) % locals_), LOCAL, shift_pairs(locals_,...  6.76 us
    ppermute x3, waiting for transfers between devices, local_fn(): arrived = lax.ppermute(piece, NODE, shift_pairs(nodes, 4 * shift))  5.05 us
    unnamed x12, local copies, waits for them, and re-layouts  4.7 us
    ppermute x3, starting transfers between devices, local_fn(): arrived = lax.ppermute(piece, NODE, shift_pairs(nodes, 4 * shift))  4.67 us
    ppermute x2, starting transfers between devices, lane_reduce(): lax.ppermute(send((lane + shift) % locals_), LOCAL, shift_pairs(locals_,...  4.56 us
    ppermute x2, starting transfers between devices, side_swap(): return lax.ppermute(array, NODE, flip_pairs(nodes, 2))  3.42 us
    ppermute x1, waiting for transfers between devices, local_fn(): pieces.append(lax.ppermute(total, LOCAL, shift_pairs(locals_, -shift)))  2.77 us
  transfers between devices with their start and end apart: 10, of which 7 were waited for; matrix products, arithmetic and copies ran while one was open for 3% of the time, Pallas kernels for 9%

profile of v1, /device:TPU:0, one launch (start us, length us, event | category | flops | bytes accessed | tf_op | source)
XLA Modules:
  0.0 47.5 jit_solution(16514702558091634223)
XLA Ops:
  0.6 0.0 copy-start
  0.7 1.6 %copy-done = bf16[512,2048]{1,0:T(8,128)(2,1)S(1)} copy-done((bf16[512,2048]{1,0:T(8,128)(2,1)S(1)}, bf16[512,2048]{1,0:T(8,128)(2,1)}, u32[]{:S(2)}) %copy-start) | copy-done | bytes 2097176
  2.2 0.0 copy-start.1
  2.2 1.4 %copy-done.1 = bf16[392,2048]{1,0:T(8,128)(2,1)S(1)} copy-done((bf16[392,2048]{1,0:T(8,128)(2,1)S(1)}, bf16[392,2048]{1,0:T(8,128)(2,1)}, u32[]{:S(2)}) %copy-start.1) | copy-done | bytes 1605656
  3.7 0.0 copy-start.2
  3.7 1.0 %copy-done.2 = bf16[392,512]{1,0:T(8,128)(2,1)S(1)} copy-done((bf16[392,512]{1,0:T(8,128)(2,1)S(1)}, bf16[392,512]{1,0:T(8,128)(2,1)}, u32[]{:S(2)}) %copy-start.2) | copy-done | bytes 401432
  4.7 0.0 copy-start.3
  4.7 0.7 %copy-done.3 = f32[2048]{0:T(1024)S(1)} copy-done((f32[2048]{0:T(1024)S(1)}, f32[2048]{0:T(1024)}, u32[]{:S(2)}) %copy-start.3) | copy-done | bytes 8216
  5.4 4.2 %term_chunk.2 = (bf16[512,512]{1,0:T(8,128)(2,1)S(1)}, bf16[512,512]{1,0:T(8,128)(2,1)S(1)}) custom-call(s32[1]{0:T(128)} %bitcast.core_ref, bf16[392,512]{1,0:T(8,128)(2,1)S(1)} %copy-done.2, bf16[512,2048]{1,0:T(8,128)(2,1)S(1)} %copy-done, f32[1,2048]{1,0:T(1,128)S(1)} %bitcast.40, bf16[392,2048]{1,0:T(8,128)(2,1)S(1)} %copy-done.1), custom_call_target="tpu_custom_call" | custom-call | flops 822083584 | bytes 3301376 | tf_op jit(solution)/shard_map/term_chunk/pallas_call | solution.py:52
  9.5 0.5 %collective-permute-start = (bf16[512,512]{1,0:T(8,128)(2,1)S(1)}, bf16[512,512]{1,0:T(8,128)(2,1)}, u32[]{:S(2)}, u32[]{:S(2)}) collective-permute-start(bf16[512,512]{1,0:T(8,128)(2,1)S(1)} %get-tuple-element.7), channel_id=1, source_target_pairs={{0,2},{2,0},{4,6},{6,4},{8,10},{10,8},{12,14},{14,12},{16,18},{18,... | collective-permute-start | bytes 1572872 | tf_op jit(solution)/shard_map/ppermute | solution.py:110
  10.0 4.2 %term_chunk.3 = (bf16[512,512]{1,0:T(8,128)(2,1)S(1)}, bf16[512,512]{1,0:T(8,128)(2,1)S(1)}) custom-call(s32[1]{0:T(128)} %bitcast.core_ref, bf16[392,512]{1,0:T(8,128)(2,1)S(1)} %copy-done.2, bf16[512,2048]{1,0:T(8,128)(2,1)S(1)} %copy-done, f32[1,2048]{1,0:T(1,128)S(1)} %bitcast.41, bf16[392,2048]{1,0:T(8,128)(2,1)S(1)} %copy-done.1), custom_call_target="tpu_custom_call" | custom-call | flops 822083584 | bytes 3301376 | tf_op jit(solution)/shard_map/term_chunk/pallas_call | solution.py:52
  14.2 0.1 collective-permute-start.3
  14.5 0.0 collective-permute-done
  14.6 1.1 %constant_dynamic-slice_fusion.6 = (bf16[2,2,1,64,512]{4,3,2,1,0:T(8,128)(2,1)S(1)}, bf16[2,2,1,64,512]{4,3,2,1,0:T(8,128)(2,1)S(1)}) fusion(bf16[2,2,2,64,512]{4,3,2,1,0:T(8,128)(2,1)} %bitcast.3, s32[]{:T(128)S(6)} %select_n.93, s32[]{:T(128)S(6)} %select_n.94), kind=kLoop, calls=%fused_computation.45 | loop fusion | bytes 1048584 | tf_op jit(solution)/shard_map/jit(dynamic_index_in_dim)/dynamic_slice | solution.py:79
  15.6 0.1 fusion
  15.7 3.0 %collective-permute-start.1 = (bf16[2,2,64,512]{3,2,0,1:T(8,128)(2,1)S(1)}, bf16[2,2,64,512]{3,2,0,1:T(8,128)(2,1)S(1)}, u32[]{:S(2)}, u32[]{:S(2)}) collective-permute-start(bf16[2,2,64,512]{3,2,0,1:T(8,128)(2,1)S(1)} %fusion), channel_id=1, source_target_pairs={{0,1},{1,0},{2,3},{3,2},{4,5},{5,4},{6,7},{7,6},{8,9},{9,8},{10,11... | collective-permute-start | bytes 786440 | tf_op jit(solution)/shard_map/ppermute | solution.py:118
  18.7 0.0 collective-permute-done.3
  18.8 0.1 fusion.1
  18.8 1.6 %collective-permute-start.4 = (bf16[2,2,64,512]{3,2,0,1:T(8,128)(2,1)S(1)}, bf16[2,2,64,512]{3,2,0,1:T(8,128)(2,1)S(1)}, u32[]{:S(2)}, u32[]{:S(2)}) collective-permute-start(bf16[2,2,64,512]{3,2,0,1:T(8,128)(2,1)S(1)} %fusion.1), channel_id=1, source_target_pairs={{0,4},{2,6},{4,0},{6,2},{8,12},{10,14},{12,8},{14,10},{16,20},{18,... | collective-permute-start | bytes 786440 | tf_op jit(solution)/shard_map/ppermute | solution.py:113
  20.4 4.8 %collective-permute-done.1 = bf16[2,2,64,512]{3,2,0,1:T(8,128)(2,1)S(1)} collective-permute-done((bf16[2,2,64,512]{3,2,0,1:T(8,128)(2,1)S(1)}, bf16[2,2,64,512]{3,2,0,1:T(8,128)(2,1)S(1)}, u32[]{:S(2)}, u32[]{:S(2)}) %collective-permute-start.1) | collective-permute-done | bytes 262176 | tf_op jit(solution)/shard_map/ppermute | solution.py:118
  25.2 0.1 bitcast_add_fusion.1
  25.4 1.8 %collective-permute-start.2 = (bf16[2,64,512]{2,1,0:T(8,128)(2,1)S(1)}, bf16[2,64,512]{2,1,0:T(8,128)(2,1)S(1)}, u32[]{:S(2)}, u32[]{:S(2)}) collective-permute-start(bf16[2,64,512]{2,1,0:T(8,128)(2,1)S(1)} %fusion.2), channel_id=1, source_target_pairs={{0,4},{2,6},{4,0},{6,2},{8,12},{10,14},{12,8},{14,10},{16,20},{18,... | collective-permute-start | bytes 393224 | tf_op jit(solution)/shard_map/ppermute | solution.py:113
  27.2 0.0 collective-permute-done.4
  27.2 0.0 copy-start.4
  27.2 0.0 copy-start.5
  27.2 0.1 bitcast_add_fusion
  27.4 1.6 %collective-permute-start.5 = (bf16[2,64,512]{2,1,0:T(8,128)(2,1)S(1)}, bf16[2,64,512]{2,1,0:T(8,128)(2,1)S(1)}, u32[]{:S(2)}, u32[]{:S(2)}) collective-permute-start(bf16[2,64,512]{2,1,0:T(8,128)(2,1)S(1)} %fusion.3), channel_id=1, source_target_pairs={{0,1},{1,0},{2,3},{3,2},{4,5},{5,4},{6,7},{7,6},{8,9},{9,8},{10,11... | collective-permute-start | bytes 393224 | tf_op jit(solution)/shard_map/ppermute | solution.py:118
  28.9 1.5 %collective-permute-done.2 = bf16[2,64,512]{2,1,0:T(8,128)(2,1)S(1)} collective-permute-done((bf16[2,64,512]{2,1,0:T(8,128)(2,1)S(1)}, bf16[2,64,512]{2,1,0:T(8,128)(2,1)S(1)}, u32[]{:S(2)}, u32[]{:S(2)}) %collective-permute-start.2) | collective-permute-done | bytes 131104 | tf_op jit(solution)/shard_map/ppermute | solution.py:113
  30.4 1.9 %collective-permute-done.5 = bf16[2,64,512]{2,1,0:T(8,128)(2,1)S(1)} collective-permute-done((bf16[2,64,512]{2,1,0:T(8,128)(2,1)S(1)}, bf16[2,64,512]{2,1,0:T(8,128)(2,1)S(1)}, u32[]{:S(2)}, u32[]{:S(2)}) %collective-permute-start.5) | collective-permute-done | bytes 131104 | tf_op jit(solution)/shard_map/ppermute | solution.py:118
  32.4 0.1 fusion.17
  32.5 3.7 %collective-permute-start.8 = (bf16[64,512]{1,0:T(8,128)(2,1)S(1)}, bf16[64,512]{1,0:T(8,128)(2,1)S(1)}, u32[]{:S(2)}, u32[]{:S(2)}) collective-permute-start(bf16[64,512]{1,0:T(8,128)(2,1)S(1)} %get-tuple-element.14), channel_id=1, source_target_pairs={{0,24},{2,26},{4,28},{6,30},{8,0},{10,2},{12,4},{14,6},{16,8},{18,... | collective-permute-start | bytes 196616 | tf_op jit(solution)/shard_map/ppermute | solution.py:151
  36.2 0.0 collective-permute-start.7
  36.2 1.0 %collective-permute-start.6 = (bf16[64,512]{1,0:T(8,128)(2,1)S(1)}, bf16[64,512]{1,0:T(8,128)(2,1)S(1)}, u32[]{:S(2)}, u32[]{:S(2)}) collective-permute-start(bf16[64,512]{1,0:T(8,128)(2,1)S(1)} %get-tuple-element.12), channel_id=1, source_target_pairs={{0,8},{2,10},{4,12},{6,14},{8,16},{10,18},{12,20},{14,22},{16,24},... | collective-permute-start | bytes 196616 | tf_op jit(solution)/shard_map/ppermute | solution.py:151
  37.2 0.9 %collective-permute-done.8 = bf16[64,512]{1,0:T(8,128)(2,1)S(1)} collective-permute-done((bf16[64,512]{1,0:T(8,128)(2,1)S(1)}, bf16[64,512]{1,0:T(8,128)(2,1)S(1)}, u32[]{:S(2)}, u32[]{:S(2)}) %collective-permute-start.8) | collective-permute-done | bytes 65568 | tf_op jit(solution)/shard_map/ppermute | solution.py:151
  38.1 3.3 %collective-permute-done.7 = bf16[64,512]{1,0:T(8,128)(2,1)S(1)} collective-permute-done((bf16[64,512]{1,0:T(8,128)(2,1)S(1)}, bf16[64,512]{1,0:T(8,128)(2,1)S(1)}, u32[]{:S(2)}, u32[]{:S(2)}) %collective-permute-start.7) | collective-permute-done | bytes 65568 | tf_op jit(solution)/shard_map/ppermute | solution.py:151
  41.3 0.9 %collective-permute-done.6 = bf16[64,512]{1,0:T(8,128)(2,1)S(1)} collective-permute-done((bf16[64,512]{1,0:T(8,128)(2,1)S(1)}, bf16[64,512]{1,0:T(8,128)(2,1)S(1)}, u32[]{:S(2)}, u32[]{:S(2)}) %collective-permute-start.6) | collective-permute-done | bytes 65568 | tf_op jit(solution)/shard_map/ppermute | solution.py:151
  42.3 1.6 %collective-permute-start.9 = (bf16[64,512]{1,0:T(8,128)(2,1)S(1)}, bf16[64,512]{1,0:T(8,128)(2,1)S(1)}, u32[]{:S(2)}, u32[]{:S(2)}) collective-permute-start(bf16[64,512]{1,0:T(8,128)(2,1)S(1)} %fusion.11), channel_id=1, source_target_pairs={{0,1},{1,0},{2,3},{3,2},{4,5},{5,4},{6,7},{7,6},{8,9},{9,8},{10,11... | collective-permute-start | bytes 196616 | tf_op jit(solution)/shard_map/ppermute | solution.py:157
  43.9 2.8 %collective-permute-done.9 = bf16[64,512]{1,0:T(8,128)(2,1)S(1)} collective-permute-done((bf16[64,512]{1,0:T(8,128)(2,1)S(1)}, bf16[64,512]{1,0:T(8,128)(2,1)S(1)}, u32[]{:S(2)}, u32[]{:S(2)}) %collective-permute-start.9) | collective-permute-done | bytes 65568 | tf_op jit(solution)/shard_map/ppermute | solution.py:157
  46.6 0.0 copy-done.4
  46.7 0.0 copy-done.5
  46.7 0.9 %multiply_subtract_fusion = (f32[128,512]{1,0:T(8,128)}, f32[128,512]{1,0:T(8,128)}) fusion(f32[128,512]{1,0:T(8,128)S(1)} %copy-done.4, bf16[64,512]{1,0:T(8,128)(2,1)S(1)} %get-tuple-element.24, bf16[64,512]{1,0:T(8,128)(2,1)S(1)} %get-tuple-element.23, f32[128,512]{1,0:T(8,128)S(1)} %copy-done.5), kind=kLoop, calls=%fused_computation.16 | loop fusion | flops 655360 | bytes 1179648 | tf_op jit(solution)/shard_map/sub | solution.py:170
  (9 shorter events, 0.3 us)
Async XLA Ops:
  0.6 1.6 %copy-start = (bf16[512,2048]{1,0:T(8,128)(2,1)S(1)}, bf16[512,2048]{1,0:T(8,128)(2,1)}, u32[]{:S(2)}) copy-start(bf16[512,2048]{1,0:T(8,128)(2,1)} %w_ref.3) | copy-start | bytes 6291460
  2.2 1.4 %copy-start.1 = (bf16[392,2048]{1,0:T(8,128)(2,1)S(1)}, bf16[392,2048]{1,0:T(8,128)(2,1)}, u32[]{:S(2)}) copy-start(bf16[392,2048]{1,0:T(8,128)(2,1)} %u_ref.3) | copy-start | bytes 4816900
  3.7 1.0 %copy-start.2 = (bf16[392,512]{1,0:T(8,128)(2,1)S(1)}, bf16[392,512]{1,0:T(8,128)(2,1)}, u32[]{:S(2)}) copy-start(bf16[392,512]{1,0:T(8,128)(2,1)} %x_ref.3) | copy-start | bytes 1204228
  4.7 0.7 %copy-start.3 = (f32[2048]{0:T(1024)S(1)}, f32[2048]{0:T(1024)}, u32[]{:S(2)}) copy-start(f32[2048]{0:T(1024)} %param.8) | copy-start | bytes 24580
  9.5 5.0 %collective-permute-start = (bf16[512,512]{1,0:T(8,128)(2,1)S(1)}, bf16[512,512]{1,0:T(8,128)(2,1)}, u32[]{:S(2)}, u32[]{:S(2)}) collective-permute-start(bf16[512,512]{1,0:T(8,128)(2,1)S(1)} %get-tuple-element.7), channel_id=1, source_target_pairs={{0,2},{2,0},{4,6},{6,4},{8,10},{10,8},{12,14},{14,12},{16,18},{18,... | collective-permute-start | bytes 1572872 | tf_op jit(solution)/shard_map/ppermute | solution.py:110
  14.2 4.5 %collective-permute-start.3 = (bf16[512,512]{1,0:T(8,128)(2,1)S(1)}, bf16[512,512]{1,0:T(8,128)(2,1)S(1)}, u32[]{:S(2)}, u32[]{:S(2)}) collective-permute-start(bf16[512,512]{1,0:T(8,128)(2,1)S(1)} %get-tuple-element.9), channel_id=1, source_target_pairs={{0,2},{2,0},{4,6},{6,4},{8,10},{10,8},{12,14},{14,12},{16,18},{18,... | collective-permute-start | bytes 1572872 | tf_op jit(solution)/shard_map/ppermute | solution.py:110
  15.7 9.5 %collective-permute-start.1 = (bf16[2,2,64,512]{3,2,0,1:T(8,128)(2,1)S(1)}, bf16[2,2,64,512]{3,2,0,1:T(8,128)(2,1)S(1)}, u32[]{:S(2)}, u32[]{:S(2)}) collective-permute-start(bf16[2,2,64,512]{3,2,0,1:T(8,128)(2,1)S(1)} %fusion), channel_id=1, source_target_pairs={{0,1},{1,0},{2,3},{3,2},{4,5},{5,4},{6,7},{7,6},{8,9},{9,8},{10,11... | collective-permute-start | bytes 786440 | tf_op jit(solution)/shard_map/ppermute | solution.py:118
  18.8 8.4 %collective-permute-start.4 = (bf16[2,2,64,512]{3,2,0,1:T(8,128)(2,1)S(1)}, bf16[2,2,64,512]{3,2,0,1:T(8,128)(2,1)S(1)}, u32[]{:S(2)}, u32[]{:S(2)}) collective-permute-start(bf16[2,2,64,512]{3,2,0,1:T(8,128)(2,1)S(1)} %fusion.1), channel_id=1, source_target_pairs={{0,4},{2,6},{4,0},{6,2},{8,12},{10,14},{12,8},{14,10},{16,20},{18,... | collective-permute-start | bytes 786440 | tf_op jit(solution)/shard_map/ppermute | solution.py:113
  25.4 5.0 %collective-permute-start.2 = (bf16[2,64,512]{2,1,0:T(8,128)(2,1)S(1)}, bf16[2,64,512]{2,1,0:T(8,128)(2,1)S(1)}, u32[]{:S(2)}, u32[]{:S(2)}) collective-permute-start(bf16[2,64,512]{2,1,0:T(8,128)(2,1)S(1)} %fusion.2), channel_id=1, source_target_pairs={{0,4},{2,6},{4,0},{6,2},{8,12},{10,14},{12,8},{14,10},{16,20},{18,... | collective-permute-start | bytes 393224 | tf_op jit(solution)/shard_map/ppermute | solution.py:113
  27.2 19.4 %copy-start.4 = (f32[128,512]{1,0:T(8,128)S(1)}, f32[128,512]{1,0:T(8,128)}, u32[]{:S(2)}) copy-start(f32[128,512]{1,0:T(8,128)} %param.10) | copy-start | bytes 786436
  27.2 19.4 %copy-start.5 = (f32[128,512]{1,0:T(8,128)S(1)}, f32[128,512]{1,0:T(8,128)}, u32[]{:S(2)}) copy-start(f32[128,512]{1,0:T(8,128)} %param.11) | copy-start | bytes 786436
  27.4 5.0 %collective-permute-start.5 = (bf16[2,64,512]{2,1,0:T(8,128)(2,1)S(1)}, bf16[2,64,512]{2,1,0:T(8,128)(2,1)S(1)}, u32[]{:S(2)}, u32[]{:S(2)}) collective-permute-start(bf16[2,64,512]{2,1,0:T(8,128)(2,1)S(1)} %fusion.3), channel_id=1, source_target_pairs={{0,1},{1,0},{2,3},{3,2},{4,5},{5,4},{6,7},{7,6},{8,9},{9,8},{10,11... | collective-permute-start | bytes 393224 | tf_op jit(solution)/shard_map/ppermute | solution.py:118
  32.5 5.6 %collective-permute-start.8 = (bf16[64,512]{1,0:T(8,128)(2,1)S(1)}, bf16[64,512]{1,0:T(8,128)(2,1)S(1)}, u32[]{:S(2)}, u32[]{:S(2)}) collective-permute-start(bf16[64,512]{1,0:T(8,128)(2,1)S(1)} %get-tuple-element.14), channel_id=1, source_target_pairs={{0,24},{2,26},{4,28},{6,30},{8,0},{10,2},{12,4},{14,6},{16,8},{18,... | collective-permute-start | bytes 196616 | tf_op jit(solution)/shard_map/ppermute | solution.py:151
  36.2 5.2 %collective-permute-start.7 = (bf16[64,512]{1,0:T(8,128)(2,1)S(1)}, bf16[64,512]{1,0:T(8,128)(2,1)S(1)}, u32[]{:S(2)}, u32[]{:S(2)}) collective-permute-start(bf16[64,512]{1,0:T(8,128)(2,1)S(1)} %get-tuple-element.13), channel_id=1, source_target_pairs={{0,16},{2,18},{4,20},{6,22},{8,24},{10,26},{12,28},{14,30},{16,0},... | collective-permute-start | bytes 196616 | tf_op jit(solution)/shard_map/ppermute | solution.py:151
  36.2 6.1 %collective-permute-start.6 = (bf16[64,512]{1,0:T(8,128)(2,1)S(1)}, bf16[64,512]{1,0:T(8,128)(2,1)S(1)}, u32[]{:S(2)}, u32[]{:S(2)}) collective-permute-start(bf16[64,512]{1,0:T(8,128)(2,1)S(1)} %get-tuple-element.12), channel_id=1, source_target_pairs={{0,8},{2,10},{4,12},{6,14},{8,16},{10,18},{12,20},{14,22},{16,24},... | collective-permute-start | bytes 196616 | tf_op jit(solution)/shard_map/ppermute | solution.py:151
  42.3 4.3 %collective-permute-start.9 = (bf16[64,512]{1,0:T(8,128)(2,1)S(1)}, bf16[64,512]{1,0:T(8,128)(2,1)S(1)}, u32[]{:S(2)}, u32[]{:S(2)}) collective-permute-start(bf16[64,512]{1,0:T(8,128)(2,1)S(1)} %fusion.11), channel_id=1, source_target_pairs={{0,1},{1,0},{2,3},{3,2},{4,5},{5,4},{6,7},{7,6},{8,9},{9,8},{10,11... | collective-permute-start | bytes 196616 | tf_op jit(solution)/shard_map/ppermute | solution.py:157

commit v2 on v1

v2 whole, which is shorter than its diff:
```python
import functools

import jax
import jax.numpy as jnp
from jax import lax
from jax.experimental import pallas as pl
from jax.experimental.pallas import tpu as pltpu
from jax.sharding import PartitionSpec as P

EPS = 1e-05
MOMENTUM = 0.9
RATE = 0.1
DECAY = 5e-05

TILE = 128
PACK = 16
NODE = "node"
LOCAL = "local"
F32 = jnp.float32
BF16 = jnp.bfloat16


def term_rows(x, weight, gain, cotangent):
    rows = x.shape[0]
    conv = jnp.dot(x, weight, preferred_element_type=F32)
    center = jnp.sum(conv, axis=0, keepdims=True) * (1.0 / rows)
    spread = conv - center
    upstream = cotangent.astype(F32)
    inverse = lax.rsqrt(jnp.sum(spread * spread, axis=0, keepdims=True) * (1.0 / rows) + EPS)
    shift_grad = jnp.sum(upstream, axis=0, keepdims=True)
    gain_grad = jnp.sum(upstream * spread, axis=0, keepdims=True) * inverse
    scale = gain * inverse
    step = scale * (1.0 / rows)
    grad = scale * upstream - (step * shift_grad + spread * (step * inverse * gain_grad))
    return lax.dot_general(
        grad.astype(BF16), x, (((0,), (0,)), ((), ())), preferred_element_type=F32
    ).astype(BF16)


def store_rows(orders, out_refs, x_ref, w_ref, gain_ref, u_ref):
    blocks = len(out_refs)
    block = w_ref.shape[1] // blocks
    for b in range(blocks):
        columns = slice(b * block, (b + 1) * block)
        term = term_rows(x_ref[...], w_ref[:, columns], gain_ref[:, columns], u_ref[:, columns])
        for source, target, count in orders[b]:
            out_refs[b][target : target + count] = term[source : source + count]


def term_kernel(
    piece, orders, sel_ref, x_hbm, w_hbm, gain_hbm, u_hbm, a_ref, b_ref, x_ref, w_ref, gain_ref, u_ref, sem
):
    parity = sel_ref[0]
    copies = [pltpu.make_async_copy(x_hbm, x_ref, sem.at[0])]
    for j in range(w_ref.shape[1] // piece):
        source = pl.ds(pl.multiple_of((2 * j + parity) * piece, piece), piece)
        target = pl.ds(j * piece, piece)
        for a, b in ((w_hbm, w_ref), (u_hbm, u_ref), (gain_hbm, gain_ref)):
            copies.append(pltpu.make_async_copy(a.at[:, source], b.at[:, target], sem.at[len(copies)]))
    for copy in copies:
        copy.start()
    for copy in copies:
        copy.wait()
    store_rows(orders, (a_ref, b_ref), x_ref, w_ref, gain_ref, u_ref)


def terms(piece, orders, parity, block_input, conv_weight, gain, out_cotangent, name):
    rows, width_in = block_input.shape
    channels = conv_weight.shape[1] // 2
    hbm = pl.BlockSpec(memory_space=pltpu.HBM)
    vmem = pl.BlockSpec(memory_space=pltpu.VMEM)
    term = pltpu.VMEM((channels // 2, width_in), BF16)

    def in_hbm(array):
        return pltpu.with_memory_space_constraint(array, pltpu.HBM)

    return pl.pallas_call(
        functools.partial(term_kernel, piece, orders),
        out_shape=(term, term),
        in_specs=[pl.BlockSpec(memory_space=pltpu.SMEM), hbm, hbm, hbm, hbm],
        out_specs=(vmem, vmem),
        scratch_shapes=[
            pltpu.VMEM((rows, width_in), BF16),
            pltpu.VMEM((width_in, channels), BF16),
            pltpu.VMEM((1, channels), F32),
            pltpu.VMEM((rows, channels), BF16),
            pltpu.SemaphoreType.DMA((1 + 3 * (channels // piece),)),
        ],
        cost_estimate=pl.CostEstimate(
            flops=4 * rows * channels * width_in,
            bytes_accessed=2 * (rows * channels + channels * width_in * 2 + rows * width_in),
            transcendentals=channels,
        ),
        compiler_params=pltpu.CompilerParams(vmem_limit_bytes=16 * 2**20),
        name=name,
    )(parity.reshape(1), in_hbm(block_input), in_hbm(conv_weight), in_hbm(gain), in_hbm(out_cotangent))


def pick(array, index, axis=0):
    return lax.dynamic_index_in_dim(array, index, axis, keepdims=False)


def shift_pairs(size, shift):
    return [(i, (i + shift) % size) for i in range(size)]


def flip_pairs(size, bit):
    return [(i, i ^ bit) for i in range(size)]


def local_fn(block_input, conv_weight, bn_gain, out_cotangent, master_weight, velocity):
    nodes = lax.axis_size(NODE)
    lanes = lax.axis_size(LOCAL)
    width_in = block_input.shape[1]
    width_out = conv_weight.shape[1]
    run = width_out // nodes
    part = run // lanes
    depth = nodes // 4
    half = depth // 2
    node = lax.axis_index(NODE)
    lane = lax.axis_index(LOCAL)
    core = node % 2
    side = (node // 2) % 2
    deep = node // 4

    gain = bn_gain.reshape(1, width_out)
    piece = run
    if run % TILE:
        piece = width_out // 2

        def split(array):
            rows = array.shape[0]
            return array.reshape(rows, nodes // 2, 2, run).swapaxes(1, 2).reshape(rows, width_out)

        conv_weight, out_cotangent, gain = split(conv_weight), split(out_cotangent), split(gain)
    shapes = ((lanes, half, 2, part, width_in), (2, half, lanes, part, width_in))
    if part % PACK:
        whole = [(0, 0, width_out // 4)]
        orders = (whole, whole)
    else:
        orders = ([], [])
        for z in range(half):
            for y in range(2):
                for l in range(lanes):
                    source = (z * 2 + y) * run + l * part
                    orders[0].append((source, ((l * half + z) * 2 + y) * part, part))
                    orders[1].append((source, ((y * half + z) * lanes + l) * part, part))
    inputs = (block_input, conv_weight, gain, out_cotangent)
    far = terms(piece, orders, 1 - core, *inputs, name="far_terms")

    def laid(array, chunk):
        if part % PACK == 0:
            return array.reshape(shapes[chunk])
        array = array.reshape(half, 2, lanes, part, width_in)
        return array.transpose((2, 0, 1, 3, 4) if chunk == 0 else (1, 0, 2, 3, 4))

    got = [laid(lax.ppermute(array, NODE, flip_pairs(nodes, 1)), c) for c, array in enumerate(far)]
    own = terms(piece, orders, core, *inputs, name="own_terms")
    own = [laid(array, c) for c, array in enumerate(own)]

    def chip(chunk, index):
        return pick(own[chunk], index).astype(F32) + pick(got[chunk], index).astype(F32)

    def over_lane(send, keep):
        arrived = [
            lax.ppermute(send((lane + s) % lanes).astype(BF16), LOCAL, shift_pairs(lanes, s))
            for s in range(1, lanes)
        ]
        total = keep(lane)
        for piece_ in arrived:
            total = total + piece_.astype(F32)
        return total

    def over_side(send, keep):
        arrived = lax.ppermute(send(1 - side).astype(BF16), NODE, flip_pairs(nodes, 2))
        return keep(side) + arrived.astype(F32)

    take = functools.partial(chip, 0)
    first = over_lane(take, take)
    take = functools.partial(chip, 1)
    second = over_side(take, take)
    take = functools.partial(pick, first, axis=1)
    first = over_side(take, take)
    take = functools.partial(pick, second, axis=1)
    second = over_lane(take, take)

    plane = jnp.concatenate([first, second], axis=0)
    total = pick(plane, deep)
    for s in range(1, depth):
        piece_ = pick(plane, (deep + s) % depth).astype(BF16)
        total = total + lax.ppermute(piece_, NODE, shift_pairs(nodes, 4 * s)).astype(F32)

    total = total.astype(BF16)
    pieces = [total] + [
        lax.ppermute(total, LOCAL, shift_pairs(lanes, -s)) for s in range(1, lanes)
    ]
    gradient = jnp.concatenate(
        [
            functools.reduce(
                lambda other, s: jnp.where((lane + s) % lanes == l, pieces[s], other),
                range(1, lanes),
                pieces[0],
            )
            for l in range(lanes)
        ],
        axis=0,
    ).astype(F32)
    new_velocity = MOMENTUM * velocity + gradient + DECAY * master_weight
    new_weight = master_weight - RATE * new_velocity
    return (new_velocity, new_weight)


def solution(mesh):
    in_specs = (
        P((NODE, LOCAL), None),
        P(),
        P(),
        P((NODE, LOCAL), None),
        P(NODE, None),
        P(NODE, None),
    )
    out_specs = (P(NODE, None), P(NODE, None))
    return jax.shard_map(local_fn, mesh=mesh, in_specs=in_specs, out_specs=out_specs, check_vma=False)
```

time: 47.8 us -> 41.4 us (0.87)
  local copies, waits for them, and re-layouts: 5.96 us -> 0.23 us
  Pallas kernels: 8.34 us -> 7.82 us
    unnamed x12 -> x4, local copies, waits for them, and re-layouts: 4.7 us -> 0.01 us
    dynamic_slice x4, local copies, waits for them, and re-layouts: 1.2 us -> 0.17 us  [pick(): return lax.dynamic_index_in_dim(array, index, axis, keepdims=False)]
    pallas_call x2, Pallas kernels: 8.34 us -> 7.82 us  [terms(): pl.pallas_call(functools.partial(term_kernel, piece, orders), out_shape=(...]
  transfers between devices with their start and end apart: 10 -> 10, of which waited for: 7 -> 7; matrix products, arithmetic and copies ran while one was open for 3% -> 1% of each run, Pallas kernels for 9% -> 9%
where the time goes in v2:
time: 41.4 us; the launch traced here: 41.2 us
  waiting for transfers between devices  16.1 us (39%)
  starting transfers between devices  14.8 us (36%)
  Pallas kernels  7.82 us (19%)
  other arithmetic  1.4 us (3%)
  between operations  0.89 us (2%)
    pallas_call x2, Pallas kernels, terms(): pl.pallas_call(functools.partial(term_kernel, piece, orders), out_shape=(...  7.82 us
    ppermute x2, waiting for transfers between devices, over_lane(): lax.ppermute(send((lane + s) % lanes).astype(BF16), LOCAL, shift_pairs(la...  6.79 us
    ppermute x3, waiting for transfers between devices, local_fn(): lax.ppermute(piece_, NODE, shift_pairs(nodes, 4 * s)).astype(F32)  5.05 us
    ppermute x3, starting transfers between devices, local_fn(): lax.ppermute(piece_, NODE, shift_pairs(nodes, 4 * s)).astype(F32)  4.67 us
    ppermute x2, starting transfers between devices, over_lane(): lax.ppermute(send((lane + s) % lanes).astype(BF16), LOCAL, shift_pairs(la...  4.55 us
    ppermute x2, starting transfers between devices, over_side(): lax.ppermute(send(1 - side).astype(BF16), NODE, flip_pairs(nodes, 2))  3.42 us
    ppermute x1, waiting for transfers between devices, local_fn(): lax.ppermute(total, LOCAL, shift_pairs(lanes, -s))  2.78 us
    ppermute x1, starting transfers between devices, local_fn(): lax.ppermute(total, LOCAL, shift_pairs(lanes, -s))  1.55 us
  transfers between devices with their start and end apart: 10, of which 7 were waited for; matrix products, arithmetic and copies ran while one was open for 1% of the time, Pallas kernels for 9%

profile of v2, /device:TPU:0, one launch (start us, length us, event | category | flops | bytes accessed | tf_op | source)
XLA Modules:
  0.0 41.2 jit_solution(16404716495993358389)
XLA Ops:
  0.6 3.9 %far_terms.1 = (bf16[512,512]{1,0:T(8,128)(2,1)S(1)}, bf16[512,512]{1,0:T(8,128)(2,1)S(1)}) custom-call(s32[1]{0:T(128)} %bitcast.3.sel_ref, bf16[392,512]{1,0:T(8,128)(2,1)} %x_hbm.3, bf16[512,2048]{1,0:T(8,128)(2,1)} %w_hbm.3, f32[1,2048]{1,0:T(1,128)} %bitcast.43, bf16[392,2048]{1,0:T(8,128)(2,1)} %u_hbm.3), custom_call_target="tpu_custom_call" | custom-call | flops 822083584 | bytes 3301376 | tf_op jit(solution)/shard_map/far_terms/pallas_call | solution.py:77
  4.6 0.5 %collective-permute-start = (bf16[512,512]{1,0:T(8,128)(2,1)S(1)}, bf16[512,512]{1,0:T(8,128)(2,1)S(1)}, u32[]{:S(2)}, u32[]{:S(2)}) collective-permute-start(bf16[512,512]{1,0:T(8,128)(2,1)S(1)} %get-tuple-element.7), channel_id=1, source_target_pairs={{0,2},{2,0},{4,6},{6,4},{8,10},{10,8},{12,14},{14,12},{16,18},{18,... | collective-permute-start | bytes 1572872 | tf_op jit(solution)/shard_map/ppermute | solution.py:157
  5.1 0.1 collective-permute-start.3
  5.2 3.9 %own_terms.1 = (bf16[512,512]{1,0:T(8,128)(2,1)S(1)}, bf16[512,512]{1,0:T(8,128)(2,1)S(1)}) custom-call(s32[1]{0:T(128)} %bitcast.sel_ref, bf16[392,512]{1,0:T(8,128)(2,1)} %x_hbm.3, bf16[512,2048]{1,0:T(8,128)(2,1)} %w_hbm.3, f32[1,2048]{1,0:T(1,128)} %bitcast.44, bf16[392,2048]{1,0:T(8,128)(2,1)} %u_hbm.3), custom_call_target="tpu_custom_call" | custom-call | flops 822083584 | bytes 3301376 | tf_op jit(solution)/shard_map/own_terms/pallas_call | solution.py:77
  9.3 0.0 collective-permute-done
  9.3 0.1 fusion
  9.4 3.0 %collective-permute-start.1 = (bf16[2,2,64,512]{3,2,0,1:T(8,128)(2,1)S(1)}, bf16[2,2,64,512]{3,2,0,1:T(8,128)(2,1)S(1)}, u32[]{:S(2)}, u32[]{:S(2)}) collective-permute-start(bf16[2,2,64,512]{3,2,0,1:T(8,128)(2,1)S(1)} %fusion), channel_id=1, source_target_pairs={{0,1},{1,0},{2,3},{3,2},{4,5},{5,4},{6,7},{7,6},{8,9},{9,8},{10,11... | collective-permute-start | bytes 786440 | tf_op jit(solution)/shard_map/ppermute | solution.py:166
  12.4 0.0 collective-permute-done.3
  12.4 0.1 fusion.1
  12.5 1.6 %collective-permute-start.4 = (bf16[2,2,64,512]{3,2,0,1:T(8,128)(2,1)S(1)}, bf16[2,2,64,512]{3,2,0,1:T(8,128)(2,1)S(1)}, u32[]{:S(2)}, u32[]{:S(2)}) collective-permute-start(bf16[2,2,64,512]{3,2,0,1:T(8,128)(2,1)S(1)} %fusion.1), channel_id=1, source_target_pairs={{0,4},{2,6},{4,0},{6,2},{8,12},{10,14},{12,8},{14,10},{16,20},{18,... | collective-permute-start | bytes 786440 | tf_op jit(solution)/shard_map/ppermute | solution.py:175
  14.1 4.8 %collective-permute-done.1 = bf16[2,2,64,512]{3,2,0,1:T(8,128)(2,1)S(1)} collective-permute-done((bf16[2,2,64,512]{3,2,0,1:T(8,128)(2,1)S(1)}, bf16[2,2,64,512]{3,2,0,1:T(8,128)(2,1)S(1)}, u32[]{:S(2)}, u32[]{:S(2)}) %collective-permute-start.1) | collective-permute-done | bytes 262176 | tf_op jit(solution)/shard_map/ppermute | solution.py:166
  18.9 0.1 bitcast_add_fusion.1
  19.1 1.8 %collective-permute-start.2 = (bf16[2,64,512]{2,1,0:T(8,128)(2,1)S(1)}, bf16[2,64,512]{2,1,0:T(8,128)(2,1)S(1)}, u32[]{:S(2)}, u32[]{:S(2)}) collective-permute-start(bf16[2,64,512]{2,1,0:T(8,128)(2,1)S(1)} %fusion.2), channel_id=1, source_target_pairs={{0,4},{2,6},{4,0},{6,2},{8,12},{10,14},{12,8},{14,10},{16,20},{18,... | collective-permute-start | bytes 393224 | tf_op jit(solution)/shard_map/ppermute | solution.py:175
  20.9 0.0 collective-permute-done.4
  20.9 0.0 copy-start
  20.9 0.0 copy-start.1
  20.9 0.1 bitcast_add_fusion
  21.1 1.6 %collective-permute-start.5 = (bf16[2,64,512]{2,1,0:T(8,128)(2,1)S(1)}, bf16[2,64,512]{2,1,0:T(8,128)(2,1)S(1)}, u32[]{:S(2)}, u32[]{:S(2)}) collective-permute-start(bf16[2,64,512]{2,1,0:T(8,128)(2,1)S(1)} %fusion.3), channel_id=1, source_target_pairs={{0,1},{1,0},{2,3},{3,2},{4,5},{5,4},{6,7},{7,6},{8,9},{9,8},{10,11... | collective-permute-start | bytes 393224 | tf_op jit(solution)/shard_map/ppermute | solution.py:166
  22.6 1.5 %collective-permute-done.2 = bf16[2,64,512]{2,1,0:T(8,128)(2,1)S(1)} collective-permute-done((bf16[2,64,512]{2,1,0:T(8,128)(2,1)S(1)}, bf16[2,64,512]{2,1,0:T(8,128)(2,1)S(1)}, u32[]{:S(2)}, u32[]{:S(2)}) %collective-permute-start.2) | collective-permute-done | bytes 131104 | tf_op jit(solution)/shard_map/ppermute | solution.py:175
  24.1 1.9 %collective-permute-done.5 = bf16[2,64,512]{2,1,0:T(8,128)(2,1)S(1)} collective-permute-done((bf16[2,64,512]{2,1,0:T(8,128)(2,1)S(1)}, bf16[2,64,512]{2,1,0:T(8,128)(2,1)S(1)}, u32[]{:S(2)}, u32[]{:S(2)}) %collective-permute-start.5) | collective-permute-done | bytes 131104 | tf_op jit(solution)/shard_map/ppermute | solution.py:166
  26.1 0.1 fusion.17
  26.2 3.7 %collective-permute-start.8 = (bf16[64,512]{1,0:T(8,128)(2,1)S(1)}, bf16[64,512]{1,0:T(8,128)(2,1)S(1)}, u32[]{:S(2)}, u32[]{:S(2)}) collective-permute-start(bf16[64,512]{1,0:T(8,128)(2,1)S(1)} %get-tuple-element.14), channel_id=1, source_target_pairs={{0,24},{2,26},{4,28},{6,30},{8,0},{10,2},{12,4},{14,6},{16,8},{18,... | collective-permute-start | bytes 196616 | tf_op jit(solution)/shard_map/ppermute | solution.py:191
  29.9 0.0 collective-permute-start.7
  29.9 1.0 %collective-permute-start.6 = (bf16[64,512]{1,0:T(8,128)(2,1)S(1)}, bf16[64,512]{1,0:T(8,128)(2,1)S(1)}, u32[]{:S(2)}, u32[]{:S(2)}) collective-permute-start(bf16[64,512]{1,0:T(8,128)(2,1)S(1)} %get-tuple-element.12), channel_id=1, source_target_pairs={{0,8},{2,10},{4,12},{6,14},{8,16},{10,18},{12,20},{14,22},{16,24},... | collective-permute-start | bytes 196616 | tf_op jit(solution)/shard_map/ppermute | solution.py:191
  30.9 0.9 %collective-permute-done.8 = bf16[64,512]{1,0:T(8,128)(2,1)S(1)} collective-permute-done((bf16[64,512]{1,0:T(8,128)(2,1)S(1)}, bf16[64,512]{1,0:T(8,128)(2,1)S(1)}, u32[]{:S(2)}, u32[]{:S(2)}) %collective-permute-start.8) | collective-permute-done | bytes 65568 | tf_op jit(solution)/shard_map/ppermute | solution.py:191
  31.8 3.3 %collective-permute-done.7 = bf16[64,512]{1,0:T(8,128)(2,1)S(1)} collective-permute-done((bf16[64,512]{1,0:T(8,128)(2,1)S(1)}, bf16[64,512]{1,0:T(8,128)(2,1)S(1)}, u32[]{:S(2)}, u32[]{:S(2)}) %collective-permute-start.7) | collective-permute-done | bytes 65568 | tf_op jit(solution)/shard_map/ppermute | solution.py:191
  35.0 0.9 %collective-permute-done.6 = bf16[64,512]{1,0:T(8,128)(2,1)S(1)} collective-permute-done((bf16[64,512]{1,0:T(8,128)(2,1)S(1)}, bf16[64,512]{1,0:T(8,128)(2,1)S(1)}, u32[]{:S(2)}, u32[]{:S(2)}) %collective-permute-start.6) | collective-permute-done | bytes 65568 | tf_op jit(solution)/shard_map/ppermute | solution.py:191
  36.0 1.6 %collective-permute-start.9 = (bf16[64,512]{1,0:T(8,128)(2,1)S(1)}, bf16[64,512]{1,0:T(8,128)(2,1)S(1)}, u32[]{:S(2)}, u32[]{:S(2)}) collective-permute-start(bf16[64,512]{1,0:T(8,128)(2,1)S(1)} %fusion.11), channel_id=1, source_target_pairs={{0,1},{1,0},{2,3},{3,2},{4,5},{5,4},{6,7},{7,6},{8,9},{9,8},{10,11... | collective-permute-start | bytes 196616 | tf_op jit(solution)/shard_map/ppermute | solution.py:195
  37.5 2.8 %collective-permute-done.9 = bf16[64,512]{1,0:T(8,128)(2,1)S(1)} collective-permute-done((bf16[64,512]{1,0:T(8,128)(2,1)S(1)}, bf16[64,512]{1,0:T(8,128)(2,1)S(1)}, u32[]{:S(2)}, u32[]{:S(2)}) %collective-permute-start.9) | collective-permute-done | bytes 65568 | tf_op jit(solution)/shard_map/ppermute | solution.py:195
  40.3 0.0 copy-done
  40.4 0.0 copy-done.1
  40.4 0.9 %multiply_subtract_fusion = (f32[128,512]{1,0:T(8,128)}, f32[128,512]{1,0:T(8,128)}) fusion(f32[128,512]{1,0:T(8,128)S(1)} %copy-done, bf16[64,512]{1,0:T(8,128)(2,1)S(1)} %get-tuple-element.24, bf16[64,512]{1,0:T(8,128)(2,1)S(1)} %get-tuple-element.23, f32[128,512]{1,0:T(8,128)S(1)} %copy-done.1), kind=kLoop, calls=%fused_computation.16 | loop fusion | flops 655360 | bytes 1179648 | tf_op jit(solution)/shard_map/sub | solution.py:209
  (10 shorter events, 0.3 us)
Async XLA Ops:
  4.6 4.7 %collective-permute-start = (bf16[512,512]{1,0:T(8,128)(2,1)S(1)}, bf16[512,512]{1,0:T(8,128)(2,1)S(1)}, u32[]{:S(2)}, u32[]{:S(2)}) collective-permute-start(bf16[512,512]{1,0:T(8,128)(2,1)S(1)} %get-tuple-element.7), channel_id=1, source_target_pairs={{0,2},{2,0},{4,6},{6,4},{8,10},{10,8},{12,14},{14,12},{16,18},{18,... | collective-permute-start | bytes 1572872 | tf_op jit(solution)/shard_map/ppermute | solution.py:157
  5.1 7.3 %collective-permute-start.3 = (bf16[512,512]{1,0:T(8,128)(2,1)S(1)}, bf16[512,512]{1,0:T(8,128)(2,1)S(1)}, u32[]{:S(2)}, u32[]{:S(2)}) collective-permute-start(bf16[512,512]{1,0:T(8,128)(2,1)S(1)} %get-tuple-element.9), channel_id=1, source_target_pairs={{0,2},{2,0},{4,6},{6,4},{8,10},{10,8},{12,14},{14,12},{16,18},{18,... | collective-permute-start | bytes 1572872 | tf_op jit(solution)/shard_map/ppermute | solution.py:157
  9.4 9.5 %collective-permute-start.1 = (bf16[2,2,64,512]{3,2,0,1:T(8,128)(2,1)S(1)}, bf16[2,2,64,512]{3,2,0,1:T(8,128)(2,1)S(1)}, u32[]{:S(2)}, u32[]{:S(2)}) collective-permute-start(bf16[2,2,64,512]{3,2,0,1:T(8,128)(2,1)S(1)} %fusion), channel_id=1, source_target_pairs={{0,1},{1,0},{2,3},{3,2},{4,5},{5,4},{6,7},{7,6},{8,9},{9,8},{10,11... | collective-permute-start | bytes 786440 | tf_op jit(solution)/shard_map/ppermute | solution.py:166
  12.5 8.4 %collective-permute-start.4 = (bf16[2,2,64,512]{3,2,0,1:T(8,128)(2,1)S(1)}, bf16[2,2,64,512]{3,2,0,1:T(8,128)(2,1)S(1)}, u32[]{:S(2)}, u32[]{:S(2)}) collective-permute-start(bf16[2,2,64,512]{3,2,0,1:T(8,128)(2,1)S(1)} %fusion.1), channel_id=1, source_target_pairs={{0,4},{2,6},{4,0},{6,2},{8,12},{10,14},{12,8},{14,10},{16,20},{18,... | collective-permute-start | bytes 786440 | tf_op jit(solution)/shard_map/ppermute | solution.py:175
  19.1 5.0 %collective-permute-start.2 = (bf16[2,64,512]{2,1,0:T(8,128)(2,1)S(1)}, bf16[2,64,512]{2,1,0:T(8,128)(2,1)S(1)}, u32[]{:S(2)}, u32[]{:S(2)}) collective-permute-start(bf16[2,64,512]{2,1,0:T(8,128)(2,1)S(1)} %fusion.2), channel_id=1, source_target_pairs={{0,4},{2,6},{4,0},{6,2},{8,12},{10,14},{12,8},{14,10},{16,20},{18,... | collective-permute-start | bytes 393224 | tf_op jit(solution)/shard_map/ppermute | solution.py:175
  20.9 19.4 %copy-start = (f32[128,512]{1,0:T(8,128)S(1)}, f32[128,512]{1,0:T(8,128)}, u32[]{:S(2)}) copy-start(f32[128,512]{1,0:T(8,128)} %param.10) | copy-start | bytes 786436
  20.9 19.4 %copy-start.1 = (f32[128,512]{1,0:T(8,128)S(1)}, f32[128,512]{1,0:T(8,128)}, u32[]{:S(2)}) copy-start(f32[128,512]{1,0:T(8,128)} %param.11) | copy-start | bytes 786436
  21.1 5.0 %collective-permute-start.5 = (bf16[2,64,512]{2,1,0:T(8,128)(2,1)S(1)}, bf16[2,64,512]{2,1,0:T(8,128)(2,1)S(1)}, u32[]{:S(2)}, u32[]{:S(2)}) collective-permute-start(bf16[2,64,512]{2,1,0:T(8,128)(2,1)S(1)} %fusion.3), channel_id=1, source_target_pairs={{0,1},{1,0},{2,3},{3,2},{4,5},{5,4},{6,7},{7,6},{8,9},{9,8},{10,11... | collective-permute-start | bytes 393224 | tf_op jit(solution)/shard_map/ppermute | solution.py:166
  26.2 5.6 %collective-permute-start.8 = (bf16[64,512]{1,0:T(8,128)(2,1)S(1)}, bf16[64,512]{1,0:T(8,128)(2,1)S(1)}, u32[]{:S(2)}, u32[]{:S(2)}) collective-permute-start(bf16[64,512]{1,0:T(8,128)(2,1)S(1)} %get-tuple-element.14), channel_id=1, source_target_pairs={{0,24},{2,26},{4,28},{6,30},{8,0},{10,2},{12,4},{14,6},{16,8},{18,... | collective-permute-start | bytes 196616 | tf_op jit(solution)/shard_map/ppermute | solution.py:191
  29.9 5.2 %collective-permute-start.7 = (bf16[64,512]{1,0:T(8,128)(2,1)S(1)}, bf16[64,512]{1,0:T(8,128)(2,1)S(1)}, u32[]{:S(2)}, u32[]{:S(2)}) collective-permute-start(bf16[64,512]{1,0:T(8,128)(2,1)S(1)} %get-tuple-element.13), channel_id=1, source_target_pairs={{0,16},{2,18},{4,20},{6,22},{8,24},{10,26},{12,28},{14,30},{16,0},... | collective-permute-start | bytes 196616 | tf_op jit(solution)/shard_map/ppermute | solution.py:191
  29.9 6.1 %collective-permute-start.6 = (bf16[64,512]{1,0:T(8,128)(2,1)S(1)}, bf16[64,512]{1,0:T(8,128)(2,1)S(1)}, u32[]{:S(2)}, u32[]{:S(2)}) collective-permute-start(bf16[64,512]{1,0:T(8,128)(2,1)S(1)} %get-tuple-element.12), channel_id=1, source_target_pairs={{0,8},{2,10},{4,12},{6,14},{8,16},{10,18},{12,20},{14,22},{16,24},... | collective-permute-start | bytes 196616 | tf_op jit(solution)/shard_map/ppermute | solution.py:191
  36.0 4.3 %collective-permute-start.9 = (bf16[64,512]{1,0:T(8,128)(2,1)S(1)}, bf16[64,512]{1,0:T(8,128)(2,1)S(1)}, u32[]{:S(2)}, u32[]{:S(2)}) collective-permute-start(bf16[64,512]{1,0:T(8,128)(2,1)S(1)} %fusion.11), channel_id=1, source_target_pairs={{0,1},{1,0},{2,3},{3,2},{4,5},{5,4},{6,7},{7,6},{8,9},{9,8},{10,11... | collective-permute-start | bytes 196616 | tf_op jit(solution)/shard_map/ppermute | solution.py:195

commit v3 on v0

v3 whole, which is shorter than its diff:
```python
import functools

import jax
import jax.numpy as jnp
from jax import lax
from jax.experimental import pallas as pl
from jax.experimental.pallas import tpu as pltpu
from jax.sharding import PartitionSpec as P

EPS = 1e-05
MOMENTUM = 0.9
RATE = 0.1
DECAY = 5e-05

TILE = 128
NODE = "node"
LOCAL = "local"
F32 = jnp.float32
BF16 = jnp.bfloat16


def term_kernel(
    piece, column, blocks, parity_ref, half_ref, x_hbm, w_hbm, gain_hbm, u_hbm, *refs
):
    *out_refs, x_ref, w_ref, gain_ref, u_ref, conv_ref, grad_ref, sem = refs
    parity, half = parity_ref[0], half_ref[0]
    rows = x_hbm.shape[0]
    channels = w_ref.shape[1]
    block = channels // blocks

    copies = [pltpu.make_async_copy(x_hbm, x_ref, sem.at[0])]
    for k in range(channels // piece):
        source = pl.ds(pl.multiple_of(column(k, parity, half) * piece, piece), piece)
        target = pl.ds(k * piece, piece)
        for a, b in ((w_hbm, w_ref), (u_hbm, u_ref), (gain_hbm, gain_ref)):
            copies.append(pltpu.make_async_copy(a.at[:, source], b.at[:, target], sem.at[len(copies)]))
    for copy in copies:
        copy.start()
    for copy in copies:
        copy.wait()

    def columns(b):
        return slice(b * block, (b + 1) * block)

    def convolve(b):
        conv_ref[b] = jnp.dot(x_ref[...], w_ref[:, columns(b)], preferred_element_type=F32)

    def differentiate(b):
        conv = conv_ref[b]
        center = jnp.sum(conv, axis=0, keepdims=True) * (1.0 / rows)
        spread = conv - center
        upstream = u_ref[:, columns(b)].astype(F32)
        inverse = lax.rsqrt(jnp.sum(spread * spread, axis=0, keepdims=True) * (1.0 / rows) + EPS)
        shift_grad = jnp.sum(upstream, axis=0, keepdims=True)
        gain_grad = jnp.sum(upstream * spread, axis=0, keepdims=True) * inverse
        scale = gain_ref[:, columns(b)] * inverse
        step = scale * (1.0 / rows)
        grad = scale * upstream - (step * shift_grad + spread * (step * inverse * gain_grad))
        grad_ref[b] = grad.astype(BF16)

    def contract(b):
        term = lax.dot_general(
            grad_ref[b], x_ref[...], (((0,), (0,)), ((), ())), preferred_element_type=F32
        ).astype(BF16)
        share = channels // len(out_refs)
        count = min(block, share)
        for row in range(0, block, count):
            to, at = divmod(b * block + row, share)
            out_refs[to][at : at + count] = term[row : row + count]

    for i in range(blocks + 2):
        if 0 <= i - 2:
            contract(i - 2)
        if i < blocks:
            convolve(i)
        if 0 <= i - 1 < blocks:
            differentiate(i - 1)


def terms(name, outs, channels, blocks, piece, column, weight, parity, half, block_input, conv_weight, gain, out_cotangent):
    rows, width_in = block_input.shape
    block = channels // blocks
    hbm = pl.BlockSpec(memory_space=pltpu.HBM)
    smem = pl.BlockSpec(memory_space=pltpu.SMEM)

    def in_hbm(array):
        return pltpu.with_memory_space_constraint(array, pltpu.HBM)

    return pl.pallas_call(
        functools.partial(term_kernel, piece, column, blocks),
        out_shape=(pltpu.VMEM((channels // outs, width_in), BF16),) * outs,
        in_specs=[smem, smem, hbm, hbm, hbm, hbm],
        out_specs=(pl.BlockSpec(memory_space=pltpu.VMEM),) * outs,
        scratch_shapes=[
            pltpu.VMEM((rows, width_in), BF16),
            pltpu.VMEM((width_in, channels), BF16),
            pltpu.VMEM((1, channels), F32),
            pltpu.VMEM((rows, channels), BF16),
            pltpu.VMEM((blocks, rows, block), F32),
            pltpu.VMEM((blocks, rows, block), BF16),
            pltpu.SemaphoreType.DMA((1 + 3 * (channels // piece),)),
        ],
        cost_estimate=pl.CostEstimate(
            flops=max(1, int(weight * 4 * rows * channels * width_in)),
            bytes_accessed=max(1, int(weight * 2 * (rows * channels + channels * width_in * 2 + rows * width_in))),
            transcendentals=max(1, int(weight * channels)),
        ),
        compiler_params=pltpu.CompilerParams(vmem_limit_bytes=16 * 2**20),
        name=name,
    )(
        parity.reshape(1),
        half.reshape(1),
        in_hbm(block_input),
        in_hbm(conv_weight),
        in_hbm(gain),
        in_hbm(out_cotangent),
    )


def pick(array, *index):
    start = [jnp.asarray(i).astype(jnp.uint32) for i in index]
    rest = array.shape[len(index) :]
    start += [jnp.uint32(0)] * len(rest)
    return lax.dynamic_slice(array, start, (1,) * len(index) + rest).reshape(rest)


def send(array, pairs):
    return lax.ppermute(array.astype(BF16), (NODE, LOCAL), pairs)


def wide(*arrays):
    return functools.reduce(lambda a, b: a + b, [a.astype(F32) for a in arrays])


def local_fn(block_input, conv_weight, bn_gain, out_cotangent, master_weight, velocity):
    nodes = lax.axis_size(NODE)
    lanes = lax.axis_size(LOCAL)
    run = conv_weight.shape[1] // nodes
    inputs = (block_input, conv_weight, bn_gain.reshape(1, -1), out_cotangent)
    if (nodes, lanes) == (16, 2) and run % TILE == 0:
        gradient, (master_weight, velocity) = sum_halves(run, *inputs, (master_weight, velocity))
    else:
        gradient = sum_lanes(run, *inputs)
    new_velocity = MOMENTUM * velocity + gradient + DECAY * master_weight
    new_weight = master_weight - RATE * new_velocity
    return (new_velocity, new_weight)


def sum_halves(run, block_input, conv_weight, gain, out_cotangent, state):
    width_in = block_input.shape[1]
    inputs = (block_input, conv_weight, gain, out_cotangent)
    node = lax.axis_index(NODE)
    core, side, low, high = node & 1, (node >> 1) & 1, (node >> 2) & 1, node >> 3
    is_one = core == 1
    first = jnp.where(is_one, low, side)
    second = jnp.where(is_one, side, low)

    def column(k, parity, half):
        half, k = (half, k) if k < 4 else (1 - half, k - 4)
        zero = (((k % 2) * 2 + k // 2) * 2 + half) * 2
        one = (((k % 2) * 2 + half) * 2 + k // 2) * 2 + 1
        return jnp.where(parity == 1, one, zero)

    def flip(array, zero, one):
        return send(array, [(i, i ^ (one if i & 2 else zero)) for i in range(32)])

    def node_terms(name, count, parity, half, weight):
        halves = count // 4
        return terms(name, halves, count * run, halves, run, column, weight, parity, half, *inputs)

    far_sent, far_kept = node_terms("far_terms", 8, 1 - core, 1 - second, 1)
    got_sent = flip(far_sent, 2, 2)
    got = flip(far_kept, 2, 2).reshape(2, 2, run, width_in)
    (own_sent,) = node_terms("own_sent", 4, core, 1 - first, 1)
    sent, core, kept = lax.optimization_barrier((wide(own_sent, got_sent).astype(BF16), core, first))
    arrived = flip(sent, 4, 8).reshape(2, 2, run, width_in)
    own = node_terms("own_kept", 4, core, kept, 1)[0].reshape(2, 2, run, width_in)

    def half_of(index):
        return wide(pick(own, index), pick(got, index), pick(arrived, index))

    again = flip(half_of(1 - second), 8, 4)
    plane = wide(half_of(second), again)
    plane, *state = lax.optimization_barrier((plane, *state))
    both = wide(pick(plane, high), flip(pick(plane, 1 - high), 16, 16)).astype(BF16)
    return wide(both, flip(both, 1, 1)), state


def sum_lanes(run, block_input, conv_weight, gain, out_cotangent):
    nodes = lax.axis_size(NODE)
    lanes = lax.axis_size(LOCAL)
    devices = nodes * lanes
    width_in = block_input.shape[1]
    width_out = conv_weight.shape[1]
    node = lax.axis_index(NODE)
    lane = lax.axis_index(LOCAL)
    core, side, deep = node % 2, (node // 2) % 2, node // 4
    depth = nodes // 4

    def split(array):
        rows = array.shape[0]
        return array.reshape(rows, nodes // 2, 2, run).swapaxes(1, 2).reshape(rows, width_out)

    inputs = (block_input, split(conv_weight), split(gain), split(out_cotangent))

    def chip_terms(name, parity):
        half = width_out // 2
        return terms(name, 1, half, 2, half, lambda k, parity, half: parity, 1, parity, parity, *inputs)[0]

    def laid(array):
        return array.reshape(depth, 2, lanes, run // lanes, width_in).transpose(2, 1, 0, 3, 4)

    got = laid(send(chip_terms("far_terms", 1 - core), [(i, i ^ lanes) for i in range(devices)]))
    own = laid(chip_terms("own_terms", core))
    half = wide(pick(own, lane), pick(got, lane))
    for s in range(1, lanes):
        to = (lane + s) % lanes
        pairs = [(i, i - i % lanes + (i + s) % lanes) for i in range(devices)]
        half = wide(half, send(wide(pick(own, to), pick(got, to)), pairs))
    other = send(pick(half, 1 - side), [(i, i ^ (2 * lanes)) for i in range(devices)])
    plane = wide(pick(half, side), other)
    total = pick(plane, deep)
    for s in range(1, depth):
        pairs = [(i, (i + 4 * s * lanes) % devices) for i in range(devices)]
        total = wide(total, send(pick(plane, (deep + s) % depth), pairs))
    total = total.astype(BF16)
    pieces = [total] + [
        send(total, [(i, i - i % lanes + (i - s) % lanes) for i in range(devices)]) for s in range(1, lanes)
    ]
    return jnp.concatenate(
        [
            functools.reduce(
                lambda other, s: jnp.where((lane + s) % lanes == l, pieces[s], other),
                range(1, lanes),
                pieces[0],
            )
            for l in range(lanes)
        ],
        axis=0,
    ).astype(F32)


def solution(mesh):
    in_specs = (
        P((NODE, LOCAL), None),
        P(),
        P(),
        P((NODE, LOCAL), None),
        P(NODE, None),
        P(NODE, None),
    )
    out_specs = (P(NODE, None), P(NODE, None))
    return jax.shard_map(local_fn, mesh=mesh, in_specs=in_specs, out_specs=out_specs, check_vma=False)
```

time: 345 us -> 38.5 us (0.11)
  waiting for transfers between devices: 301 us -> 17.2 us
  between operations: 13.9 us -> 0.74 us
  matrix products: 11.1 us -> 0 us
  other arithmetic: 11.6 us -> 1.27 us
  starting transfers between devices: 0.21 us -> 10.5 us
  Pallas kernels: 0 us -> 8.61 us
  local copies, waits for them, and re-layouts: 6.37 us -> 0.04 us
    reduce_scatter x4 -> x0, waiting for transfers between devices: 235 us -> none  [reduce_shards(): return lax.psum_scatter(summed, 'node', scatter_dimension=1, tiled=True)]
    psum x1 -> x0, waiting for transfers between devices: 66.3 us -> none  [reduce_shards(): lax.psum(contribution.astype(jnp.bfloat16), 'local').astype(jnp.float32)]
    ppermute x0 -> x6, waiting for transfers between devices: none -> 17.2 us  [send(): return lax.ppermute(array.astype(BF16), (NODE, LOCAL), pairs)]
    dot_general x5 -> x0, matrix products: 11.1 us -> none  [the longest x4 9.14 us: local(): lax.dot_general(columns, block_input, contract, preferred_element_type=jn...]
    ppermute x0 -> x6, starting transfers between devices: none -> 10.5 us  [send(): return lax.ppermute(array.astype(BF16), (NODE, LOCAL), pairs)]
    pallas_call x0 -> x3, Pallas kernels: none -> 8.61 us  [terms(): pl.pallas_call(functools.partial(term_kernel, piece, column, blocks), out...]
    convert_element_type x5 -> x3, other arithmetic: 8.73 us -> 0.26 us  [the longest x1 0.13 us: sum_halves(): wide(own_sent, got_sent).astype(BF16)]
    convert_element_type x1, local copies, waits for them, and re-layouts: 3.79 us -> 0.03 us  [send(): return lax.ppermute(array.astype(BF16), (NODE, LOCAL), pairs)]
  transfers between devices with their start and end apart: 5 -> 6, of which waited for: 5 -> 4; matrix products, arithmetic and copies ran while one was open for 1% -> 0% of each run, Pallas kernels for 0% -> 13%
where the time goes in v3:
time: 38.5 us; the launch traced here: 38.3 us
  waiting for transfers between devices  17.2 us (45%)
  starting transfers between devices  10.5 us (27%)
  Pallas kernels  8.61 us (22%)
  other arithmetic  1.27 us (3%)
  between operations  0.74 us (2%)
    ppermute x6, waiting for transfers between devices, send(): return lax.ppermute(array.astype(BF16), (NODE, LOCAL), pairs)  17.2 us
    ppermute x6, starting transfers between devices, send(): return lax.ppermute(array.astype(BF16), (NODE, LOCAL), pairs)  10.5 us
    pallas_call x3, Pallas kernels, terms(): pl.pallas_call(functools.partial(term_kernel, piece, column, blocks), out...  8.61 us
    sub x1, other arithmetic, local_fn(): new_weight = master_weight - RATE * new_velocity  0.88 us
  transfers between devices with their start and end apart: 6, of which 4 were waited for; matrix products, arithmetic and copies ran while one was open for 0% of the time, Pallas kernels for 13%

profile of v3, /device:TPU:0, one launch (start us, length us, event | category | flops | bytes accessed | tf_op | source)
XLA Modules:
  0.0 38.3 jit_solution(5325478930973554801)
XLA Ops:
  0.6 3.5 %far_terms.1 = (bf16[512,512]{1,0:T(8,128)(2,1)S(1)}, bf16[512,512]{1,0:T(8,128)(2,1)S(1)}) custom-call(s32[1]{0:T(128)} %bitcast.3.parity_ref, s32[1]{0:T(128)} %bitcast.4.half_ref, bf16[392,512]{1,0:T(8,128)(2,1)} %x_hbm.5, bf16[512,2048]{1,0:T(8,128)(2,1)} %w_hbm.5, f32[1,2048]{1,0:T(1,128)} %bitcast.26, bf16[392,2048]{1,0:T(8,128)(2,1)} %u_hbm.5), custom_call_target="tpu_custom_call" | custom-call | flops 822083584 | bytes 3301376 | tf_op jit(solution)/shard_map/far_terms/pallas_call | solution.py:89
  4.2 0.5 %collective-permute-start = (bf16[512,512]{1,0:T(8,128)(2,1)S(1)}, bf16[512,512]{1,0:T(8,128)(2,1)S(1)}, u32[]{:S(2)}, u32[]{:S(2)}) collective-permute-start(bf16[512,512]{1,0:T(8,128)(2,1)S(1)} %get-tuple-element.10), channel_id=1, source_target_pairs={{0,2},{1,3},{2,0},{3,1},{4,6},{5,7},{6,4},{7,5},{8,10},{9,11},{10,... | collective-permute-start | bytes 1572872 | tf_op jit(solution)/shard_map/ppermute | solution.py:128
  4.7 0.1 collective-permute-start.1
  4.8 2.5 %own_sent.1 = bf16[512,512]{1,0:T(8,128)(2,1)S(1)} custom-call(s32[1]{0:T(128)} %bitcast.parity_ref, s32[1]{0:T(128)} %bitcast.1.half_ref, bf16[392,512]{1,0:T(8,128)(2,1)} %x_hbm.5, bf16[512,2048]{1,0:T(8,128)(2,1)} %w_hbm.5, f32[1,2048]{1,0:T(1,128)} %bitcast.27, bf16[392,2048]{1,0:T(8,128)(2,1)} %u_hbm.5), custom_call_target="tpu_custom_call" | custom-call | flops 411041792 | bytes 1851392 | tf_op jit(solution)/shard_map/own_sent/pallas_call | solution.py:89
  7.3 0.0 collective-permute-done
  7.3 0.1 add_convert_fusion
  7.5 3.0 %collective-permute-start.2 = (bf16[512,512]{1,0:T(8,128)(2,1)S(1)}, bf16[512,512]{1,0:T(8,128)(2,1)S(1)}, u32[]{:S(2)}, u32[]{:S(2)}) collective-permute-start(bf16[512,512]{1,0:T(8,128)(2,1)S(1)} %add_convert_fusion), channel_id=1, source_target_pairs={{0,4},{1,5},{2,10},{3,11},{4,0},{5,1},{6,14},{7,15},{8,12},{9,13},... | collective-permute-start | bytes 1572872 | tf_op jit(solution)/shard_map/ppermute | solution.py:128
  10.5 2.5 %own_kept.1 = bf16[512,512]{1,0:T(8,128)(2,1)S(1)} custom-call(s32[1]{0:T(128)} %bitcast.5.parity_ref, s32[1]{0:T(128)} %bitcast.6.half_ref, bf16[392,512]{1,0:T(8,128)(2,1)} %x_hbm.5, bf16[512,2048]{1,0:T(8,128)(2,1)} %w_hbm.5, f32[1,2048]{1,0:T(1,128)} %bitcast.28, bf16[392,2048]{1,0:T(8,128)(2,1)} %u_hbm.5), custom_call_target="tpu_custom_call" | custom-call | flops 411041792 | bytes 1851392 | tf_op jit(solution)/shard_map/own_kept/pallas_call | solution.py:89
  13.0 0.0 copy-start
  13.0 0.0 copy-start.1
  13.1 0.0 collective-permute-done.1
  13.1 4.6 %collective-permute-done.2 = bf16[512,512]{1,0:T(8,128)(2,1)S(1)} collective-permute-done((bf16[512,512]{1,0:T(8,128)(2,1)S(1)}, bf16[512,512]{1,0:T(8,128)(2,1)S(1)}, u32[]{:S(2)}, u32[]{:S(2)}) %collective-permute-start.2) | collective-permute-done | bytes 524320 | tf_op jit(solution)/shard_map/ppermute | solution.py:128
  17.6 0.1 fusion
  17.7 2.1 %collective-permute-start.3 = (bf16[2,128,512]{2,1,0:T(8,128)(2,1)S(1)}, bf16[2,128,512]{2,1,0:T(8,128)(2,1)S(1)}, u32[]{:S(2)}, u32[]{:S(2)}) collective-permute-start(bf16[2,128,512]{2,1,0:T(8,128)(2,1)S(1)} %fusion), channel_id=1, source_target_pairs={{0,8},{1,9},{2,6},{3,7},{4,12},{5,13},{6,2},{7,3},{8,0},{9,1},{10,... | collective-permute-start | bytes 786440 | tf_op jit(solution)/shard_map/ppermute | solution.py:128
  19.9 4.4 %collective-permute-done.3 = bf16[2,128,512]{2,1,0:T(8,128)(2,1)S(1)} collective-permute-done((bf16[2,128,512]{2,1,0:T(8,128)(2,1)S(1)}, bf16[2,128,512]{2,1,0:T(8,128)(2,1)S(1)}, u32[]{:S(2)}, u32[]{:S(2)}) %collective-permute-start.3) | collective-permute-done | bytes 262176 | tf_op jit(solution)/shard_map/ppermute | solution.py:128
  24.2 0.1 bitcast_add_fusion
  24.4 3.1 %collective-permute-start.4 = (bf16[128,512]{1,0:T(8,128)(2,1)S(1)}, bf16[128,512]{1,0:T(8,128)(2,1)S(1)}, u32[]{:S(2)}, u32[]{:S(2)}) collective-permute-start(bf16[128,512]{1,0:T(8,128)(2,1)S(1)} %fusion.2), channel_id=1, source_target_pairs={{0,16},{1,17},{2,18},{3,19},{4,20},{5,21},{6,22},{7,23},{8,24},{9,... | collective-permute-start | bytes 393224 | tf_op jit(solution)/shard_map/ppermute | solution.py:128
  27.5 4.8 %collective-permute-done.4 = bf16[128,512]{1,0:T(8,128)(2,1)S(1)} collective-permute-done((bf16[128,512]{1,0:T(8,128)(2,1)S(1)}, bf16[128,512]{1,0:T(8,128)(2,1)S(1)}, u32[]{:S(2)}, u32[]{:S(2)}) %collective-permute-start.4) | collective-permute-done | bytes 131104 | tf_op jit(solution)/shard_map/ppermute | solution.py:128
  32.4 1.6 %collective-permute-start.5 = (bf16[128,512]{1,0:T(8,128)(2,1)S(1)}, bf16[128,512]{1,0:T(8,128)(2,1)S(1)}, u32[]{:S(2)}, u32[]{:S(2)}) collective-permute-start(bf16[128,512]{1,0:T(8,128)(2,1)S(1)} %fusion.1), channel_id=1, source_target_pairs={{0,1},{1,0},{2,3},{3,2},{4,5},{5,4},{6,7},{7,6},{8,9},{9,8},{10,11... | collective-permute-start | bytes 393224 | tf_op jit(solution)/shard_map/ppermute | solution.py:128
  34.0 3.4 %collective-permute-done.5 = bf16[128,512]{1,0:T(8,128)(2,1)S(1)} collective-permute-done((bf16[128,512]{1,0:T(8,128)(2,1)S(1)}, bf16[128,512]{1,0:T(8,128)(2,1)S(1)}, u32[]{:S(2)}, u32[]{:S(2)}) %collective-permute-start.5) | collective-permute-done | bytes 131104 | tf_op jit(solution)/shard_map/ppermute | solution.py:128
  37.4 0.0 copy-done
  37.4 0.0 copy-done.1
  37.4 0.9 %multiply_subtract_fusion = (f32[128,512]{1,0:T(8,128)}, f32[128,512]{1,0:T(8,128)}) fusion(f32[128,512]{1,0:T(8,128)S(1)} %copy-done, bf16[128,512]{1,0:T(8,128)(2,1)S(1)} %collective-permute-done.5, bf16[128,512]{1,0:T(8,128)(2,1)S(1)} %fusion.1, f32[128,512]{1,0:T(8,128)S(1)} %copy-done.1), kind=kLoop, calls=%fused_computation.6 | loop fusion | flops 589824 | bytes 1310720 | tf_op jit(solution)/shard_map/sub | solution.py:145
  (2 shorter events, 0.1 us)
Async XLA Ops:
  4.2 3.2 %collective-permute-start = (bf16[512,512]{1,0:T(8,128)(2,1)S(1)}, bf16[512,512]{1,0:T(8,128)(2,1)S(1)}, u32[]{:S(2)}, u32[]{:S(2)}) collective-permute-start(bf16[512,512]{1,0:T(8,128)(2,1)S(1)} %get-tuple-element.10), channel_id=1, source_target_pairs={{0,2},{1,3},{2,0},{3,1},{4,6},{5,7},{6,4},{7,5},{8,10},{9,11},{10,... | collective-permute-start | bytes 1572872 | tf_op jit(solution)/shard_map/ppermute | solution.py:128
  4.7 8.4 %collective-permute-start.1 = (bf16[512,512]{1,0:T(8,128)(2,1)S(1)}, bf16[512,512]{1,0:T(8,128)(2,1)S(1)}, u32[]{:S(2)}, u32[]{:S(2)}) collective-permute-start(bf16[512,512]{1,0:T(8,128)(2,1)S(1)} %get-tuple-element.13), channel_id=1, source_target_pairs={{0,2},{1,3},{2,0},{3,1},{4,6},{5,7},{6,4},{7,5},{8,10},{9,11},{10,... | collective-permute-start | bytes 1572872 | tf_op jit(solution)/shard_map/ppermute | solution.py:128
  7.5 10.2 %collective-permute-start.2 = (bf16[512,512]{1,0:T(8,128)(2,1)S(1)}, bf16[512,512]{1,0:T(8,128)(2,1)S(1)}, u32[]{:S(2)}, u32[]{:S(2)}) collective-permute-start(bf16[512,512]{1,0:T(8,128)(2,1)S(1)} %add_convert_fusion), channel_id=1, source_target_pairs={{0,4},{1,5},{2,10},{3,11},{4,0},{5,1},{6,14},{7,15},{8,12},{9,13},... | collective-permute-start | bytes 1572872 | tf_op jit(solution)/shard_map/ppermute | solution.py:128
  13.0 24.4 %copy-start = (f32[128,512]{1,0:T(8,128)S(1)}, f32[128,512]{1,0:T(8,128)}, u32[]{:S(2)}) copy-start(f32[128,512]{1,0:T(8,128)} %param.10) | copy-start | bytes 786436
  13.0 24.4 %copy-start.1 = (f32[128,512]{1,0:T(8,128)S(1)}, f32[128,512]{1,0:T(8,128)}, u32[]{:S(2)}) copy-start(f32[128,512]{1,0:T(8,128)} %param.11) | copy-start | bytes 786436
  17.7 6.5 %collective-permute-start.3 = (bf16[2,128,512]{2,1,0:T(8,128)(2,1)S(1)}, bf16[2,128,512]{2,1,0:T(8,128)(2,1)S(1)}, u32[]{:S(2)}, u32[]{:S(2)}) collective-permute-start(bf16[2,128,512]{2,1,0:T(8,128)(2,1)S(1)} %fusion), channel_id=1, source_target_pairs={{0,8},{1,9},{2,6},{3,7},{4,12},{5,13},{6,2},{7,3},{8,0},{9,1},{10,... | collective-permute-start | bytes 786440 | tf_op jit(solution)/shard_map/ppermute | solution.py:128
  24.4 7.9 %collective-permute-start.4 = (bf16[128,512]{1,0:T(8,128)(2,1)S(1)}, bf16[128,512]{1,0:T(8,128)(2,1)S(1)}, u32[]{:S(2)}, u32[]{:S(2)}) collective-permute-start(bf16[128,512]{1,0:T(8,128)(2,1)S(1)} %fusion.2), channel_id=1, source_target_pairs={{0,16},{1,17},{2,18},{3,19},{4,20},{5,21},{6,22},{7,23},{8,24},{9,... | collective-permute-start | bytes 393224 | tf_op jit(solution)/shard_map/ppermute | solution.py:128
  32.4 5.0 %collective-permute-start.5 = (bf16[128,512]{1,0:T(8,128)(2,1)S(1)}, bf16[128,512]{1,0:T(8,128)(2,1)S(1)}, u32[]{:S(2)}, u32[]{:S(2)}) collective-permute-start(bf16[128,512]{1,0:T(8,128)(2,1)S(1)} %fusion.1), channel_id=1, source_target_pairs={{0,1},{1,0},{2,3},{3,2},{4,5},{5,4},{6,7},{7,6},{8,9},{9,8},{10,11... | collective-permute-start | bytes 393224 | tf_op jit(solution)/shard_map/ppermute | solution.py:128

commit v4 on v3

--- a/solution.py
+++ b/solution.py
@@ -13,6 +13,7 @@
 DECAY = 5e-05
 
 TILE = 128
+STREAMS = 2
 NODE = "node"
 LOCAL = "local"
 F32 = jnp.float32
@@ -20,7 +21,7 @@
 
 
 def term_kernel(
-    piece, column, blocks, parity_ref, half_ref, x_hbm, w_hbm, gain_hbm, u_hbm, *refs
+    piece, streams, column, blocks, parity_ref, half_ref, x_hbm, w_hbm, gain_hbm, u_hbm, *refs
 ):
     *out_refs, x_ref, w_ref, gain_ref, u_ref, conv_ref, grad_ref, sem = refs
     parity, half = parity_ref[0], half_ref[0]
@@ -62,11 +63,14 @@
         term = lax.dot_general(
             grad_ref[b], x_ref[...], (((0,), (0,)), ((), ())), preferred_element_type=F32
         ).astype(BF16)
-        share = channels // len(out_refs)
-        count = min(block, share)
-        for row in range(0, block, count):
-            to, at = divmod(b * block + row, share)
-            out_refs[to][at : at + count] = term[row : row + count]
+        if streams == 1:
+            out_refs[0][b * block : (b + 1) * block] = term
+            return
+        part = piece // streams
+        for k in range(block // piece):
+            for t in range(streams):
+                row = k * piece + t * part
+                out_refs[b * streams + t][k * part : (k + 1) * part] = term[row : row + part]
 
     for i in range(blocks + 2):
         if 0 <= i - 2:
@@ -77,7 +81,7 @@
             differentiate(i - 1)
 
 
-def terms(name, outs, channels, blocks, piece, column, weight, parity, half, block_input, conv_weight, gain, out_cotangent):
+def terms(name, outs, channels, blocks, piece, streams, column, weight, parity, half, block_input, conv_weight, gain, out_cotangent):
     rows, width_in = block_input.shape
     block = channels // blocks
     hbm = pl.BlockSpec(memory_space=pltpu.HBM)
@@ -87,7 +91,7 @@
         return pltpu.with_memory_space_constraint(array, pltpu.HBM)
 
     return pl.pallas_call(
-        functools.partial(term_kernel, piece, column, blocks),
+        functools.partial(term_kernel, piece, streams, column, blocks),
         out_shape=(pltpu.VMEM((channels // outs, width_in), BF16),) * outs,
         in_specs=[smem, smem, hbm, hbm, hbm, hbm],
         out_specs=(pl.BlockSpec(memory_space=pltpu.VMEM),) * outs,
@@ -166,24 +170,30 @@
 
     def node_terms(name, count, parity, half, weight):
         halves = count // 4
-        return terms(name, halves, count * run, halves, run, column, weight, parity, half, *inputs)
-
-    far_sent, far_kept = node_terms("far_terms", 8, 1 - core, 1 - second, 1)
-    got_sent = flip(far_sent, 2, 2)
-    got = flip(far_kept, 2, 2).reshape(2, 2, run, width_in)
-    (own_sent,) = node_terms("own_sent", 4, core, 1 - first, 1)
-    sent, core, kept = lax.optimization_barrier((wide(own_sent, got_sent).astype(BF16), core, first))
-    arrived = flip(sent, 4, 8).reshape(2, 2, run, width_in)
-    own = node_terms("own_kept", 4, core, kept, 1)[0].reshape(2, 2, run, width_in)
-
-    def half_of(index):
-        return wide(pick(own, index), pick(got, index), pick(arrived, index))
-
-    again = flip(half_of(1 - second), 8, 4)
-    plane = wide(half_of(second), again)
-    plane, *state = lax.optimization_barrier((plane, *state))
-    both = wide(pick(plane, high), flip(pick(plane, 1 - high), 16, 16)).astype(BF16)
-    return wide(both, flip(both, 1, 1)), state
+        return terms(name, halves * STREAMS, count * run, halves, run, STREAMS, column, weight, parity, half, *inputs)
+
+    part = run // STREAMS
+
+    def laid(arrays):
+        return [array.reshape(2, 2, part, width_in) for array in arrays]
+
+    far = node_terms("far_terms", 8, 1 - core, 1 - second, 1)
+    got_sent = [flip(array, 2, 2) for array in far[:STREAMS]]
+    got = laid([flip(array, 2, 2) for array in far[STREAMS:]])
+    own_sent = node_terms("own_sent", 4, core, 1 - first, 1)
+    sent = [wide(*pair).astype(BF16) for pair in zip(own_sent, got_sent)]
+    sent, core, kept = lax.optimization_barrier((sent, core, first))
+    arrived = laid([flip(array, 4, 8) for array in sent])
+    own = laid(node_terms("own_kept", 4, core, kept, 1))
+
+    def half_of(t, index):
+        return wide(pick(own[t], index), pick(got[t], index), pick(arrived[t], index))
+
+    again = [flip(half_of(t, 1 - second), 8, 4) for t in range(STREAMS)]
+    planes = [wide(half_of(t, second), again[t]) for t in range(STREAMS)]
+    planes[0], *state = lax.optimization_barrier((planes[0], *state))
+    both = [wide(pick(plane, high), flip(pick(plane, 1 - high), 16, 16)).astype(BF16) for plane in planes]
+    return jnp.concatenate([wide(array, flip(array, 1, 1)) for array in both], axis=0), state
 
 
 def sum_lanes(run, block_input, conv_weight, gain, out_cotangent):
@@ -205,7 +215,7 @@
 
     def chip_terms(name, parity):
         half = width_out // 2
-        return terms(name, 1, half, 2, half, lambda k, parity, half: parity, 1, parity, parity, *inputs)[0]
+        return terms(name, 1, half, 2, half, 1, lambda k, parity, half: parity, 1, parity, parity, *inputs)[0]
 
     def laid(array):
         return array.reshape(depth, 2, lanes, run // lanes, width_in).transpose(2, 1, 0, 3, 4)

time: 38.5 us -> 35.4 us (0.919)
  waiting for transfers between devices: 17.2 us -> 3.61 us
  starting transfers between devices: 10.5 us -> 20.9 us
    ppermute x6 -> x12, waiting for transfers between devices: 17.2 us -> 3.61 us  [send(): return lax.ppermute(array.astype(BF16), (NODE, LOCAL), pairs)]
    ppermute x6 -> x12, starting transfers between devices: 10.5 us -> 20.9 us  [send(): return lax.ppermute(array.astype(BF16), (NODE, LOCAL), pairs)]
  transfers between devices with their start and end apart: 6 -> 12, of which waited for: 4 -> 5; matrix products, arithmetic and copies ran while one was open for 0% -> 1% of each run, Pallas kernels for 13% -> 14%
where the time goes in v4:
time: 35.4 us; the launch traced here: 35.2 us
  starting transfers between devices  20.9 us (59%)
  Pallas kernels  8.6 us (24%)
  waiting for transfers between devices  3.61 us (10%)
  other arithmetic  1.31 us (4%)
  between operations  0.79 us (2%)
    ppermute x12, starting transfers between devices, send(): return lax.ppermute(array.astype(BF16), (NODE, LOCAL), pairs)  20.9 us
    pallas_call x3, Pallas kernels, terms(): pl.pallas_call(functools.partial(term_kernel, piece, streams, column, blo...  8.6 us
    ppermute x12, waiting for transfers between devices, send(): return lax.ppermute(array.astype(BF16), (NODE, LOCAL), pairs)  3.61 us
    sub x1, other arithmetic, local_fn(): new_weight = master_weight - RATE * new_velocity  0.87 us
  transfers between devices with their start and end apart: 12, of which 5 were waited for; matrix products, arithmetic and copies ran while one was open for 1% of the time, Pallas kernels for 14%

profile of v4, /device:TPU:0, one launch (start us, length us, event | category | flops | bytes accessed | tf_op | source)
XLA Modules:
  0.0 35.2 jit_solution(18231839346840817635)
XLA Ops:
  0.6 3.5 %far_terms.1 = (bf16[256,512]{1,0:T(8,128)(2,1)S(1)}, bf16[256,512]{1,0:T(8,128)(2,1)S(1)}, bf16[256,512]{1,0:T(8,128)(2,1)S(1)}, bf16[256,512]{1,0:T(8,128)(2,1)S(1)}) custom-call(s32[1]{0:T(128)} %bitcast.3.parity_ref, s32[1]{0:T(128)} %bitcast.4.half_ref, bf16[392,512]{1,0:T(8,128)(2,1)} %x_hbm.5, bf16[512,2048]{1,0:T(8,128)(2,1)} %w_hbm.5, ...), custom_call_target="tpu_custom_call" | custom-call | flops 822083584 | bytes 3301376 | tf_op jit(solution)/shard_map/far_terms/pallas_call | solution.py:93
  4.2 0.5 %collective-permute-start.1 = (bf16[256,512]{1,0:T(8,128)(2,1)S(1)}, bf16[256,512]{1,0:T(8,128)(2,1)S(1)}, u32[]{:S(2)}, u32[]{:S(2)}) collective-permute-start(bf16[256,512]{1,0:T(8,128)(2,1)S(1)} %get-tuple-element.20), channel_id=1, source_target_pairs={{0,2},{1,3},{2,0},{3,1},{4,6},{5,7},{6,4},{7,5},{8,10},{9,11},{10,... | collective-permute-start | bytes 786440 | tf_op jit(solution)/shard_map/ppermute | solution.py:132
  4.7 0.1 collective-permute-start
  4.8 0.4 %collective-permute-start.2 = (bf16[256,512]{1,0:T(8,128)(2,1)S(1)}, bf16[256,512]{1,0:T(8,128)(2,1)S(1)}, u32[]{:S(2)}, u32[]{:S(2)}) collective-permute-start(bf16[256,512]{1,0:T(8,128)(2,1)S(1)} %get-tuple-element.24), channel_id=1, source_target_pairs={{0,2},{1,3},{2,0},{3,1},{4,6},{5,7},{6,4},{7,5},{8,10},{9,11},{10,... | collective-permute-start | bytes 786440 | tf_op jit(solution)/shard_map/ppermute | solution.py:132
  5.2 2.6 %own_sent.1 = (bf16[256,512]{1,0:T(8,128)(2,1)S(1)}, bf16[256,512]{1,0:T(8,128)(2,1)S(1)}) custom-call(s32[1]{0:T(128)} %bitcast.parity_ref, s32[1]{0:T(128)} %bitcast.1.half_ref, bf16[392,512]{1,0:T(8,128)(2,1)} %x_hbm.5, bf16[512,2048]{1,0:T(8,128)(2,1)} %w_hbm.5, f32[1,2048]{1,0:T(1,128)} %bitcast.46, bf16[392,2048]{1,0:T(8,128)(2,1)} %u_hbm.5), custom_call_target="tpu_custom_call" | custom-call | flops 411041792 | bytes 1851392 | tf_op jit(solution)/shard_map/own_sent/pallas_call | solution.py:93
  7.7 0.0 collective-permute-done.1
  7.8 0.1 add_convert_fusion
  7.8 0.0 collective-permute-done
  7.8 0.1 add_convert_fusion.1
  7.9 2.7 %collective-permute-start.3 = (bf16[256,512]{1,0:T(8,128)(2,1)S(1)}, bf16[256,512]{1,0:T(8,128)(2,1)S(1)}, u32[]{:S(2)}, u32[]{:S(2)}) collective-permute-start(bf16[256,512]{1,0:T(8,128)(2,1)S(1)} %add_convert_fusion.1), channel_id=1, source_target_pairs={{0,4},{1,5},{2,10},{3,11},{4,0},{5,1},{6,14},{7,15},{8,12},{9,13},... | collective-permute-start | bytes 786440 | tf_op jit(solution)/shard_map/ppermute | solution.py:132
  10.6 0.2 collective-permute-start.7
  10.8 1.5 %collective-permute-start.8 = (bf16[256,512]{1,0:T(8,128)(2,1)S(1)}, bf16[256,512]{1,0:T(8,128)(2,1)S(1)}, u32[]{:S(2)}, u32[]{:S(2)}) collective-permute-start(bf16[256,512]{1,0:T(8,128)(2,1)S(1)} %add_convert_fusion), channel_id=1, source_target_pairs={{0,4},{1,5},{2,10},{3,11},{4,0},{5,1},{6,14},{7,15},{8,12},{9,13},... | collective-permute-start | bytes 786440 | tf_op jit(solution)/shard_map/ppermute | solution.py:132
  12.3 2.5 %own_kept.1 = (bf16[256,512]{1,0:T(8,128)(2,1)S(1)}, bf16[256,512]{1,0:T(8,128)(2,1)S(1)}) custom-call(s32[1]{0:T(128)} %bitcast.5.parity_ref, s32[1]{0:T(128)} %bitcast.6.half_ref, bf16[392,512]{1,0:T(8,128)(2,1)} %x_hbm.5, bf16[512,2048]{1,0:T(8,128)(2,1)} %w_hbm.5, f32[1,2048]{1,0:T(1,128)} %bitcast.47, bf16[392,2048]{1,0:T(8,128)(2,1)} %u_hbm.5), custom_call_target="tpu_custom_call" | custom-call | flops 411041792 | bytes 1851392 | tf_op jit(solution)/shard_map/own_kept/pallas_call | solution.py:93
  14.9 0.0 copy-start
  14.9 0.0 copy-start.1
  14.9 0.0 collective-permute-done.2
  14.9 0.0 collective-permute-done.3
  14.9 0.1 fusion.1
  15.0 2.2 %collective-permute-start.4 = (bf16[2,64,512]{2,1,0:T(8,128)(2,1)S(1)}, bf16[2,64,512]{2,1,0:T(8,128)(2,1)S(1)}, u32[]{:S(2)}, u32[]{:S(2)}) collective-permute-start(bf16[2,64,512]{2,1,0:T(8,128)(2,1)S(1)} %fusion.1), channel_id=1, source_target_pairs={{0,8},{1,9},{2,6},{3,7},{4,12},{5,13},{6,2},{7,3},{8,0},{9,1},{10,... | collective-permute-start | bytes 393224 | tf_op jit(solution)/shard_map/ppermute | solution.py:132
  17.1 0.0 collective-permute-done.7
  17.1 0.6 %collective-permute-done.8 = bf16[256,512]{1,0:T(8,128)(2,1)S(1)} collective-permute-done((bf16[256,512]{1,0:T(8,128)(2,1)S(1)}, bf16[256,512]{1,0:T(8,128)(2,1)S(1)}, u32[]{:S(2)}, u32[]{:S(2)}) %collective-permute-start.8) | collective-permute-done | bytes 262176 | tf_op jit(solution)/shard_map/ppermute | solution.py:132
  17.7 0.1 fusion.2
  17.8 2.6 %collective-permute-start.9 = (bf16[2,64,512]{2,1,0:T(8,128)(2,1)S(1)}, bf16[2,64,512]{2,1,0:T(8,128)(2,1)S(1)}, u32[]{:S(2)}, u32[]{:S(2)}) collective-permute-start(bf16[2,64,512]{2,1,0:T(8,128)(2,1)S(1)} %fusion.2), channel_id=1, source_target_pairs={{0,8},{1,9},{2,6},{3,7},{4,12},{5,13},{6,2},{7,3},{8,0},{9,1},{10,... | collective-permute-start | bytes 393224 | tf_op jit(solution)/shard_map/ppermute | solution.py:132
  20.4 0.0 collective-permute-done.4
  20.4 0.1 bitcast_add_fusion.1
  20.5 2.8 %collective-permute-start.5 = (bf16[64,512]{1,0:T(8,128)(2,1)S(1)}, bf16[64,512]{1,0:T(8,128)(2,1)S(1)}, u32[]{:S(2)}, u32[]{:S(2)}) collective-permute-start(bf16[64,512]{1,0:T(8,128)(2,1)S(1)} %fusion.5), channel_id=1, source_target_pairs={{0,16},{1,17},{2,18},{3,19},{4,20},{5,21},{6,22},{7,23},{8,24},{9,... | collective-permute-start | bytes 196616 | tf_op jit(solution)/shard_map/ppermute | solution.py:132
  23.3 0.1 collective-permute-done.9
  23.3 0.1 bitcast_add_fusion
  23.4 3.8 %collective-permute-start.10 = (bf16[64,512]{1,0:T(8,128)(2,1)S(1)}, bf16[64,512]{1,0:T(8,128)(2,1)S(1)}, u32[]{:S(2)}, u32[]{:S(2)}) collective-permute-start(bf16[64,512]{1,0:T(8,128)(2,1)S(1)} %fusion.6), channel_id=1, source_target_pairs={{0,16},{1,17},{2,18},{3,19},{4,20},{5,21},{6,22},{7,23},{8,24},{9,... | collective-permute-start | bytes 196616 | tf_op jit(solution)/shard_map/ppermute | solution.py:132
  27.2 0.0 collective-permute-done.5
  27.3 1.5 %collective-permute-start.6 = (bf16[64,512]{1,0:T(8,128)(2,1)S(1)}, bf16[64,512]{1,0:T(8,128)(2,1)S(1)}, u32[]{:S(2)}, u32[]{:S(2)}) collective-permute-start(bf16[64,512]{1,0:T(8,128)(2,1)S(1)} %fusion.4), channel_id=1, source_target_pairs={{0,1},{1,0},{2,3},{3,2},{4,5},{5,4},{6,7},{7,6},{8,9},{9,8},{10,11... | collective-permute-start | bytes 196616 | tf_op jit(solution)/shard_map/ppermute | solution.py:132
  28.8 0.7 %collective-permute-done.10 = bf16[64,512]{1,0:T(8,128)(2,1)S(1)} collective-permute-done((bf16[64,512]{1,0:T(8,128)(2,1)S(1)}, bf16[64,512]{1,0:T(8,128)(2,1)S(1)}, u32[]{:S(2)}, u32[]{:S(2)}) %collective-permute-start.10) | collective-permute-done | bytes 65568 | tf_op jit(solution)/shard_map/ppermute | solution.py:132
  29.5 2.6 %collective-permute-start.11 = (bf16[64,512]{1,0:T(8,128)(2,1)S(1)}, bf16[64,512]{1,0:T(8,128)(2,1)S(1)}, u32[]{:S(2)}, u32[]{:S(2)}) collective-permute-start(bf16[64,512]{1,0:T(8,128)(2,1)S(1)} %fusion.3), channel_id=1, source_target_pairs={{0,1},{1,0},{2,3},{3,2},{4,5},{5,4},{6,7},{7,6},{8,9},{9,8},{10,11... | collective-permute-start | bytes 196616 | tf_op jit(solution)/shard_map/ppermute | solution.py:132
  32.1 0.1 collective-permute-done.6
  32.2 2.2 %collective-permute-done.11 = bf16[64,512]{1,0:T(8,128)(2,1)S(1)} collective-permute-done((bf16[64,512]{1,0:T(8,128)(2,1)S(1)}, bf16[64,512]{1,0:T(8,128)(2,1)S(1)}, u32[]{:S(2)}, u32[]{:S(2)}) %collective-permute-start.11) | collective-permute-done | bytes 65568 | tf_op jit(solution)/shard_map/ppermute | solution.py:132
  34.3 0.0 copy-done
  34.3 0.0 copy-done.1
  34.4 0.9 %multiply_subtract_fusion = (f32[128,512]{1,0:T(8,128)}, f32[128,512]{1,0:T(8,128)}) fusion(f32[128,512]{1,0:T(8,128)S(1)} %copy-done, f32[64,512]{1,0:T(8,128)S(1)} %convert_add_fusion, f32[64,512]{1,0:T(8,128)S(1)} %convert_add_fusion.1, f32[128,512]{1,0:T(8,128)S(1)} %copy-done.1), kind=kLoop, calls=%fused_computation.6 | loop fusion | flops 458752 | bytes 1310720 | tf_op jit(solution)/shard_map/sub | solution.py:149
  (6 shorter events, 0.1 us)
Async XLA Ops:
  4.2 3.6 %collective-permute-start.1 = (bf16[256,512]{1,0:T(8,128)(2,1)S(1)}, bf16[256,512]{1,0:T(8,128)(2,1)S(1)}, u32[]{:S(2)}, u32[]{:S(2)}) collective-permute-start(bf16[256,512]{1,0:T(8,128)(2,1)S(1)} %get-tuple-element.20), channel_id=1, source_target_pairs={{0,2},{1,3},{2,0},{3,1},{4,6},{5,7},{6,4},{7,5},{8,10},{9,11},{10,... | collective-permute-start | bytes 786440 | tf_op jit(solution)/shard_map/ppermute | solution.py:132
  4.7 3.2 %collective-permute-start = (bf16[256,512]{1,0:T(8,128)(2,1)S(1)}, bf16[256,512]{1,0:T(8,128)(2,1)S(1)}, u32[]{:S(2)}, u32[]{:S(2)}) collective-permute-start(bf16[256,512]{1,0:T(8,128)(2,1)S(1)} %get-tuple-element.18), channel_id=1, source_target_pairs={{0,2},{1,3},{2,0},{3,1},{4,6},{5,7},{6,4},{7,5},{8,10},{9,11},{10,... | collective-permute-start | bytes 786440 | tf_op jit(solution)/shard_map/ppermute | solution.py:132
  4.8 10.1 %collective-permute-start.2 = (bf16[256,512]{1,0:T(8,128)(2,1)S(1)}, bf16[256,512]{1,0:T(8,128)(2,1)S(1)}, u32[]{:S(2)}, u32[]{:S(2)}) collective-permute-start(bf16[256,512]{1,0:T(8,128)(2,1)S(1)} %get-tuple-element.24), channel_id=1, source_target_pairs={{0,2},{1,3},{2,0},{3,1},{4,6},{5,7},{6,4},{7,5},{8,10},{9,11},{10,... | collective-permute-start | bytes 786440 | tf_op jit(solution)/shard_map/ppermute | solution.py:132
  7.9 7.0 %collective-permute-start.3 = (bf16[256,512]{1,0:T(8,128)(2,1)S(1)}, bf16[256,512]{1,0:T(8,128)(2,1)S(1)}, u32[]{:S(2)}, u32[]{:S(2)}) collective-permute-start(bf16[256,512]{1,0:T(8,128)(2,1)S(1)} %add_convert_fusion.1), channel_id=1, source_target_pairs={{0,4},{1,5},{2,10},{3,11},{4,0},{5,1},{6,14},{7,15},{8,12},{9,13},... | collective-permute-start | bytes 786440 | tf_op jit(solution)/shard_map/ppermute | solution.py:132
  10.6 6.6 %collective-permute-start.7 = (bf16[256,512]{1,0:T(8,128)(2,1)S(1)}, bf16[256,512]{1,0:T(8,128)(2,1)S(1)}, u32[]{:S(2)}, u32[]{:S(2)}) collective-permute-start(bf16[256,512]{1,0:T(8,128)(2,1)S(1)} %get-tuple-element.29), channel_id=1, source_target_pairs={{0,2},{1,3},{2,0},{3,1},{4,6},{5,7},{6,4},{7,5},{8,10},{9,11},{10,... | collective-permute-start | bytes 786440 | tf_op jit(solution)/shard_map/ppermute | solution.py:132
  10.8 6.9 %collective-permute-start.8 = (bf16[256,512]{1,0:T(8,128)(2,1)S(1)}, bf16[256,512]{1,0:T(8,128)(2,1)S(1)}, u32[]{:S(2)}, u32[]{:S(2)}) collective-permute-start(bf16[256,512]{1,0:T(8,128)(2,1)S(1)} %add_convert_fusion), channel_id=1, source_target_pairs={{0,4},{1,5},{2,10},{3,11},{4,0},{5,1},{6,14},{7,15},{8,12},{9,13},... | collective-permute-start | bytes 786440 | tf_op jit(solution)/shard_map/ppermute | solution.py:132
  14.9 19.5 %copy-start = (f32[128,512]{1,0:T(8,128)S(1)}, f32[128,512]{1,0:T(8,128)}, u32[]{:S(2)}) copy-start(f32[128,512]{1,0:T(8,128)} %param.10) | copy-start | bytes 786436
  14.9 19.5 %copy-start.1 = (f32[128,512]{1,0:T(8,128)S(1)}, f32[128,512]{1,0:T(8,128)}, u32[]{:S(2)}) copy-start(f32[128,512]{1,0:T(8,128)} %param.11) | copy-start | bytes 786436
  15.0 5.4 %collective-permute-start.4 = (bf16[2,64,512]{2,1,0:T(8,128)(2,1)S(1)}, bf16[2,64,512]{2,1,0:T(8,128)(2,1)S(1)}, u32[]{:S(2)}, u32[]{:S(2)}) collective-permute-start(bf16[2,64,512]{2,1,0:T(8,128)(2,1)S(1)} %fusion.1), channel_id=1, source_target_pairs={{0,8},{1,9},{2,6},{3,7},{4,12},{5,13},{6,2},{7,3},{8,0},{9,1},{10,... | collective-permute-start | bytes 393224 | tf_op jit(solution)/shard_map/ppermute | solution.py:132
  17.8 5.6 %collective-permute-start.9 = (bf16[2,64,512]{2,1,0:T(8,128)(2,1)S(1)}, bf16[2,64,512]{2,1,0:T(8,128)(2,1)S(1)}, u32[]{:S(2)}, u32[]{:S(2)}) collective-permute-start(bf16[2,64,512]{2,1,0:T(8,128)(2,1)S(1)} %fusion.2), channel_id=1, source_target_pairs={{0,8},{1,9},{2,6},{3,7},{4,12},{5,13},{6,2},{7,3},{8,0},{9,1},{10,... | collective-permute-start | bytes 393224 | tf_op jit(solution)/shard_map/ppermute | solution.py:132
  20.5 6.7 %collective-permute-start.5 = (bf16[64,512]{1,0:T(8,128)(2,1)S(1)}, bf16[64,512]{1,0:T(8,128)(2,1)S(1)}, u32[]{:S(2)}, u32[]{:S(2)}) collective-permute-start(bf16[64,512]{1,0:T(8,128)(2,1)S(1)} %fusion.5), channel_id=1, source_target_pairs={{0,16},{1,17},{2,18},{3,19},{4,20},{5,21},{6,22},{7,23},{8,24},{9,... | collective-permute-start | bytes 196616 | tf_op jit(solution)/shard_map/ppermute | solution.py:132
  23.4 6.0 %collective-permute-start.10 = (bf16[64,512]{1,0:T(8,128)(2,1)S(1)}, bf16[64,512]{1,0:T(8,128)(2,1)S(1)}, u32[]{:S(2)}, u32[]{:S(2)}) collective-permute-start(bf16[64,512]{1,0:T(8,128)(2,1)S(1)} %fusion.6), channel_id=1, source_target_pairs={{0,16},{1,17},{2,18},{3,19},{4,20},{5,21},{6,22},{7,23},{8,24},{9,... | collective-permute-start | bytes 196616 | tf_op jit(solution)/shard_map/ppermute | solution.py:132
  27.3 4.9 %collective-permute-start.6 = (bf16[64,512]{1,0:T(8,128)(2,1)S(1)}, bf16[64,512]{1,0:T(8,128)(2,1)S(1)}, u32[]{:S(2)}, u32[]{:S(2)}) collective-permute-start(bf16[64,512]{1,0:T(8,128)(2,1)S(1)} %fusion.4), channel_id=1, source_target_pairs={{0,1},{1,0},{2,3},{3,2},{4,5},{5,4},{6,7},{7,6},{8,9},{9,8},{10,11... | collective-permute-start | bytes 196616 | tf_op jit(solution)/shard_map/ppermute | solution.py:132
  29.5 4.8 %collective-permute-start.11 = (bf16[64,512]{1,0:T(8,128)(2,1)S(1)}, bf16[64,512]{1,0:T(8,128)(2,1)S(1)}, u32[]{:S(2)}, u32[]{:S(2)}) collective-permute-start(bf16[64,512]{1,0:T(8,128)(2,1)S(1)} %fusion.3), channel_id=1, source_target_pairs={{0,1},{1,0},{2,3},{3,2},{4,5},{5,4},{6,7},{7,6},{8,9},{9,8},{10,11... | collective-permute-start | bytes 196616 | tf_op jit(solution)/shard_map/ppermute | solution.py:132

commit v5 on v4

--- a/solution.py
+++ b/solution.py
@@ -13,32 +13,16 @@
 DECAY = 5e-05
 
 TILE = 128
-STREAMS = 2
+STREAMS = (4, 4)
 NODE = "node"
 LOCAL = "local"
 F32 = jnp.float32
 BF16 = jnp.bfloat16
 
 
-def term_kernel(
-    piece, streams, column, blocks, parity_ref, half_ref, x_hbm, w_hbm, gain_hbm, u_hbm, *refs
-):
-    *out_refs, x_ref, w_ref, gain_ref, u_ref, conv_ref, grad_ref, sem = refs
-    parity, half = parity_ref[0], half_ref[0]
-    rows = x_hbm.shape[0]
-    channels = w_ref.shape[1]
+def term_rows(piece, parts, blocks, out_refs, x_ref, w_ref, gain_ref, u_ref, conv_ref, grad_ref):
+    rows, channels = u_ref.shape
     block = channels // blocks
-
-    copies = [pltpu.make_async_copy(x_hbm, x_ref, sem.at[0])]
-    for k in range(channels // piece):
-        source = pl.ds(pl.multiple_of(column(k, parity, half) * piece, piece), piece)
-        target = pl.ds(k * piece, piece)
-        for a, b in ((w_hbm, w_ref), (u_hbm, u_ref), (gain_hbm, gain_ref)):
-            copies.append(pltpu.make_async_copy(a.at[:, source], b.at[:, target], sem.at[len(copies)]))
-    for copy in copies:
-        copy.start()
-    for copy in copies:
-        copy.wait()
 
     def columns(b):
         return slice(b * block, (b + 1) * block)
@@ -63,14 +47,14 @@
         term = lax.dot_general(
             grad_ref[b], x_ref[...], (((0,), (0,)), ((), ())), preferred_element_type=F32
         ).astype(BF16)
-        if streams == 1:
+        if parts is None:
             out_refs[0][b * block : (b + 1) * block] = term
             return
-        part = piece // streams
         for k in range(block // piece):
-            for t in range(streams):
-                row = k * piece + t * part
-                out_refs[b * streams + t][k * part : (k + 1) * part] = term[row : row + part]
+            row = k * piece
+            for t, part in enumerate(parts):
+                out_refs[b * len(parts) + t][k * part : (k + 1) * part] = term[row : row + part]
+                row += part
 
     for i in range(blocks + 2):
         if 0 <= i - 2:
@@ -81,44 +65,83 @@
             differentiate(i - 1)
 
 
-def terms(name, outs, channels, blocks, piece, streams, column, weight, parity, half, block_input, conv_weight, gain, out_cotangent):
-    rows, width_in = block_input.shape
+def reading_kernel(piece, column, next_column, parts, blocks, outs, parity_ref, half_ref, next_ref, *refs):
+    hbm, out_refs, refs = refs[:4], refs[4 : 4 + outs], refs[4 + outs :]
+    held = None
+    if next_column is not None:
+        x_ref, *held = refs[:4]
+        *own, conv_ref, grad_ref, sem = refs[4:]
+    else:
+        x_ref, *own, conv_ref, grad_ref, sem = refs
+    copies = [pltpu.make_async_copy(hbm[0], x_ref, sem.at[0])]
+    used = 1
+
+    def reads(to, column, *where):
+        nonlocal used
+        made = []
+        for k in range(to[0].shape[1] // piece):
+            source = pl.ds(pl.multiple_of(column(k, *where) * piece, piece), piece)
+            for a, b in zip(hbm[1:], to):
+                copy = pltpu.make_async_copy(a.at[:, source], b.at[:, pl.ds(k * piece, piece)], sem.at[used])
+                made.append(copy)
+                used += 1
+        return made
+
+    copies += reads(own, column, parity_ref[0], half_ref[0])
+    later = [] if held is None else reads(held, next_column, 1 - parity_ref[0], next_ref[0])
+    for copy in copies + later:
+        copy.start()
+    for copy in copies:
+        copy.wait()
+    term_rows(piece, parts, blocks, out_refs, x_ref, *own, conv_ref, grad_ref)
+    for copy in later:
+        copy.wait()
+
+
+def holding_kernel(piece, parts, blocks, outs, *refs):
+    term_rows(piece, parts, blocks, refs[4 : 4 + outs], *refs[:4], *refs[4 + outs :])
+
+
+def term_call(name, inputs, channels, blocks, piece, parts, column=None, where=(), next_column=None, next_channels=0):
+    rows, width_in = inputs[0].shape
     block = channels // blocks
+    sizes = [channels] if parts is None else [part * (block // piece) for part in parts] * blocks
     hbm = pl.BlockSpec(memory_space=pltpu.HBM)
+    vmem = pl.BlockSpec(memory_space=pltpu.VMEM)
     smem = pl.BlockSpec(memory_space=pltpu.SMEM)
-
-    def in_hbm(array):
-        return pltpu.with_memory_space_constraint(array, pltpu.HBM)
-
+    x = pltpu.VMEM((rows, width_in), BF16)
+    outs = [pltpu.VMEM((size, width_in), BF16) for size in sizes]
+
+    def read(count):
+        return [pltpu.VMEM((width_in, count), BF16), pltpu.VMEM((1, count), F32), pltpu.VMEM((rows, count), BF16)]
+
+    scratch = [pltpu.VMEM((blocks, rows, block), F32), pltpu.VMEM((blocks, rows, block), BF16)]
+    if column is None:
+        kernel = functools.partial(holding_kernel, piece, parts, blocks, len(outs))
+        in_specs = [vmem] * 4
+    else:
+        kernel = functools.partial(reading_kernel, piece, column, next_column, parts, blocks, len(outs))
+        in_specs = [smem] * 3 + [hbm] * 4
+        inputs = [i.reshape(1) for i in where] + [pltpu.with_memory_space_constraint(a, pltpu.HBM) for a in inputs]
+        scratch = read(channels) + scratch + [pltpu.SemaphoreType.DMA((1 + 3 * ((channels + next_channels) // piece),))]
+        if next_column is None:
+            scratch = [x] + scratch
+        else:
+            outs += [x] + read(next_channels)
     return pl.pallas_call(
-        functools.partial(term_kernel, piece, streams, column, blocks),
-        out_shape=(pltpu.VMEM((channels // outs, width_in), BF16),) * outs,
-        in_specs=[smem, smem, hbm, hbm, hbm, hbm],
-        out_specs=(pl.BlockSpec(memory_space=pltpu.VMEM),) * outs,
-        scratch_shapes=[
-            pltpu.VMEM((rows, width_in), BF16),
-            pltpu.VMEM((width_in, channels), BF16),
-            pltpu.VMEM((1, channels), F32),
-            pltpu.VMEM((rows, channels), BF16),
-            pltpu.VMEM((blocks, rows, block), F32),
-            pltpu.VMEM((blocks, rows, block), BF16),
-            pltpu.SemaphoreType.DMA((1 + 3 * (channels // piece),)),
-        ],
+        kernel,
+        out_shape=tuple(outs),
+        in_specs=in_specs,
+        out_specs=(vmem,) * len(outs),
+        scratch_shapes=scratch,
         cost_estimate=pl.CostEstimate(
-            flops=max(1, int(weight * 4 * rows * channels * width_in)),
-            bytes_accessed=max(1, int(weight * 2 * (rows * channels + channels * width_in * 2 + rows * width_in))),
-            transcendentals=max(1, int(weight * channels)),
+            flops=4 * rows * channels * width_in,
+            bytes_accessed=2 * (rows * channels + channels * width_in * 2 + rows * width_in),
+            transcendentals=channels,
         ),
         compiler_params=pltpu.CompilerParams(vmem_limit_bytes=16 * 2**20),
         name=name,
-    )(
-        parity.reshape(1),
-        half.reshape(1),
-        in_hbm(block_input),
-        in_hbm(conv_weight),
-        in_hbm(gain),
-        in_hbm(out_cotangent),
-    )
+    )(*inputs)
 
 
 def pick(array, *index):
@@ -155,42 +178,42 @@
     inputs = (block_input, conv_weight, gain, out_cotangent)
     node = lax.axis_index(NODE)
     core, side, low, high = node & 1, (node >> 1) & 1, (node >> 2) & 1, node >> 3
-    is_one = core == 1
+    is_one = core == 0
     first = jnp.where(is_one, low, side)
     second = jnp.where(is_one, side, low)
 
     def column(k, parity, half):
         half, k = (half, k) if k < 4 else (1 - half, k - 4)
-        zero = (((k % 2) * 2 + k // 2) * 2 + half) * 2
-        one = (((k % 2) * 2 + half) * 2 + k // 2) * 2 + 1
-        return jnp.where(parity == 1, one, zero)
+        zero = (((k % 2) * 2 + k // 2) * 2 + half) * 2 + 1
+        one = (((k % 2) * 2 + half) * 2 + k // 2) * 2
+        return jnp.where(parity == 0, one, zero)
 
     def flip(array, zero, one):
-        return send(array, [(i, i ^ (one if i & 2 else zero)) for i in range(32)])
-
-    def node_terms(name, count, parity, half, weight):
-        halves = count // 4
-        return terms(name, halves * STREAMS, count * run, halves, run, STREAMS, column, weight, parity, half, *inputs)
-
-    part = run // STREAMS
+        return send(array, [(i, i ^ (zero if i & 2 else one)) for i in range(32)])
+
+    parts = [run * share // sum(STREAMS) for share in STREAMS]
+    count = len(parts)
 
     def laid(arrays):
-        return [array.reshape(2, 2, part, width_in) for array in arrays]
-
-    far = node_terms("far_terms", 8, 1 - core, 1 - second, 1)
-    got_sent = [flip(array, 2, 2) for array in far[:STREAMS]]
-    got = laid([flip(array, 2, 2) for array in far[STREAMS:]])
-    own_sent = node_terms("own_sent", 4, core, 1 - first, 1)
+        return [array.reshape(2, 2, part, width_in) for array, part in zip(arrays, parts)]
+
+    far = term_call(
+        "far_terms", inputs, 8 * run, 2, run, parts, column, (1 - core, 1 - second, 1 - first), column, 4 * run
+    )
+    far, held = far[: 2 * count], far[2 * count :]
+    got_sent = [flip(array, 2, 2) for array in far[:count]]
+    got = laid([flip(array, 2, 2) for array in far[count:]])
+    own_sent = term_call("own_sent", held, 4 * run, 1, run, parts)
     sent = [wide(*pair).astype(BF16) for pair in zip(own_sent, got_sent)]
     sent, core, kept = lax.optimization_barrier((sent, core, first))
     arrived = laid([flip(array, 4, 8) for array in sent])
-    own = laid(node_terms("own_kept", 4, core, kept, 1))
+    own = laid(term_call("own_kept", inputs, 4 * run, 1, run, parts, column, (core, kept, kept)))
 
     def half_of(t, index):
         return wide(pick(own[t], index), pick(got[t], index), pick(arrived[t], index))
 
-    again = [flip(half_of(t, 1 - second), 8, 4) for t in range(STREAMS)]
-    planes = [wide(half_of(t, second), again[t]) for t in range(STREAMS)]
+    again = [flip(half_of(t, 1 - second), 8, 4) for t in range(count)]
+    planes = [wide(half_of(t, second), again[t]) for t in range(count)]
     planes[0], *state = lax.optimization_barrier((planes[0], *state))
     both = [wide(pick(plane, high), flip(pick(plane, 1 - high), 16, 16)).astype(BF16) for plane in planes]
     return jnp.concatenate([wide(array, flip(array, 1, 1)) for array in both], axis=0), state
@@ -215,7 +238,7 @@
 
     def chip_terms(name, parity):
         half = width_out // 2
-        return terms(name, 1, half, 2, half, 1, lambda k, parity, half: parity, 1, parity, parity, *inputs)[0]
+        return term_call(name, inputs, half, 2, half, None, lambda k, parity, half: parity, (parity,) * 3)[0]
 
     def laid(array):
         return array.reshape(depth, 2, lanes, run // lanes, width_in).transpose(2, 1, 0, 3, 4)

time: 35.4 us -> 33 us (0.932)
  starting transfers between devices: 20.9 us -> 19.1 us
  Pallas kernels: 8.6 us -> 7.27 us
  waiting for transfers between devices: 3.61 us -> 4.28 us
    ppermute x12, starting transfers between devices: 20.9 us -> 19.1 us  [send(): return lax.ppermute(array.astype(BF16), (NODE, LOCAL), pairs)]
    pallas_call x3, Pallas kernels: 8.6 us -> 7.27 us  [term_call(): pl.pallas_call(kernel, out_shape=tuple(outs), in_specs=in_specs, out_spec...]
    ppermute x12, waiting for transfers between devices: 3.61 us -> 4.28 us  [send(): return lax.ppermute(array.astype(BF16), (NODE, LOCAL), pairs)]
  transfers between devices with their start and end apart: 12 -> 12, of which waited for: 5 -> 6; matrix products, arithmetic and copies ran while one was open for 1% -> 1% of each run, Pallas kernels for 14% -> 11%
where the time goes in v5:
time: 33 us; the launch traced here: 32.8 us
  starting transfers between devices  19.1 us (58%)
  Pallas kernels  7.27 us (22%)
  waiting for transfers between devices  4.28 us (13%)
  other arithmetic  1.3 us (4%)
  between operations  0.79 us (2%)
    ppermute x12, starting transfers between devices, send(): return lax.ppermute(array.astype(BF16), (NODE, LOCAL), pairs)  19.1 us
    pallas_call x3, Pallas kernels, term_call(): pl.pallas_call(kernel, out_shape=tuple(outs), in_specs=in_specs, out_spec...  7.27 us
    ppermute x12, waiting for transfers between devices, send(): return lax.ppermute(array.astype(BF16), (NODE, LOCAL), pairs)  4.28 us
    sub x1, other arithmetic, local_fn(): new_weight = master_weight - RATE * new_velocity  0.87 us
  transfers between devices with their start and end apart: 12, of which 6 were waited for; matrix products, arithmetic and copies ran while one was open for 1% of the time, Pallas kernels for 11%

profile of v5, /device:TPU:0, one launch (start us, length us, event | category | flops | bytes accessed | tf_op | source)
XLA Modules:
  0.0 32.8 jit_solution(9790166229991666488)
XLA Ops:
  0.6 3.6 %far_terms.1 = (bf16[256,512]{1,0:T(8,128)(2,1)S(1)}, bf16[256,512]{1,0:T(8,128)(2,1)S(1)}, bf16[256,512]{1,0:T(8,128)(2,1)S(1)}, bf16[256,512]{1,0:T(8,128)(2,1...) custom-call(s32[1]{0:T(128)} %bitcast.parity_ref, ...), custom_call_target="tpu_custom_call" | custom-call | flops 822083584 | bytes 3301376 | tf_op jit(solution)/shard_map/far_terms/pallas_call | solution.py:131
  4.3 0.5 %collective-permute-start.1 = (bf16[256,512]{1,0:T(8,128)(2,1)S(1)}, bf16[256,512]{1,0:T(8,128)(2,1)S(1)}, u32[]{:S(2)}, u32[]{:S(2)}) collective-permute-start(bf16[256,512]{1,0:T(8,128)(2,1)S(1)} %get-tuple-element.28), channel_id=1, source_target_pairs={{0,2},{1,3},{2,0},{3,1},{4,6},{5,7},{6,4},{7,5},{8,10},{9,11},{10,... | collective-permute-start | bytes 786440 | tf_op jit(solution)/shard_map/ppermute | solution.py:155
  4.8 0.1 collective-permute-start
  4.9 0.4 %collective-permute-start.2 = (bf16[256,512]{1,0:T(8,128)(2,1)S(1)}, bf16[256,512]{1,0:T(8,128)(2,1)S(1)}, u32[]{:S(2)}, u32[]{:S(2)}) collective-permute-start(bf16[256,512]{1,0:T(8,128)(2,1)S(1)} %get-tuple-element.32), channel_id=1, source_target_pairs={{0,2},{1,3},{2,0},{3,1},{4,6},{5,7},{6,4},{7,5},{8,10},{9,11},{10,... | collective-permute-start | bytes 786440 | tf_op jit(solution)/shard_map/ppermute | solution.py:155
  5.3 1.1 %own_sent.1 = (bf16[256,512]{1,0:T(8,128)(2,1)S(1)}, bf16[256,512]{1,0:T(8,128)(2,1)S(1)}) custom-call(bf16[392,512]{1,0:T(8,128)(2,1)S(1)} %get-tuple-element.21.refs_0_, bf16[512,512]{1,0:T(8,128)(2,1)S(1)} %get-tuple-element.22.refs_1_, f32[1,512]{1,0:T(1,128)S(1)} %get-tuple-element.23.refs_2_, bf16[392,512]{1,0:T(8,128)(2,1)S(1)} %get-tuple-element.24.refs_3_), custom_call_target="tpu_custom_call" | custom-call | flops 411041792 | bytes 1851392 | tf_op jit(solution)/shard_map/own_sent/pallas_call | solution.py:131
  6.4 0.0 collective-permute-done.1
  6.4 0.1 add_convert_fusion
  6.5 0.0 collective-permute-done
  6.5 0.1 add_convert_fusion.1
  6.6 2.8 %collective-permute-start.3 = (bf16[256,512]{1,0:T(8,128)(2,1)S(1)}, bf16[256,512]{1,0:T(8,128)(2,1)S(1)}, u32[]{:S(2)}, u32[]{:S(2)}) collective-permute-start(bf16[256,512]{1,0:T(8,128)(2,1)S(1)} %add_convert_fusion.1), channel_id=1, source_target_pairs={{0,8},{1,9},{2,6},{3,7},{4,12},{5,13},{6,2},{7,3},{8,0},{9,1},{10,... | collective-permute-start | bytes 786440 | tf_op jit(solution)/shard_map/ppermute | solution.py:155
  9.4 0.0 collective-permute-start.7
  9.4 1.5 %collective-permute-start.8 = (bf16[256,512]{1,0:T(8,128)(2,1)S(1)}, bf16[256,512]{1,0:T(8,128)(2,1)S(1)}, u32[]{:S(2)}, u32[]{:S(2)}) collective-permute-start(bf16[256,512]{1,0:T(8,128)(2,1)S(1)} %add_convert_fusion), channel_id=1, source_target_pairs={{0,8},{1,9},{2,6},{3,7},{4,12},{5,13},{6,2},{7,3},{8,0},{9,1},{10,... | collective-permute-start | bytes 786440 | tf_op jit(solution)/shard_map/ppermute | solution.py:155
  11.0 2.5 %own_kept.1 = (bf16[256,512]{1,0:T(8,128)(2,1)S(1)}, bf16[256,512]{1,0:T(8,128)(2,1)S(1)}) custom-call(s32[1]{0:T(128)} %bitcast.4.parity_ref, s32[1]{0:T(128)} %bitcast.5.half_ref.next_ref, s32[1]{0:T(128)} %bitcast.5.half_ref.next_ref, bf16[392,512]{1,0:T(8,128)(2,1)} %refs_0_.3, bf16[512,2048]{1,0:T(8,128)(2,1)} %refs_1_.3, f32[1,2048]{1,0:T(1,128)} %bitcast.45, ...), custom_call_target="tpu_custom_call" | custom-call | flops 411041792 | bytes 1851392 | tf_op jit(solution)/shard_map/own_kept/pallas_call | solution.py:131
  13.5 0.0 copy-start
  13.6 0.0 copy-start.1
  13.6 0.0 collective-permute-done.2
  13.6 0.2 collective-permute-done.3
  13.8 0.1 fusion.1
  13.8 2.0 %collective-permute-start.4 = (bf16[2,64,512]{2,1,0:T(8,128)(2,1)S(1)}, bf16[2,64,512]{2,1,0:T(8,128)(2,1)S(1)}, u32[]{:S(2)}, u32[]{:S(2)}) collective-permute-start(bf16[2,64,512]{2,1,0:T(8,128)(2,1)S(1)} %fusion.1), channel_id=1, source_target_pairs={{0,4},{1,5},{2,10},{3,11},{4,0},{5,1},{6,14},{7,15},{8,12},{9,13},... | collective-permute-start | bytes 393224 | tf_op jit(solution)/shard_map/ppermute | solution.py:155
  15.9 0.0 collective-permute-done.7
  15.9 0.8 %collective-permute-done.8 = bf16[256,512]{1,0:T(8,128)(2,1)S(1)} collective-permute-done((bf16[256,512]{1,0:T(8,128)(2,1)S(1)}, bf16[256,512]{1,0:T(8,128)(2,1)S(1)}, u32[]{:S(2)}, u32[]{:S(2)}) %collective-permute-start.8) | collective-permute-done | bytes 262176 | tf_op jit(solution)/shard_map/ppermute | solution.py:155
  16.7 0.1 fusion.2
  16.8 2.5 %collective-permute-start.9 = (bf16[2,64,512]{2,1,0:T(8,128)(2,1)S(1)}, bf16[2,64,512]{2,1,0:T(8,128)(2,1)S(1)}, u32[]{:S(2)}, u32[]{:S(2)}) collective-permute-start(bf16[2,64,512]{2,1,0:T(8,128)(2,1)S(1)} %fusion.2), channel_id=1, source_target_pairs={{0,4},{1,5},{2,10},{3,11},{4,0},{5,1},{6,14},{7,15},{8,12},{9,13},... | collective-permute-start | bytes 393224 | tf_op jit(solution)/shard_map/ppermute | solution.py:155
  19.2 0.0 collective-permute-done.4
  19.3 0.1 bitcast_add_fusion.1
  19.3 2.7 %collective-permute-start.5 = (bf16[64,512]{1,0:T(8,128)(2,1)S(1)}, bf16[64,512]{1,0:T(8,128)(2,1)S(1)}, u32[]{:S(2)}, u32[]{:S(2)}) collective-permute-start(bf16[64,512]{1,0:T(8,128)(2,1)S(1)} %fusion.5), channel_id=1, source_target_pairs={{0,16},{1,17},{2,18},{3,19},{4,20},{5,21},{6,22},{7,23},{8,24},{9,... | collective-permute-start | bytes 196616 | tf_op jit(solution)/shard_map/ppermute | solution.py:155
  22.1 0.1 collective-permute-done.9
  22.2 0.1 bitcast_add_fusion
  22.3 3.0 %collective-permute-start.10 = (bf16[64,512]{1,0:T(8,128)(2,1)S(1)}, bf16[64,512]{1,0:T(8,128)(2,1)S(1)}, u32[]{:S(2)}, u32[]{:S(2)}) collective-permute-start(bf16[64,512]{1,0:T(8,128)(2,1)S(1)} %fusion.6), channel_id=1, source_target_pairs={{0,16},{1,17},{2,18},{3,19},{4,20},{5,21},{6,22},{7,23},{8,24},{9,... | collective-permute-start | bytes 196616 | tf_op jit(solution)/shard_map/ppermute | solution.py:155
  25.3 0.0 collective-permute-done.5
  25.4 1.6 %collective-permute-start.6 = (bf16[64,512]{1,0:T(8,128)(2,1)S(1)}, bf16[64,512]{1,0:T(8,128)(2,1)S(1)}, u32[]{:S(2)}, u32[]{:S(2)}) collective-permute-start(bf16[64,512]{1,0:T(8,128)(2,1)S(1)} %fusion.4), channel_id=1, source_target_pairs={{0,1},{1,0},{2,3},{3,2},{4,5},{5,4},{6,7},{7,6},{8,9},{9,8},{10,11... | collective-permute-start | bytes 196616 | tf_op jit(solution)/shard_map/ppermute | solution.py:155
  26.9 0.7 %collective-permute-done.10 = bf16[64,512]{1,0:T(8,128)(2,1)S(1)} collective-permute-done((bf16[64,512]{1,0:T(8,128)(2,1)S(1)}, bf16[64,512]{1,0:T(8,128)(2,1)S(1)}, u32[]{:S(2)}, u32[]{:S(2)}) %collective-permute-start.10) | collective-permute-done | bytes 65568 | tf_op jit(solution)/shard_map/ppermute | solution.py:155
  27.6 1.9 %collective-permute-start.11 = (bf16[64,512]{1,0:T(8,128)(2,1)S(1)}, bf16[64,512]{1,0:T(8,128)(2,1)S(1)}, u32[]{:S(2)}, u32[]{:S(2)}) collective-permute-start(bf16[64,512]{1,0:T(8,128)(2,1)S(1)} %fusion.3), channel_id=1, source_target_pairs={{0,1},{1,0},{2,3},{3,2},{4,5},{5,4},{6,7},{7,6},{8,9},{9,8},{10,11... | collective-permute-start | bytes 196616 | tf_op jit(solution)/shard_map/ppermute | solution.py:155
  29.5 0.6 %collective-permute-done.6 = bf16[64,512]{1,0:T(8,128)(2,1)S(1)} collective-permute-done((bf16[64,512]{1,0:T(8,128)(2,1)S(1)}, bf16[64,512]{1,0:T(8,128)(2,1)S(1)}, u32[]{:S(2)}, u32[]{:S(2)}) %collective-permute-start.6) | collective-permute-done | bytes 65568 | tf_op jit(solution)/shard_map/ppermute | solution.py:155
  30.1 1.8 %collective-permute-done.11 = bf16[64,512]{1,0:T(8,128)(2,1)S(1)} collective-permute-done((bf16[64,512]{1,0:T(8,128)(2,1)S(1)}, bf16[64,512]{1,0:T(8,128)(2,1)S(1)}, u32[]{:S(2)}, u32[]{:S(2)}) %collective-permute-start.11) | collective-permute-done | bytes 65568 | tf_op jit(solution)/shard_map/ppermute | solution.py:155
  31.9 0.0 copy-done
  32.0 0.0 copy-done.1
  32.0 0.9 %multiply_subtract_fusion = (f32[128,512]{1,0:T(8,128)}, f32[128,512]{1,0:T(8,128)}) fusion(f32[128,512]{1,0:T(8,128)S(1)} %copy-done, f32[64,512]{1,0:T(8,128)S(1)} %convert_add_fusion, f32[64,512]{1,0:T(8,128)S(1)} %convert_add_fusion.1, f32[128,512]{1,0:T(8,128)S(1)} %copy-done.1), kind=kLoop, calls=%fused_computation.6 | loop fusion | flops 458752 | bytes 1310720 | tf_op jit(solution)/shard_map/sub | solution.py:172
  (6 shorter events, 0.1 us)
Async XLA Ops:
  4.3 2.1 %collective-permute-start.1 = (bf16[256,512]{1,0:T(8,128)(2,1)S(1)}, bf16[256,512]{1,0:T(8,128)(2,1)S(1)}, u32[]{:S(2)}, u32[]{:S(2)}) collective-permute-start(bf16[256,512]{1,0:T(8,128)(2,1)S(1)} %get-tuple-element.28), channel_id=1, source_target_pairs={{0,2},{1,3},{2,0},{3,1},{4,6},{5,7},{6,4},{7,5},{8,10},{9,11},{10,... | collective-permute-start | bytes 786440 | tf_op jit(solution)/shard_map/ppermute | solution.py:155
  4.8 1.7 %collective-permute-start = (bf16[256,512]{1,0:T(8,128)(2,1)S(1)}, bf16[256,512]{1,0:T(8,128)(2,1)S(1)}, u32[]{:S(2)}, u32[]{:S(2)}) collective-permute-start(bf16[256,512]{1,0:T(8,128)(2,1)S(1)} %get-tuple-element.26), channel_id=1, source_target_pairs={{0,2},{1,3},{2,0},{3,1},{4,6},{5,7},{6,4},{7,5},{8,10},{9,11},{10,... | collective-permute-start | bytes 786440 | tf_op jit(solution)/shard_map/ppermute | solution.py:155
  4.9 8.7 %collective-permute-start.2 = (bf16[256,512]{1,0:T(8,128)(2,1)S(1)}, bf16[256,512]{1,0:T(8,128)(2,1)S(1)}, u32[]{:S(2)}, u32[]{:S(2)}) collective-permute-start(bf16[256,512]{1,0:T(8,128)(2,1)S(1)} %get-tuple-element.32), channel_id=1, source_target_pairs={{0,2},{1,3},{2,0},{3,1},{4,6},{5,7},{6,4},{7,5},{8,10},{9,11},{10,... | collective-permute-start | bytes 786440 | tf_op jit(solution)/shard_map/ppermute | solution.py:155
  6.6 7.2 %collective-permute-start.3 = (bf16[256,512]{1,0:T(8,128)(2,1)S(1)}, bf16[256,512]{1,0:T(8,128)(2,1)S(1)}, u32[]{:S(2)}, u32[]{:S(2)}) collective-permute-start(bf16[256,512]{1,0:T(8,128)(2,1)S(1)} %add_convert_fusion.1), channel_id=1, source_target_pairs={{0,8},{1,9},{2,6},{3,7},{4,12},{5,13},{6,2},{7,3},{8,0},{9,1},{10,... | collective-permute-start | bytes 786440 | tf_op jit(solution)/shard_map/ppermute | solution.py:155
  9.4 6.4 %collective-permute-start.7 = (bf16[256,512]{1,0:T(8,128)(2,1)S(1)}, bf16[256,512]{1,0:T(8,128)(2,1)S(1)}, u32[]{:S(2)}, u32[]{:S(2)}) collective-permute-start(bf16[256,512]{1,0:T(8,128)(2,1)S(1)} %get-tuple-element.37), channel_id=1, source_target_pairs={{0,2},{1,3},{2,0},{3,1},{4,6},{5,7},{6,4},{7,5},{8,10},{9,11},{10,... | collective-permute-start | bytes 786440 | tf_op jit(solution)/shard_map/ppermute | solution.py:155
  9.4 7.3 %collective-permute-start.8 = (bf16[256,512]{1,0:T(8,128)(2,1)S(1)}, bf16[256,512]{1,0:T(8,128)(2,1)S(1)}, u32[]{:S(2)}, u32[]{:S(2)}) collective-permute-start(bf16[256,512]{1,0:T(8,128)(2,1)S(1)} %add_convert_fusion), channel_id=1, source_target_pairs={{0,8},{1,9},{2,6},{3,7},{4,12},{5,13},{6,2},{7,3},{8,0},{9,1},{10,... | collective-permute-start | bytes 786440 | tf_op jit(solution)/shard_map/ppermute | solution.py:155
  13.5 18.4 %copy-start = (f32[128,512]{1,0:T(8,128)S(1)}, f32[128,512]{1,0:T(8,128)}, u32[]{:S(2)}) copy-start(f32[128,512]{1,0:T(8,128)} %param.10) | copy-start | bytes 786436
  13.6 18.4 %copy-start.1 = (f32[128,512]{1,0:T(8,128)S(1)}, f32[128,512]{1,0:T(8,128)}, u32[]{:S(2)}) copy-start(f32[128,512]{1,0:T(8,128)} %param.11) | copy-start | bytes 786436
  13.8 5.4 %collective-permute-start.4 = (bf16[2,64,512]{2,1,0:T(8,128)(2,1)S(1)}, bf16[2,64,512]{2,1,0:T(8,128)(2,1)S(1)}, u32[]{:S(2)}, u32[]{:S(2)}) collective-permute-start(bf16[2,64,512]{2,1,0:T(8,128)(2,1)S(1)} %fusion.1), channel_id=1, source_target_pairs={{0,4},{1,5},{2,10},{3,11},{4,0},{5,1},{6,14},{7,15},{8,12},{9,13},... | collective-permute-start | bytes 393224 | tf_op jit(solution)/shard_map/ppermute | solution.py:155
  16.8 5.4 %collective-permute-start.9 = (bf16[2,64,512]{2,1,0:T(8,128)(2,1)S(1)}, bf16[2,64,512]{2,1,0:T(8,128)(2,1)S(1)}, u32[]{:S(2)}, u32[]{:S(2)}) collective-permute-start(bf16[2,64,512]{2,1,0:T(8,128)(2,1)S(1)} %fusion.2), channel_id=1, source_target_pairs={{0,4},{1,5},{2,10},{3,11},{4,0},{5,1},{6,14},{7,15},{8,12},{9,13},... | collective-permute-start | bytes 393224 | tf_op jit(solution)/shard_map/ppermute | solution.py:155
  19.3 6.0 %collective-permute-start.5 = (bf16[64,512]{1,0:T(8,128)(2,1)S(1)}, bf16[64,512]{1,0:T(8,128)(2,1)S(1)}, u32[]{:S(2)}, u32[]{:S(2)}) collective-permute-start(bf16[64,512]{1,0:T(8,128)(2,1)S(1)} %fusion.5), channel_id=1, source_target_pairs={{0,16},{1,17},{2,18},{3,19},{4,20},{5,21},{6,22},{7,23},{8,24},{9,... | collective-permute-start | bytes 196616 | tf_op jit(solution)/shard_map/ppermute | solution.py:155
  22.3 5.3 %collective-permute-start.10 = (bf16[64,512]{1,0:T(8,128)(2,1)S(1)}, bf16[64,512]{1,0:T(8,128)(2,1)S(1)}, u32[]{:S(2)}, u32[]{:S(2)}) collective-permute-start(bf16[64,512]{1,0:T(8,128)(2,1)S(1)} %fusion.6), channel_id=1, source_target_pairs={{0,16},{1,17},{2,18},{3,19},{4,20},{5,21},{6,22},{7,23},{8,24},{9,... | collective-permute-start | bytes 196616 | tf_op jit(solution)/shard_map/ppermute | solution.py:155
  25.4 4.7 %collective-permute-start.6 = (bf16[64,512]{1,0:T(8,128)(2,1)S(1)}, bf16[64,512]{1,0:T(8,128)(2,1)S(1)}, u32[]{:S(2)}, u32[]{:S(2)}) collective-permute-start(bf16[64,512]{1,0:T(8,128)(2,1)S(1)} %fusion.4), channel_id=1, source_target_pairs={{0,1},{1,0},{2,3},{3,2},{4,5},{5,4},{6,7},{7,6},{8,9},{9,8},{10,11... | collective-permute-start | bytes 196616 | tf_op jit(solution)/shard_map/ppermute | solution.py:155
  27.6 4.3 %collective-permute-start.11 = (bf16[64,512]{1,0:T(8,128)(2,1)S(1)}, bf16[64,512]{1,0:T(8,128)(2,1)S(1)}, u32[]{:S(2)}, u32[]{:S(2)}) collective-permute-start(bf16[64,512]{1,0:T(8,128)(2,1)S(1)} %fusion.3), channel_id=1, source_target_pairs={{0,1},{1,0},{2,3},{3,2},{4,5},{5,4},{6,7},{7,6},{8,9},{9,8},{10,11... | collective-permute-start | bytes 196616 | tf_op jit(solution)/shard_map/ppermute | solution.py:155

commit v6 on v5

--- a/solution.py
+++ b/solution.py
@@ -20,32 +20,38 @@
 BF16 = jnp.bfloat16
 
 
-def term_rows(piece, parts, blocks, out_refs, x_ref, w_ref, gain_ref, u_ref, conv_ref, grad_ref):
-    rows, channels = u_ref.shape
+def term_rows(piece, parts, blocks, groups, out_refs, w_ref, gain_ref, conv_ref, grad_ref):
+    rows, channels = groups[0][1].shape
     block = channels // blocks
+    count = len(groups)
 
     def columns(b):
         return slice(b * block, (b + 1) * block)
 
-    def convolve(b):
-        conv_ref[b] = jnp.dot(x_ref[...], w_ref[:, columns(b)], preferred_element_type=F32)
-
-    def differentiate(b):
-        conv = conv_ref[b]
+    def convolve(i):
+        b, g = divmod(i, count)
+        conv_ref[i] = jnp.dot(groups[g][0][...], w_ref[:, columns(b)], preferred_element_type=F32)
+
+    def differentiate(i):
+        b, g = divmod(i, count)
+        conv = conv_ref[i]
         center = jnp.sum(conv, axis=0, keepdims=True) * (1.0 / rows)
         spread = conv - center
-        upstream = u_ref[:, columns(b)].astype(F32)
+        upstream = groups[g][1][:, columns(b)].astype(F32)
         inverse = lax.rsqrt(jnp.sum(spread * spread, axis=0, keepdims=True) * (1.0 / rows) + EPS)
         shift_grad = jnp.sum(upstream, axis=0, keepdims=True)
         gain_grad = jnp.sum(upstream * spread, axis=0, keepdims=True) * inverse
         scale = gain_ref[:, columns(b)] * inverse
         step = scale * (1.0 / rows)
         grad = scale * upstream - (step * shift_grad + spread * (step * inverse * gain_grad))
-        grad_ref[b] = grad.astype(BF16)
+        grad_ref[i] = grad.astype(BF16)
 
     def contract(b):
-        term = lax.dot_general(
-            grad_ref[b], x_ref[...], (((0,), (0,)), ((), ())), preferred_element_type=F32
+        term = sum(
+            lax.dot_general(
+                grad_ref[b * count + g], groups[g][0][...], (((0,), (0,)), ((), ())), preferred_element_type=F32
+            )
+            for g in range(count)
         ).astype(BF16)
         if parts is None:
             out_refs[0][b * block : (b + 1) * block] = term
@@ -56,78 +62,92 @@
                 out_refs[b * len(parts) + t][k * part : (k + 1) * part] = term[row : row + part]
                 row += part
 
-    for i in range(blocks + 2):
-        if 0 <= i - 2:
-            contract(i - 2)
-        if i < blocks:
+    for i in range(blocks * count + 2):
+        if i >= 2 and (i - 1) % count == 0:
+            contract((i - 1) // count - 1)
+        if i < blocks * count:
             convolve(i)
-        if 0 <= i - 1 < blocks:
+        if 0 <= i - 1 < blocks * count:
             differentiate(i - 1)
 
 
-def reading_kernel(piece, column, next_column, parts, blocks, outs, parity_ref, half_ref, next_ref, *refs):
-    hbm, out_refs, refs = refs[:4], refs[4 : 4 + outs], refs[4 + outs :]
-    held = None
-    if next_column is not None:
-        x_ref, *held = refs[:4]
-        *own, conv_ref, grad_ref, sem = refs[4:]
+def reading_kernel(piece, column, parts, blocks, outs, ahead, borrows, parity_ref, half_ref, next_ref, *refs):
+    hbm, refs = refs[:4], refs[4:]
+    width = hbm[0].shape[1]
+    borrowed, refs = refs[:borrows], refs[borrows:]
+    out_refs, refs = refs[:outs], refs[outs:]
+    if ahead is not None:
+        loan_ref, *held = refs[:4]
+        refs = refs[4:]
+        x_ref, lent_ref = loan_ref.at[:, pl.ds(0, width)], loan_ref.at[:, pl.ds(width, held[2].shape[1])]
     else:
-        x_ref, *own, conv_ref, grad_ref, sem = refs
-    copies = [pltpu.make_async_copy(hbm[0], x_ref, sem.at[0])]
-    used = 1
-
-    def reads(to, column, *where):
+        x_ref, *refs = refs
+    w_ref, gain_ref, u_ref, *loans, conv_ref, grad_ref, sem = refs
+    used = 0
+
+    def read(a, b):
         nonlocal used
+        used += 1
+        return pltpu.make_async_copy(a, b, sem.at[used - 1])
+
+    def reads(sources, targets, column, first, *where):
         made = []
-        for k in range(to[0].shape[1] // piece):
-            source = pl.ds(pl.multiple_of(column(k, *where) * piece, piece), piece)
-            for a, b in zip(hbm[1:], to):
-                copy = pltpu.make_async_copy(a.at[:, source], b.at[:, pl.ds(k * piece, piece)], sem.at[used])
-                made.append(copy)
-                used += 1
+        for k in range(targets[0].shape[1] // piece):
+            at = pl.ds(pl.multiple_of(column(first + k, *where) * piece, piece), piece)
+            made += [read(a.at[:, at], b.at[:, pl.ds(k * piece, piece)]) for a, b in zip(sources, targets)]
         return made
 
-    copies += reads(own, column, parity_ref[0], half_ref[0])
-    later = [] if held is None else reads(held, next_column, 1 - parity_ref[0], next_ref[0])
+    here = parity_ref[0], half_ref[0]
+    copies = [read(hbm[0], x_ref)] + reads(hbm[1:], (w_ref, gain_ref, u_ref), column, 0, *here)
+    later = []
+    groups = [(x_ref, u_ref)]
+    if ahead is not None:
+        later = reads(hbm[1:], held, ahead, 0, 1 - parity_ref[0], next_ref[0])
+        later += reads(hbm[3:], [lent_ref], column, u_ref.shape[1] // piece, *here)
+    for a, b in zip(borrowed, loans):
+        copies.append(read(a, b))
+        groups.append((b.at[:, pl.ds(0, width)], b.at[:, pl.ds(width, u_ref.shape[1])]))
     for copy in copies + later:
         copy.start()
     for copy in copies:
         copy.wait()
-    term_rows(piece, parts, blocks, out_refs, x_ref, *own, conv_ref, grad_ref)
+    term_rows(piece, parts, blocks, groups, out_refs, w_ref, gain_ref, conv_ref, grad_ref)
     for copy in later:
         copy.wait()
 
 
-def holding_kernel(piece, parts, blocks, outs, *refs):
-    term_rows(piece, parts, blocks, refs[4 : 4 + outs], *refs[:4], *refs[4 + outs :])
-
-
-def term_call(name, inputs, channels, blocks, piece, parts, column=None, where=(), next_column=None, next_channels=0):
-    rows, width_in = inputs[0].shape
+def holding_kernel(piece, parts, blocks, outs, loan_ref, w_ref, gain_ref, u_ref, *refs):
+    x_ref = loan_ref.at[:, pl.ds(0, w_ref.shape[0])]
+    term_rows(piece, parts, blocks, [(x_ref, u_ref)], refs[:outs], w_ref, gain_ref, *refs[outs:])
+
+
+def term_call(name, inputs, channels, blocks, piece, parts, column=None, where=(), ahead=None, far=()):
+    rows, width_in = inputs[0].shape[0], inputs[1].shape[0]
     block = channels // blocks
+    groups = 2 if far else 1
     sizes = [channels] if parts is None else [part * (block // piece) for part in parts] * blocks
     hbm = pl.BlockSpec(memory_space=pltpu.HBM)
     vmem = pl.BlockSpec(memory_space=pltpu.VMEM)
     smem = pl.BlockSpec(memory_space=pltpu.SMEM)
     x = pltpu.VMEM((rows, width_in), BF16)
+    loan = pltpu.VMEM((rows, width_in + channels), BF16)
+    read = [pltpu.VMEM((width_in, channels), BF16), pltpu.VMEM((1, channels), F32), pltpu.VMEM((rows, channels), BF16)]
     outs = [pltpu.VMEM((size, width_in), BF16) for size in sizes]
-
-    def read(count):
-        return [pltpu.VMEM((width_in, count), BF16), pltpu.VMEM((1, count), F32), pltpu.VMEM((rows, count), BF16)]
-
-    scratch = [pltpu.VMEM((blocks, rows, block), F32), pltpu.VMEM((blocks, rows, block), BF16)]
+    scratch = [pltpu.VMEM((blocks * groups, rows, block), F32), pltpu.VMEM((blocks * groups, rows, block), BF16)]
     if column is None:
         kernel = functools.partial(holding_kernel, piece, parts, blocks, len(outs))
         in_specs = [vmem] * 4
     else:
-        kernel = functools.partial(reading_kernel, piece, column, next_column, parts, blocks, len(outs))
-        in_specs = [smem] * 3 + [hbm] * 4
-        inputs = [i.reshape(1) for i in where] + [pltpu.with_memory_space_constraint(a, pltpu.HBM) for a in inputs]
-        scratch = read(channels) + scratch + [pltpu.SemaphoreType.DMA((1 + 3 * ((channels + next_channels) // piece),))]
-        if next_column is None:
-            scratch = [x] + scratch
+        kernel = functools.partial(reading_kernel, piece, column, parts, blocks, len(outs), ahead, len(far))
+        in_specs = [smem] * 3 + [hbm] * 4 + [pl.BlockSpec(memory_space=pl.ANY)] * len(far)
+        inputs = [pltpu.with_memory_space_constraint(a, pltpu.HBM) for a in inputs]
+        inputs = [*(i.reshape(1) for i in where), *inputs, *far]
+        pieces = channels // piece
+        if ahead is None:
+            scratch = [x, *read] + [loan] * len(far) + scratch + [pltpu.SemaphoreType.DMA((2 + 3 * pieces,))]
         else:
-            outs += [x] + read(next_channels)
+            outs += [loan, *read]
+            scratch = read + scratch + [pltpu.SemaphoreType.DMA((1 + 7 * pieces,))]
     return pl.pallas_call(
         kernel,
         out_shape=tuple(outs),
@@ -135,9 +155,9 @@
         out_specs=(vmem,) * len(outs),
         scratch_shapes=scratch,
         cost_estimate=pl.CostEstimate(
-            flops=4 * rows * channels * width_in,
-            bytes_accessed=2 * (rows * channels + channels * width_in * 2 + rows * width_in),
-            transcendentals=channels,
+            flops=4 * groups * rows * channels * width_in,
+            bytes_accessed=2 * (groups * rows * (channels + width_in) + channels * width_in * 2),
+            transcendentals=groups * channels,
         ),
         compiler_params=pltpu.CompilerParams(vmem_limit_bytes=16 * 2**20),
         name=name,
@@ -197,20 +217,19 @@
     def laid(arrays):
         return [array.reshape(2, 2, part, width_in) for array, part in zip(arrays, parts)]
 
-    far = term_call(
-        "far_terms", inputs, 8 * run, 2, run, parts, column, (1 - core, 1 - second, 1 - first), column, 4 * run
+    *far_sent, loan, w, g, u = term_call(
+        "far_sent", inputs, 4 * run, 1, run, parts, column, (1 - core, 1 - second, 1 - first), column
     )
-    far, held = far[: 2 * count], far[2 * count :]
-    got_sent = [flip(array, 2, 2) for array in far[:count]]
-    got = laid([flip(array, 2, 2) for array in far[count:]])
-    own_sent = term_call("own_sent", held, 4 * run, 1, run, parts)
+    got_sent = jnp.split(flip(jnp.concatenate(far_sent, axis=0), 2, 2), len(parts), axis=0)
+    far = (flip(loan, 2, 2),)
+    own_sent = term_call("own_sent", (loan, w, g, u), 4 * run, 1, run, parts)
     sent = [wide(*pair).astype(BF16) for pair in zip(own_sent, got_sent)]
     sent, core, kept = lax.optimization_barrier((sent, core, first))
     arrived = laid([flip(array, 4, 8) for array in sent])
-    own = laid(term_call("own_kept", inputs, 4 * run, 1, run, parts, column, (core, kept, kept)))
+    own = laid(term_call("kept", inputs, 4 * run, 1, run, parts, column, (core, kept, kept), None, far))
 
     def half_of(t, index):
-        return wide(pick(own[t], index), pick(got[t], index), pick(arrived[t], index))
+        return wide(pick(own[t], index), pick(arrived[t], index))
 
     again = [flip(half_of(t, 1 - second), 8, 4) for t in range(count)]
     planes = [wide(half_of(t, second), again[t]) for t in range(count)]

time: 33 us -> 32.5 us (0.985)
  starting transfers between devices: 19.1 us -> 17.3 us
  waiting for transfers between devices: 4.28 us -> 5.94 us
    ppermute x12 -> x10, starting transfers between devices: 19.1 us -> 17.3 us  [send(): return lax.ppermute(array.astype(BF16), (NODE, LOCAL), pairs)]
    ppermute x12 -> x10, waiting for transfers between devices: 4.28 us -> 5.94 us  [send(): return lax.ppermute(array.astype(BF16), (NODE, LOCAL), pairs)]
  transfers between devices with their start and end apart: 12 -> 10, of which waited for: 6 -> 7; matrix products, arithmetic and copies ran while one was open for 1% -> 1% of each run, Pallas kernels for 11% -> 13%
where the time goes in v6:
time: 32.5 us; the launch traced here: 32.3 us
  starting transfers between devices  17.3 us (53%)
  Pallas kernels  7.03 us (22%)
  waiting for transfers between devices  5.94 us (18%)
  other arithmetic  1.27 us (4%)
  between operations  0.77 us (2%)
    ppermute x10, starting transfers between devices, send(): return lax.ppermute(array.astype(BF16), (NODE, LOCAL), pairs)  17.3 us
    pallas_call x3, Pallas kernels, term_call(): pl.pallas_call(kernel, out_shape=tuple(outs), in_specs=in_specs, out_spec...  7.03 us
    ppermute x10, waiting for transfers between devices, send(): return lax.ppermute(array.astype(BF16), (NODE, LOCAL), pairs)  5.94 us
    sub x1, other arithmetic, local_fn(): new_weight = master_weight - RATE * new_velocity  0.87 us
  transfers between devices with their start and end apart: 10, of which 7 were waited for; matrix products, arithmetic and copies ran while one was open for 1% of the time, Pallas kernels for 13%

profile of v6, /device:TPU:0, one launch (start us, length us, event | category | flops | bytes accessed | tf_op | source)
XLA Modules:
  0.0 32.3 jit_solution(3863155683564585604)
XLA Ops:
  0.6 2.7 %far_sent.1 = (bf16[256,512]{1,0:T(8,128)(2,1)S(1)}, bf16[256,512]{1,0:T(8,128)(2,1)S(1)}, bf16[392,1024]{1,0:T(8,128)(2,1)S(1)}, bf16[512,512]{1,0:T(8,128)(2,1...) custom-call(s32[1]{0:T(128)} %bitcast.parity_ref, s32[1]{0:T(128)} %bitcast.1.half_ref, s32[1]{0:T(128)} %bitcast.2.next_ref, ...), custom_call_target="tpu_custom_call" | custom-call | flops 411041792 | bytes 1851392 | tf_op jit(solution)/shard_map/far_sent/pallas_call | solution.py:151
  3.4 0.5 %collective-permute-start = (bf16[512,512]{1,0:T(8,128)(2,1)S(1)}, bf16[512,512]{1,0:T(8,128)(2,1)S(1)}, u32[]{:S(2)}, u32[]{:S(2)}) collective-permute-start(bf16[512,512]{1,0:T(8,128)(2,1)S(1)} %pad_maximum_fusion), channel_id=1, source_target_pairs={{0,2},{1,3},{2,0},{3,1},{4,6},{5,7},{6,4},{7,5},{8,10},{9,11},{10,... | collective-permute-start | bytes 1572872 | tf_op jit(solution)/shard_map/ppermute | solution.py:175
  4.0 0.1 collective-permute-start.1
  4.0 1.1 %own_sent.1 = (bf16[256,512]{1,0:T(8,128)(2,1)S(1)}, bf16[256,512]{1,0:T(8,128)(2,1)S(1)}) custom-call(bf16[392,1024]{1,0:T(8,128)(2,1)S(1)} %get-tuple-element.19.loan_ref, bf16[512,512]{1,0:T(8,128)(2,1)S(1)} %get-tuple-element.20.w_ref, f32[1,512]{1,0:T(1,128)S(1)} %get-tuple-element.21.gain_ref, bf16[392,512]{1,0:T(8,128)(2,1)S(1)} %get-tuple-element.22.u_ref), custom_call_target="tpu_custom_call" | custom-call | flops 411041792 | bytes 1851392 | tf_op jit(solution)/shard_map/own_sent/pallas_call | solution.py:151
  5.2 0.4 %collective-permute-done = bf16[512,512]{1,0:T(8,128)(2,1)S(1)} collective-permute-done((bf16[512,512]{1,0:T(8,128)(2,1)S(1)}, bf16[512,512]{1,0:T(8,128)(2,1)S(1)}, u32[]{:S(2)}, u32[]{:S(2)}) %collective-permute-start) | collective-permute-done | bytes 524320 | tf_op jit(solution)/shard_map/ppermute | solution.py:175
  5.5 0.1 add_convert_fusion
  5.6 3.0 %collective-permute-start.2 = (bf16[256,512]{1,0:T(8,128)(2,1)S(1)}, bf16[256,512]{1,0:T(8,128)(2,1)S(1)}, u32[]{:S(2)}, u32[]{:S(2)}) collective-permute-start(bf16[256,512]{1,0:T(8,128)(2,1)S(1)} %get-tuple-element.30), channel_id=1, source_target_pairs={{0,8},{1,9},{2,6},{3,7},{4,12},{5,13},{6,2},{7,3},{8,0},{9,1},{10,... | collective-permute-start | bytes 786440 | tf_op jit(solution)/shard_map/ppermute | solution.py:175
  8.6 0.1 collective-permute-start.6
  8.7 0.0 collective-permute-done.1.refs_4_
  8.7 3.2 %kept.1 = (bf16[256,512]{1,0:T(8,128)(2,1)S(1)}, bf16[256,512]{1,0:T(8,128)(2,1)S(1)}) custom-call(s32[1]{0:T(128)} %bitcast.4.parity_ref, s32[1]{0:T(128)} %bitcast.5.half_ref.next_ref, s32[1]{0:T(128)} %bitcast.5.half_ref.next_ref, bf16[392,512]{1,0:T(8,128)(2,1)} %refs_0_.3, bf16[512,2048]{1,0:T(8,128)(2,1)} %refs_1_.3, f32[1,2048]{1,0:T(1,128)} %bitcast.39, ...), custom_call_target="tpu_custom_call" | custom-call | flops 822083584 | bytes 2654208 | tf_op jit(solution)/shard_map/kept/pallas_call | solution.py:151
  11.9 0.0 copy-start
  11.9 0.0 copy-start.1
  11.9 1.0 %collective-permute-done.2 = bf16[256,512]{1,0:T(8,128)(2,1)S(1)} collective-permute-done((bf16[256,512]{1,0:T(8,128)(2,1)S(1)}, bf16[256,512]{1,0:T(8,128)(2,1)S(1)}, u32[]{:S(2)}, u32[]{:S(2)}) %collective-permute-start.2) | collective-permute-done | bytes 262176 | tf_op jit(solution)/shard_map/ppermute | solution.py:175
  13.0 2.0 %collective-permute-start.3 = (bf16[2,64,512]{2,1,0:T(8,128)(2,1)S(1)}, bf16[2,64,512]{2,1,0:T(8,128)(2,1)S(1)}, u32[]{:S(2)}, u32[]{:S(2)}) collective-permute-start(bf16[2,64,512]{2,1,0:T(8,128)(2,1)S(1)} %fusion.1), channel_id=1, source_target_pairs={{0,4},{1,5},{2,10},{3,11},{4,0},{5,1},{6,14},{7,15},{8,12},{9,13},... | collective-permute-start | bytes 393224 | tf_op jit(solution)/shard_map/ppermute | solution.py:175
  15.1 1.2 %collective-permute-done.6 = bf16[256,512]{1,0:T(8,128)(2,1)S(1)} collective-permute-done((bf16[256,512]{1,0:T(8,128)(2,1)S(1)}, bf16[256,512]{1,0:T(8,128)(2,1)S(1)}, u32[]{:S(2)}, u32[]{:S(2)}) %collective-permute-start.6) | collective-permute-done | bytes 262176 | tf_op jit(solution)/shard_map/ppermute | solution.py:175
  16.3 2.3 %collective-permute-start.7 = (bf16[2,64,512]{2,1,0:T(8,128)(2,1)S(1)}, bf16[2,64,512]{2,1,0:T(8,128)(2,1)S(1)}, u32[]{:S(2)}, u32[]{:S(2)}) collective-permute-start(bf16[2,64,512]{2,1,0:T(8,128)(2,1)S(1)} %fusion.2), channel_id=1, source_target_pairs={{0,4},{1,5},{2,10},{3,11},{4,0},{5,1},{6,14},{7,15},{8,12},{9,13},... | collective-permute-start | bytes 393224 | tf_op jit(solution)/shard_map/ppermute | solution.py:175
  18.6 0.0 collective-permute-done.3
  18.7 2.7 %collective-permute-start.4 = (bf16[64,512]{1,0:T(8,128)(2,1)S(1)}, bf16[64,512]{1,0:T(8,128)(2,1)S(1)}, u32[]{:S(2)}, u32[]{:S(2)}) collective-permute-start(bf16[64,512]{1,0:T(8,128)(2,1)S(1)} %fusion.5), channel_id=1, source_target_pairs={{0,16},{1,17},{2,18},{3,19},{4,20},{5,21},{6,22},{7,23},{8,24},{9,... | collective-permute-start | bytes 196616 | tf_op jit(solution)/shard_map/ppermute | solution.py:175
  21.4 0.2 collective-permute-done.7
  21.7 3.2 %collective-permute-start.8 = (bf16[64,512]{1,0:T(8,128)(2,1)S(1)}, bf16[64,512]{1,0:T(8,128)(2,1)S(1)}, u32[]{:S(2)}, u32[]{:S(2)}) collective-permute-start(bf16[64,512]{1,0:T(8,128)(2,1)S(1)} %fusion.6), channel_id=1, source_target_pairs={{0,16},{1,17},{2,18},{3,19},{4,20},{5,21},{6,22},{7,23},{8,24},{9,... | collective-permute-start | bytes 196616 | tf_op jit(solution)/shard_map/ppermute | solution.py:175
  24.8 0.0 collective-permute-done.4
  24.8 1.6 %collective-permute-start.5 = (bf16[64,512]{1,0:T(8,128)(2,1)S(1)}, bf16[64,512]{1,0:T(8,128)(2,1)S(1)}, u32[]{:S(2)}, u32[]{:S(2)}) collective-permute-start(bf16[64,512]{1,0:T(8,128)(2,1)S(1)} %fusion.4), channel_id=1, source_target_pairs={{0,1},{1,0},{2,3},{3,2},{4,5},{5,4},{6,7},{7,6},{8,9},{9,8},{10,11... | collective-permute-start | bytes 196616 | tf_op jit(solution)/shard_map/ppermute | solution.py:175
  26.4 0.7 %collective-permute-done.8 = bf16[64,512]{1,0:T(8,128)(2,1)S(1)} collective-permute-done((bf16[64,512]{1,0:T(8,128)(2,1)S(1)}, bf16[64,512]{1,0:T(8,128)(2,1)S(1)}, u32[]{:S(2)}, u32[]{:S(2)}) %collective-permute-start.8) | collective-permute-done | bytes 65568 | tf_op jit(solution)/shard_map/ppermute | solution.py:175
  27.1 1.9 %collective-permute-start.9 = (bf16[64,512]{1,0:T(8,128)(2,1)S(1)}, bf16[64,512]{1,0:T(8,128)(2,1)S(1)}, u32[]{:S(2)}, u32[]{:S(2)}) collective-permute-start(bf16[64,512]{1,0:T(8,128)(2,1)S(1)} %fusion.3), channel_id=1, source_target_pairs={{0,1},{1,0},{2,3},{3,2},{4,5},{5,4},{6,7},{7,6},{8,9},{9,8},{10,11... | collective-permute-start | bytes 196616 | tf_op jit(solution)/shard_map/ppermute | solution.py:175
  29.0 0.8 %collective-permute-done.5 = bf16[64,512]{1,0:T(8,128)(2,1)S(1)} collective-permute-done((bf16[64,512]{1,0:T(8,128)(2,1)S(1)}, bf16[64,512]{1,0:T(8,128)(2,1)S(1)}, u32[]{:S(2)}, u32[]{:S(2)}) %collective-permute-start.5) | collective-permute-done | bytes 65568 | tf_op jit(solution)/shard_map/ppermute | solution.py:175
  29.8 1.6 %collective-permute-done.9 = bf16[64,512]{1,0:T(8,128)(2,1)S(1)} collective-permute-done((bf16[64,512]{1,0:T(8,128)(2,1)S(1)}, bf16[64,512]{1,0:T(8,128)(2,1)S(1)}, u32[]{:S(2)}, u32[]{:S(2)}) %collective-permute-start.9) | collective-permute-done | bytes 65568 | tf_op jit(solution)/shard_map/ppermute | solution.py:175
  31.4 0.0 copy-done
  31.4 0.0 copy-done.1
  31.4 0.9 %multiply_subtract_fusion = (f32[128,512]{1,0:T(8,128)}, f32[128,512]{1,0:T(8,128)}) fusion(f32[128,512]{1,0:T(8,128)S(1)} %copy-done, f32[64,512]{1,0:T(8,128)S(1)} %convert_add_fusion, f32[64,512]{1,0:T(8,128)S(1)} %convert_add_fusion.1, f32[128,512]{1,0:T(8,128)S(1)} %copy-done.1), kind=kLoop, calls=%fused_computation.7 | loop fusion | flops 458752 | bytes 1310720 | tf_op jit(solution)/shard_map/sub | solution.py:192
  (11 shorter events, 0.3 us)
Async XLA Ops:
  3.4 2.1 %collective-permute-start = (bf16[512,512]{1,0:T(8,128)(2,1)S(1)}, bf16[512,512]{1,0:T(8,128)(2,1)S(1)}, u32[]{:S(2)}, u32[]{:S(2)}) collective-permute-start(bf16[512,512]{1,0:T(8,128)(2,1)S(1)} %pad_maximum_fusion), channel_id=1, source_target_pairs={{0,2},{1,3},{2,0},{3,1},{4,6},{5,7},{6,4},{7,5},{8,10},{9,11},{10,... | collective-permute-start | bytes 1572872 | tf_op jit(solution)/shard_map/ppermute | solution.py:175
  4.0 4.8 %collective-permute-start.1 = (bf16[392,1024]{1,0:T(8,128)(2,1)S(1)}, bf16[392,1024]{1,0:T(8,128)(2,1)S(1)}, u32[]{:S(2)}, u32[]{:S(2)}) collective-permute-start(bf16[392,1024]{1,0:T(8,128)(2,1)S(1)} %get-tuple-element.19.loan_ref), channel_id=1, source_target_pairs={{0,2},{1,3},{2,0},{3,1},{4,6},{5,7},{6,4},{7,5},{8,10},{9,11},{10,... | collective-permute-start | bytes 2408456 | tf_op jit(solution)/shard_map/ppermute | solution.py:175
  5.6 7.3 %collective-permute-start.2 = (bf16[256,512]{1,0:T(8,128)(2,1)S(1)}, bf16[256,512]{1,0:T(8,128)(2,1)S(1)}, u32[]{:S(2)}, u32[]{:S(2)}) collective-permute-start(bf16[256,512]{1,0:T(8,128)(2,1)S(1)} %get-tuple-element.30), channel_id=1, source_target_pairs={{0,8},{1,9},{2,6},{3,7},{4,12},{5,13},{6,2},{7,3},{8,0},{9,1},{10,... | collective-permute-start | bytes 786440 | tf_op jit(solution)/shard_map/ppermute | solution.py:175
  8.6 7.6 %collective-permute-start.6 = (bf16[256,512]{1,0:T(8,128)(2,1)S(1)}, bf16[256,512]{1,0:T(8,128)(2,1)S(1)}, u32[]{:S(2)}, u32[]{:S(2)}) collective-permute-start(bf16[256,512]{1,0:T(8,128)(2,1)S(1)} %get-tuple-element.34), channel_id=1, source_target_pairs={{0,8},{1,9},{2,6},{3,7},{4,12},{5,13},{6,2},{7,3},{8,0},{9,1},{10,... | collective-permute-start | bytes 786440 | tf_op jit(solution)/shard_map/ppermute | solution.py:175
  11.9 19.5 %copy-start = (f32[128,512]{1,0:T(8,128)S(1)}, f32[128,512]{1,0:T(8,128)}, u32[]{:S(2)}) copy-start(f32[128,512]{1,0:T(8,128)} %param.10) | copy-start | bytes 786436
  11.9 19.5 %copy-start.1 = (f32[128,512]{1,0:T(8,128)S(1)}, f32[128,512]{1,0:T(8,128)}, u32[]{:S(2)}) copy-start(f32[128,512]{1,0:T(8,128)} %param.11) | copy-start | bytes 786436
  13.0 5.6 %collective-permute-start.3 = (bf16[2,64,512]{2,1,0:T(8,128)(2,1)S(1)}, bf16[2,64,512]{2,1,0:T(8,128)(2,1)S(1)}, u32[]{:S(2)}, u32[]{:S(2)}) collective-permute-start(bf16[2,64,512]{2,1,0:T(8,128)(2,1)S(1)} %fusion.1), channel_id=1, source_target_pairs={{0,4},{1,5},{2,10},{3,11},{4,0},{5,1},{6,14},{7,15},{8,12},{9,13},... | collective-permute-start | bytes 393224 | tf_op jit(solution)/shard_map/ppermute | solution.py:175
  16.3 5.3 %collective-permute-start.7 = (bf16[2,64,512]{2,1,0:T(8,128)(2,1)S(1)}, bf16[2,64,512]{2,1,0:T(8,128)(2,1)S(1)}, u32[]{:S(2)}, u32[]{:S(2)}) collective-permute-start(bf16[2,64,512]{2,1,0:T(8,128)(2,1)S(1)} %fusion.2), channel_id=1, source_target_pairs={{0,4},{1,5},{2,10},{3,11},{4,0},{5,1},{6,14},{7,15},{8,12},{9,13},... | collective-permute-start | bytes 393224 | tf_op jit(solution)/shard_map/ppermute | solution.py:175
  18.7 6.1 %collective-permute-start.4 = (bf16[64,512]{1,0:T(8,128)(2,1)S(1)}, bf16[64,512]{1,0:T(8,128)(2,1)S(1)}, u32[]{:S(2)}, u32[]{:S(2)}) collective-permute-start(bf16[64,512]{1,0:T(8,128)(2,1)S(1)} %fusion.5), channel_id=1, source_target_pairs={{0,16},{1,17},{2,18},{3,19},{4,20},{5,21},{6,22},{7,23},{8,24},{9,... | collective-permute-start | bytes 196616 | tf_op jit(solution)/shard_map/ppermute | solution.py:175
  21.7 5.4 %collective-permute-start.8 = (bf16[64,512]{1,0:T(8,128)(2,1)S(1)}, bf16[64,512]{1,0:T(8,128)(2,1)S(1)}, u32[]{:S(2)}, u32[]{:S(2)}) collective-permute-start(bf16[64,512]{1,0:T(8,128)(2,1)S(1)} %fusion.6), channel_id=1, source_target_pairs={{0,16},{1,17},{2,18},{3,19},{4,20},{5,21},{6,22},{7,23},{8,24},{9,... | collective-permute-start | bytes 196616 | tf_op jit(solution)/shard_map/ppermute | solution.py:175
  24.8 4.9 %collective-permute-start.5 = (bf16[64,512]{1,0:T(8,128)(2,1)S(1)}, bf16[64,512]{1,0:T(8,128)(2,1)S(1)}, u32[]{:S(2)}, u32[]{:S(2)}) collective-permute-start(bf16[64,512]{1,0:T(8,128)(2,1)S(1)} %fusion.4), channel_id=1, source_target_pairs={{0,1},{1,0},{2,3},{3,2},{4,5},{5,4},{6,7},{7,6},{8,9},{9,8},{10,11... | collective-permute-start | bytes 196616 | tf_op jit(solution)/shard_map/ppermute | solution.py:175
  27.1 4.3 %collective-permute-start.9 = (bf16[64,512]{1,0:T(8,128)(2,1)S(1)}, bf16[64,512]{1,0:T(8,128)(2,1)S(1)}, u32[]{:S(2)}, u32[]{:S(2)}) collective-permute-start(bf16[64,512]{1,0:T(8,128)(2,1)S(1)} %fusion.3), channel_id=1, source_target_pairs={{0,1},{1,0},{2,3},{3,2},{4,5},{5,4},{6,7},{7,6},{8,9},{9,8},{10,11... | collective-permute-start | bytes 196616 | tf_op jit(solution)/shard_map/ppermute | solution.py:175

commit v7 on v6

--- a/solution.py
+++ b/solution.py
@@ -83,37 +83,39 @@
     else:
         x_ref, *refs = refs
     w_ref, gain_ref, u_ref, *loans, conv_ref, grad_ref, sem = refs
-    used = 0
-
-    def read(a, b):
-        nonlocal used
-        used += 1
-        return pltpu.make_async_copy(a, b, sem.at[used - 1])
+    copies, waits = [], []
+
+    def read(target, *pairs):
+        done = sem.at[len(waits)]
+        copies.extend(pltpu.make_async_copy(a, b, done) for a, b in pairs)
+        waits.append(pltpu.make_async_copy(target, target, done))
 
     def reads(sources, targets, column, first, *where):
-        made = []
-        for k in range(targets[0].shape[1] // piece):
-            at = pl.ds(pl.multiple_of(column(first + k, *where) * piece, piece), piece)
-            made += [read(a.at[:, at], b.at[:, pl.ds(k * piece, piece)]) for a, b in zip(sources, targets)]
-        return made
+        at = [
+            pl.ds(pl.multiple_of(column(first + k, *where) * piece, piece), piece)
+            for k in range(targets[0].shape[1] // piece)
+        ]
+        for a, b in zip(sources, targets):
+            read(b, *((a.at[:, there], b.at[:, pl.ds(k * piece, piece)]) for k, there in enumerate(at)))
 
     here = parity_ref[0], half_ref[0]
-    copies = [read(hbm[0], x_ref)] + reads(hbm[1:], (w_ref, gain_ref, u_ref), column, 0, *here)
-    later = []
+    read(x_ref, (hbm[0], x_ref))
+    reads(hbm[1:], (w_ref, gain_ref, u_ref), column, 0, *here)
     groups = [(x_ref, u_ref)]
+    for a, b in zip(borrowed, loans):
+        read(b, (a, b))
+        groups.append((b.at[:, pl.ds(0, width)], b.at[:, pl.ds(width, u_ref.shape[1])]))
+    needed = len(waits)
     if ahead is not None:
-        later = reads(hbm[1:], held, ahead, 0, 1 - parity_ref[0], next_ref[0])
-        later += reads(hbm[3:], [lent_ref], column, u_ref.shape[1] // piece, *here)
-    for a, b in zip(borrowed, loans):
-        copies.append(read(a, b))
-        groups.append((b.at[:, pl.ds(0, width)], b.at[:, pl.ds(width, u_ref.shape[1])]))
-    for copy in copies + later:
+        reads(hbm[1:], held, ahead, 0, 1 - parity_ref[0], next_ref[0])
+        reads(hbm[3:], [lent_ref], column, u_ref.shape[1] // piece, *here)
+    for copy in copies:
         copy.start()
-    for copy in copies:
-        copy.wait()
+    for wait in waits[:needed]:
+        wait.wait()
     term_rows(piece, parts, blocks, groups, out_refs, w_ref, gain_ref, conv_ref, grad_ref)
-    for copy in later:
-        copy.wait()
+    for wait in waits[needed:]:
+        wait.wait()
 
 
 def holding_kernel(piece, parts, blocks, outs, loan_ref, w_ref, gain_ref, u_ref, *refs):
@@ -142,12 +144,11 @@
         in_specs = [smem] * 3 + [hbm] * 4 + [pl.BlockSpec(memory_space=pl.ANY)] * len(far)
         inputs = [pltpu.with_memory_space_constraint(a, pltpu.HBM) for a in inputs]
         inputs = [*(i.reshape(1) for i in where), *inputs, *far]
-        pieces = channels // piece
         if ahead is None:
-            scratch = [x, *read] + [loan] * len(far) + scratch + [pltpu.SemaphoreType.DMA((2 + 3 * pieces,))]
+            scratch = [x, *read] + [loan] * len(far) + scratch + [pltpu.SemaphoreType.DMA((4 + len(far),))]
         else:
             outs += [loan, *read]
-            scratch = read + scratch + [pltpu.SemaphoreType.DMA((1 + 7 * pieces,))]
+            scratch = read + scratch + [pltpu.SemaphoreType.DMA((8,))]
     return pl.pallas_call(
         kernel,
         out_shape=tuple(outs),
@@ -164,6 +165,38 @@
     )(*inputs)
 
 
+def update_kernel(part, rows, grad_ref, rest_ref, velocity_ref, weight_ref, *refs):
+    new_velocity_hbm, new_weight_hbm, new_velocity_ref, new_weight_ref, sem = refs[-5:]
+    at = pl.ds(rows * part, part)
+    weight = weight_ref[at, :]
+    gradient = grad_ref[...].astype(F32) + rest_ref[...].astype(F32)
+    new_velocity = MOMENTUM * velocity_ref[at, :] + gradient + DECAY * weight
+    new_velocity_ref[...] = new_velocity
+    first = pltpu.make_async_copy(new_velocity_ref, new_velocity_hbm.at[at, :], sem.at[0])
+    first.start()
+    new_weight_ref[...] = weight - RATE * new_velocity
+    second = pltpu.make_async_copy(new_weight_ref, new_weight_hbm.at[at, :], sem.at[1])
+    second.start()
+    first.wait()
+    second.wait()
+
+
+def update_call(rows, grad, rest, velocity, weight, previous):
+    part, width_in = grad.shape
+    vmem = pl.BlockSpec(memory_space=pltpu.VMEM)
+    hbm = pl.BlockSpec(memory_space=pltpu.HBM)
+    return pl.pallas_call(
+        functools.partial(update_kernel, part, rows),
+        out_shape=(jax.ShapeDtypeStruct(velocity.shape, F32),) * 2,
+        in_specs=[vmem] * 4 + [hbm] * len(previous),
+        out_specs=(hbm, hbm),
+        scratch_shapes=[pltpu.VMEM((part, width_in), F32)] * 2 + [pltpu.SemaphoreType.DMA((2,))],
+        input_output_aliases={4 + i: i for i in range(len(previous))},
+        compiler_params=pltpu.CompilerParams(vmem_limit_bytes=4 * 2**20),
+        name="update",
+    )(grad, rest, velocity, weight, *previous)
+
+
 def pick(array, *index):
     start = [jnp.asarray(i).astype(jnp.uint32) for i in index]
     rest = array.shape[len(index) :]
@@ -185,22 +218,21 @@
     run = conv_weight.shape[1] // nodes
     inputs = (block_input, conv_weight, bn_gain.reshape(1, -1), out_cotangent)
     if (nodes, lanes) == (16, 2) and run % TILE == 0:
-        gradient, (master_weight, velocity) = sum_halves(run, *inputs, (master_weight, velocity))
-    else:
-        gradient = sum_lanes(run, *inputs)
+        return step_halves(run, *inputs, master_weight, velocity)
+    gradient = sum_lanes(run, *inputs)
     new_velocity = MOMENTUM * velocity + gradient + DECAY * master_weight
     new_weight = master_weight - RATE * new_velocity
     return (new_velocity, new_weight)
 
 
-def sum_halves(run, block_input, conv_weight, gain, out_cotangent, state):
+def step_halves(run, block_input, conv_weight, gain, out_cotangent, master_weight, velocity):
     width_in = block_input.shape[1]
     inputs = (block_input, conv_weight, gain, out_cotangent)
     node = lax.axis_index(NODE)
     core, side, low, high = node & 1, (node >> 1) & 1, (node >> 2) & 1, node >> 3
-    is_one = core == 0
-    first = jnp.where(is_one, low, side)
-    second = jnp.where(is_one, side, low)
+    is_zero = core == 0
+    first = jnp.where(is_zero, low, side)
+    second = jnp.where(is_zero, side, low)
 
     def column(k, parity, half):
         half, k = (half, k) if k < 4 else (1 - half, k - 4)
@@ -233,9 +265,12 @@
 
     again = [flip(half_of(t, 1 - second), 8, 4) for t in range(count)]
     planes = [wide(half_of(t, second), again[t]) for t in range(count)]
-    planes[0], *state = lax.optimization_barrier((planes[0], *state))
+    planes[0], velocity, master_weight = lax.optimization_barrier((planes[0], velocity, master_weight))
     both = [wide(pick(plane, high), flip(pick(plane, 1 - high), 16, 16)).astype(BF16) for plane in planes]
-    return jnp.concatenate([wide(array, flip(array, 1, 1)) for array in both], axis=0), state
+    out = ()
+    for t, array in enumerate(both):
+        out = update_call(t, array, flip(array, 1, 1), velocity, master_weight, out)
+    return out
 
 
 def sum_lanes(run, block_input, conv_weight, gain, out_cotangent):

time: 32.5 us -> 32.1 us (0.988)
  Pallas kernels: 7.03 us -> 8.27 us
  other arithmetic: 1.27 us -> 0.36 us
  waiting for transfers between devices: 5.94 us -> 5.26 us
    pallas_call x0 -> x2, Pallas kernels: none -> 1.5 us  [update_call(): pl.pallas_call(functools.partial(update_kernel, part, rows), out_shape=(j...]
    sub x1 -> x0, other arithmetic: 0.87 us -> none  [local_fn(): new_weight = master_weight - RATE * new_velocity]
    ppermute x10, waiting for transfers between devices: 5.94 us -> 5.26 us  [send(): return lax.ppermute(array.astype(BF16), (NODE, LOCAL), pairs)]
  transfers between devices with their start and end apart: 10 -> 10, of which waited for: 7 -> 7; matrix products, arithmetic and copies ran while one was open for 1% -> 1% of each run, Pallas kernels for 13% -> 16%
where the time goes in v7:
time: 32.1 us; the launch traced here: 32 us
  starting transfers between devices  17.3 us (54%)
  Pallas kernels  8.27 us (26%)
  waiting for transfers between devices  5.26 us (16%)
  between operations  0.76 us (2%)
  other arithmetic  0.36 us (1%)
    ppermute x10, starting transfers between devices, send(): return lax.ppermute(array.astype(BF16), (NODE, LOCAL), pairs)  17.3 us
    pallas_call x3, Pallas kernels, term_call(): pl.pallas_call(kernel, out_shape=tuple(outs), in_specs=in_specs, out_spec...  6.76 us
    ppermute x10, waiting for transfers between devices, send(): return lax.ppermute(array.astype(BF16), (NODE, LOCAL), pairs)  5.26 us
    pallas_call x2, Pallas kernels, update_call(): pl.pallas_call(functools.partial(update_kernel, part, rows), out_shape=(j...  1.5 us
  transfers between devices with their start and end apart: 10, of which 7 were waited for; matrix products, arithmetic and copies ran while one was open for 1% of the time, Pallas kernels for 16%

profile of v7, /device:TPU:0, one launch (start us, length us, event | category | flops | bytes accessed | tf_op | source)
XLA Modules:
  0.0 32.0 jit_solution(5464463351689509717)
XLA Ops:
  0.6 2.5 %far_sent.1 = (bf16[256,512]{1,0:T(8,128)(2,1)S(1)}, bf16[256,512]{1,0:T(8,128)(2,1)S(1)}, bf16[392,1024]{1,0:T(8,128)(2,1)S(1)}, bf16[512,512]{1,0:T(8,128)(2,1...) custom-call(s32[1]{0:T(128)} %bitcast.parity_ref, s32[1]{0:T(128)} %bitcast.1.half_ref, s32[1]{0:T(128)} %bitcast.2.next_ref, ...), custom_call_target="tpu_custom_call" | custom-call | flops 411041792 | bytes 1851392 | tf_op jit(solution)/shard_map/far_sent/pallas_call | solution.py:152
  3.2 0.5 %collective-permute-start = (bf16[512,512]{1,0:T(8,128)(2,1)S(1)}, bf16[512,512]{1,0:T(8,128)(2,1)S(1)}, u32[]{:S(2)}, u32[]{:S(2)}) collective-permute-start(bf16[512,512]{1,0:T(8,128)(2,1)S(1)} %pad_maximum_fusion), channel_id=1, source_target_pairs={{0,2},{1,3},{2,0},{3,1},{4,6},{5,7},{6,4},{7,5},{8,10},{9,11},{10,... | collective-permute-start | bytes 1572872 | tf_op jit(solution)/shard_map/ppermute | solution.py:208
  3.8 0.1 collective-permute-start.1
  3.8 1.1 %own_sent.1 = (bf16[256,512]{1,0:T(8,128)(2,1)S(1)}, bf16[256,512]{1,0:T(8,128)(2,1)S(1)}) custom-call(bf16[392,1024]{1,0:T(8,128)(2,1)S(1)} %get-tuple-element.21.loan_ref, bf16[512,512]{1,0:T(8,128)(2,1)S(1)} %get-tuple-element.22.w_ref, f32[1,512]{1,0:T(1,128)S(1)} %get-tuple-element.23.gain_ref, bf16[392,512]{1,0:T(8,128)(2,1)S(1)} %get-tuple-element.24.u_ref), custom_call_target="tpu_custom_call" | custom-call | flops 411041792 | bytes 1851392 | tf_op jit(solution)/shard_map/own_sent/pallas_call | solution.py:152
  5.0 0.3 %collective-permute-done = bf16[512,512]{1,0:T(8,128)(2,1)S(1)} collective-permute-done((bf16[512,512]{1,0:T(8,128)(2,1)S(1)}, bf16[512,512]{1,0:T(8,128)(2,1)S(1)}, u32[]{:S(2)}, u32[]{:S(2)}) %collective-permute-start) | collective-permute-done | bytes 524320 | tf_op jit(solution)/shard_map/ppermute | solution.py:208
  5.3 0.1 add_convert_fusion
  5.4 3.0 %collective-permute-start.6 = (bf16[256,512]{1,0:T(8,128)(2,1)S(1)}, bf16[256,512]{1,0:T(8,128)(2,1)S(1)}, u32[]{:S(2)}, u32[]{:S(2)}) collective-permute-start(bf16[256,512]{1,0:T(8,128)(2,1)S(1)} %get-tuple-element.34), channel_id=1, source_target_pairs={{0,8},{1,9},{2,6},{3,7},{4,12},{5,13},{6,2},{7,3},{8,0},{9,1},{10,... | collective-permute-start | bytes 786440 | tf_op jit(solution)/shard_map/ppermute | solution.py:208
  8.4 0.1 collective-permute-start.2
  8.5 0.0 collective-permute-done.1.refs_4_
  8.5 3.1 %kept.1 = (bf16[256,512]{1,0:T(8,128)(2,1)S(1)}, bf16[256,512]{1,0:T(8,128)(2,1)S(1)}) custom-call(s32[1]{0:T(128)} %bitcast.4.parity_ref, s32[1]{0:T(128)} %bitcast.5.half_ref.next_ref, s32[1]{0:T(128)} %bitcast.5.half_ref.next_ref, bf16[392,512]{1,0:T(8,128)(2,1)} %refs_0_.3, bf16[512,2048]{1,0:T(8,128)(2,1)} %refs_1_.3, f32[1,2048]{1,0:T(1,128)} %bitcast.39, ...), custom_call_target="tpu_custom_call" | custom-call | flops 822083584 | bytes 2654208 | tf_op jit(solution)/shard_map/kept/pallas_call | solution.py:152
  11.7 0.0 copy-start
  11.7 0.0 copy-start.1
  11.7 1.1 %collective-permute-done.6 = bf16[256,512]{1,0:T(8,128)(2,1)S(1)} collective-permute-done((bf16[256,512]{1,0:T(8,128)(2,1)S(1)}, bf16[256,512]{1,0:T(8,128)(2,1)S(1)}, u32[]{:S(2)}, u32[]{:S(2)}) %collective-permute-start.6) | collective-permute-done | bytes 262176 | tf_op jit(solution)/shard_map/ppermute | solution.py:208
  12.8 2.0 %collective-permute-start.7 = (bf16[2,64,512]{2,1,0:T(8,128)(2,1)S(1)}, bf16[2,64,512]{2,1,0:T(8,128)(2,1)S(1)}, u32[]{:S(2)}, u32[]{:S(2)}) collective-permute-start(bf16[2,64,512]{2,1,0:T(8,128)(2,1)S(1)} %fusion.1), channel_id=1, source_target_pairs={{0,4},{1,5},{2,10},{3,11},{4,0},{5,1},{6,14},{7,15},{8,12},{9,13},... | collective-permute-start | bytes 393224 | tf_op jit(solution)/shard_map/ppermute | solution.py:208
  14.9 1.2 %collective-permute-done.2 = bf16[256,512]{1,0:T(8,128)(2,1)S(1)} collective-permute-done((bf16[256,512]{1,0:T(8,128)(2,1)S(1)}, bf16[256,512]{1,0:T(8,128)(2,1)S(1)}, u32[]{:S(2)}, u32[]{:S(2)}) %collective-permute-start.2) | collective-permute-done | bytes 262176 | tf_op jit(solution)/shard_map/ppermute | solution.py:208
  16.1 2.3 %collective-permute-start.3 = (bf16[2,64,512]{2,1,0:T(8,128)(2,1)S(1)}, bf16[2,64,512]{2,1,0:T(8,128)(2,1)S(1)}, u32[]{:S(2)}, u32[]{:S(2)}) collective-permute-start(bf16[2,64,512]{2,1,0:T(8,128)(2,1)S(1)} %fusion), channel_id=1, source_target_pairs={{0,4},{1,5},{2,10},{3,11},{4,0},{5,1},{6,14},{7,15},{8,12},{9,13},... | collective-permute-start | bytes 393224 | tf_op jit(solution)/shard_map/ppermute | solution.py:208
  18.4 0.0 collective-permute-done.7
  18.5 2.7 %collective-permute-start.8 = (bf16[64,512]{1,0:T(8,128)(2,1)S(1)}, bf16[64,512]{1,0:T(8,128)(2,1)S(1)}, u32[]{:S(2)}, u32[]{:S(2)}) collective-permute-start(bf16[64,512]{1,0:T(8,128)(2,1)S(1)} %fusion.5), channel_id=1, source_target_pairs={{0,16},{1,17},{2,18},{3,19},{4,20},{5,21},{6,22},{7,23},{8,24},{9,... | collective-permute-start | bytes 196616 | tf_op jit(solution)/shard_map/ppermute | solution.py:208
  21.2 0.2 collective-permute-done.3
  21.5 3.2 %collective-permute-start.4 = (bf16[64,512]{1,0:T(8,128)(2,1)S(1)}, bf16[64,512]{1,0:T(8,128)(2,1)S(1)}, u32[]{:S(2)}, u32[]{:S(2)}) collective-permute-start(bf16[64,512]{1,0:T(8,128)(2,1)S(1)} %fusion.4), channel_id=1, source_target_pairs={{0,16},{1,17},{2,18},{3,19},{4,20},{5,21},{6,22},{7,23},{8,24},{9,... | collective-permute-start | bytes 196616 | tf_op jit(solution)/shard_map/ppermute | solution.py:208
  24.6 0.0 collective-permute-done.8
  24.6 1.6 %collective-permute-start.9 = (bf16[64,512]{1,0:T(8,128)(2,1)S(1)}, bf16[64,512]{1,0:T(8,128)(2,1)S(1)}, u32[]{:S(2)}, u32[]{:S(2)}) collective-permute-start(bf16[64,512]{1,0:T(8,128)(2,1)S(1)} %fusion.2.grad_ref), channel_id=1, source_target_pairs={{0,1},{1,0},{2,3},{3,2},{4,5},{5,4},{6,7},{7,6},{8,9},{9,8},{10,11... | collective-permute-start | bytes 196616 | tf_op jit(solution)/shard_map/ppermute | solution.py:208
  26.2 0.7 %collective-permute-done.4 = bf16[64,512]{1,0:T(8,128)(2,1)S(1)} collective-permute-done((bf16[64,512]{1,0:T(8,128)(2,1)S(1)}, bf16[64,512]{1,0:T(8,128)(2,1)S(1)}, u32[]{:S(2)}, u32[]{:S(2)}) %collective-permute-start.4) | collective-permute-done | bytes 65568 | tf_op jit(solution)/shard_map/ppermute | solution.py:208
  26.9 1.9 %collective-permute-start.5 = (bf16[64,512]{1,0:T(8,128)(2,1)S(1)}, bf16[64,512]{1,0:T(8,128)(2,1)S(1)}, u32[]{:S(2)}, u32[]{:S(2)}) collective-permute-start(bf16[64,512]{1,0:T(8,128)(2,1)S(1)} %fusion.3.grad_ref), channel_id=1, source_target_pairs={{0,1},{1,0},{2,3},{3,2},{4,5},{5,4},{6,7},{7,6},{8,9},{9,8},{10,11... | collective-permute-start | bytes 196616 | tf_op jit(solution)/shard_map/ppermute | solution.py:208
  28.8 0.8 %collective-permute-done.9.rest_ref = bf16[64,512]{1,0:T(8,128)(2,1)S(1)} collective-permute-done((bf16[64,512]{1,0:T(8,128)(2,1)S(1)}, bf16[64,512]{1,0:T(8,128)(2,1)S(1)}, u32[]{:S(2)}, u32[]{:S(2)}) %collective-permute-start.9) | collective-permute-done | bytes 65568 | tf_op jit(solution)/shard_map/ppermute | solution.py:208
  29.6 0.0 copy-done
  29.6 0.0 copy-done.1
  29.6 0.8 %update.2 = (f32[128,512]{1,0:T(8,128)}, f32[128,512]{1,0:T(8,128)}) custom-call(bf16[64,512]{1,0:T(8,128)(2,1)S(1)} %fusion.2.grad_ref, bf16[64,512]{1,0:T(8,128)(2,1)S(1)} %collective-permute-done.9.rest_ref, f32[128,512]{1,0:T(8,128)S(1)} %copy-done, f32[128,512]{1,0:T(8,128)S(1)} %copy-done.1), custom_call_target="tpu_custom_call" | custom-call | tf_op jit(solution)/shard_map/update/pallas_call | solution.py:188
  30.4 0.9 %collective-permute-done.5.rest_ref = bf16[64,512]{1,0:T(8,128)(2,1)S(1)} collective-permute-done((bf16[64,512]{1,0:T(8,128)(2,1)S(1)}, bf16[64,512]{1,0:T(8,128)(2,1)S(1)}, u32[]{:S(2)}, u32[]{:S(2)}) %collective-permute-start.5) | collective-permute-done | bytes 65568 | tf_op jit(solution)/shard_map/ppermute | solution.py:208
  31.2 0.8 %update.3 = (f32[128,512]{1,0:T(8,128)}, f32[128,512]{1,0:T(8,128)}) custom-call(bf16[64,512]{1,0:T(8,128)(2,1)S(1)} %fusion.3.grad_ref, bf16[64,512]{1,0:T(8,128)(2,1)S(1)} %collective-permute-done.5.rest_ref, f32[128,512]{1,0:T(8,128)S(1)} %copy-done, f32[128,512]{1,0:T(8,128)S(1)} %copy-done.1, ...), custom_call_target="tpu_custom_call", output_to_operand_aliasing={{0}: (4, {}), {1}: (5, {})} | custom-call | tf_op jit(solution)/shard_map/update/pallas_call | solution.py:188
  (9 shorter events, 0.3 us)
Async XLA Ops:
  3.2 2.1 %collective-permute-start = (bf16[512,512]{1,0:T(8,128)(2,1)S(1)}, bf16[512,512]{1,0:T(8,128)(2,1)S(1)}, u32[]{:S(2)}, u32[]{:S(2)}) collective-permute-start(bf16[512,512]{1,0:T(8,128)(2,1)S(1)} %pad_maximum_fusion), channel_id=1, source_target_pairs={{0,2},{1,3},{2,0},{3,1},{4,6},{5,7},{6,4},{7,5},{8,10},{9,11},{10,... | collective-permute-start | bytes 1572872 | tf_op jit(solution)/shard_map/ppermute | solution.py:208
  3.8 4.8 %collective-permute-start.1 = (bf16[392,1024]{1,0:T(8,128)(2,1)S(1)}, bf16[392,1024]{1,0:T(8,128)(2,1)S(1)}, u32[]{:S(2)}, u32[]{:S(2)}) collective-permute-start(bf16[392,1024]{1,0:T(8,128)(2,1)S(1)} %get-tuple-element.21.loan_ref), channel_id=1, source_target_pairs={{0,2},{1,3},{2,0},{3,1},{4,6},{5,7},{6,4},{7,5},{8,10},{9,11},{10,... | collective-permute-start | bytes 2408456 | tf_op jit(solution)/shard_map/ppermute | solution.py:208
  5.4 7.4 %collective-permute-start.6 = (bf16[256,512]{1,0:T(8,128)(2,1)S(1)}, bf16[256,512]{1,0:T(8,128)(2,1)S(1)}, u32[]{:S(2)}, u32[]{:S(2)}) collective-permute-start(bf16[256,512]{1,0:T(8,128)(2,1)S(1)} %get-tuple-element.34), channel_id=1, source_target_pairs={{0,8},{1,9},{2,6},{3,7},{4,12},{5,13},{6,2},{7,3},{8,0},{9,1},{10,... | collective-permute-start | bytes 786440 | tf_op jit(solution)/shard_map/ppermute | solution.py:208
  8.4 7.6 %collective-permute-start.2 = (bf16[256,512]{1,0:T(8,128)(2,1)S(1)}, bf16[256,512]{1,0:T(8,128)(2,1)S(1)}, u32[]{:S(2)}, u32[]{:S(2)}) collective-permute-start(bf16[256,512]{1,0:T(8,128)(2,1)S(1)} %get-tuple-element.32), channel_id=1, source_target_pairs={{0,8},{1,9},{2,6},{3,7},{4,12},{5,13},{6,2},{7,3},{8,0},{9,1},{10,... | collective-permute-start | bytes 786440 | tf_op jit(solution)/shard_map/ppermute | solution.py:208
  11.7 17.9 %copy-start = (f32[128,512]{1,0:T(8,128)S(1)}, f32[128,512]{1,0:T(8,128)}, u32[]{:S(2)}) copy-start(f32[128,512]{1,0:T(8,128)} %velocity_ref.1) | copy-start | bytes 786436
  11.7 17.9 %copy-start.1 = (f32[128,512]{1,0:T(8,128)S(1)}, f32[128,512]{1,0:T(8,128)}, u32[]{:S(2)}) copy-start(f32[128,512]{1,0:T(8,128)} %weight_ref.1) | copy-start | bytes 786436
  12.8 5.6 %collective-permute-start.7 = (bf16[2,64,512]{2,1,0:T(8,128)(2,1)S(1)}, bf16[2,64,512]{2,1,0:T(8,128)(2,1)S(1)}, u32[]{:S(2)}, u32[]{:S(2)}) collective-permute-start(bf16[2,64,512]{2,1,0:T(8,128)(2,1)S(1)} %fusion.1), channel_id=1, source_target_pairs={{0,4},{1,5},{2,10},{3,11},{4,0},{5,1},{6,14},{7,15},{8,12},{9,13},... | collective-permute-start | bytes 393224 | tf_op jit(solution)/shard_map/ppermute | solution.py:208
  16.1 5.3 %collective-permute-start.3 = (bf16[2,64,512]{2,1,0:T(8,128)(2,1)S(1)}, bf16[2,64,512]{2,1,0:T(8,128)(2,1)S(1)}, u32[]{:S(2)}, u32[]{:S(2)}) collective-permute-start(bf16[2,64,512]{2,1,0:T(8,128)(2,1)S(1)} %fusion), channel_id=1, source_target_pairs={{0,4},{1,5},{2,10},{3,11},{4,0},{5,1},{6,14},{7,15},{8,12},{9,13},... | collective-permute-start | bytes 393224 | tf_op jit(solution)/shard_map/ppermute | solution.py:208
  18.5 6.1 %collective-permute-start.8 = (bf16[64,512]{1,0:T(8,128)(2,1)S(1)}, bf16[64,512]{1,0:T(8,128)(2,1)S(1)}, u32[]{:S(2)}, u32[]{:S(2)}) collective-permute-start(bf16[64,512]{1,0:T(8,128)(2,1)S(1)} %fusion.5), channel_id=1, source_target_pairs={{0,16},{1,17},{2,18},{3,19},{4,20},{5,21},{6,22},{7,23},{8,24},{9,... | collective-permute-start | bytes 196616 | tf_op jit(solution)/shard_map/ppermute | solution.py:208
  21.5 5.4 %collective-permute-start.4 = (bf16[64,512]{1,0:T(8,128)(2,1)S(1)}, bf16[64,512]{1,0:T(8,128)(2,1)S(1)}, u32[]{:S(2)}, u32[]{:S(2)}) collective-permute-start(bf16[64,512]{1,0:T(8,128)(2,1)S(1)} %fusion.4), channel_id=1, source_target_pairs={{0,16},{1,17},{2,18},{3,19},{4,20},{5,21},{6,22},{7,23},{8,24},{9,... | collective-permute-start | bytes 196616 | tf_op jit(solution)/shard_map/ppermute | solution.py:208
  24.6 5.0 %collective-permute-start.9 = (bf16[64,512]{1,0:T(8,128)(2,1)S(1)}, bf16[64,512]{1,0:T(8,128)(2,1)S(1)}, u32[]{:S(2)}, u32[]{:S(2)}) collective-permute-start(bf16[64,512]{1,0:T(8,128)(2,1)S(1)} %fusion.2.grad_ref), channel_id=1, source_target_pairs={{0,1},{1,0},{2,3},{3,2},{4,5},{5,4},{6,7},{7,6},{8,9},{9,8},{10,11... | collective-permute-start | bytes 196616 | tf_op jit(solution)/shard_map/ppermute | solution.py:208
  26.9 4.3 %collective-permute-start.5 = (bf16[64,512]{1,0:T(8,128)(2,1)S(1)}, bf16[64,512]{1,0:T(8,128)(2,1)S(1)}, u32[]{:S(2)}, u32[]{:S(2)}) collective-permute-start(bf16[64,512]{1,0:T(8,128)(2,1)S(1)} %fusion.3.grad_ref), channel_id=1, source_target_pairs={{0,1},{1,0},{2,3},{3,2},{4,5},{5,4},{6,7},{7,6},{8,9},{9,8},{10,11... | collective-permute-start | bytes 196616 | tf_op jit(solution)/shard_map/ppermute | solution.py:208

commit v8 on v7

--- a/solution.py
+++ b/solution.py
@@ -236,12 +236,12 @@
 
     def column(k, parity, half):
         half, k = (half, k) if k < 4 else (1 - half, k - 4)
-        zero = (((k % 2) * 2 + k // 2) * 2 + half) * 2 + 1
-        one = (((k % 2) * 2 + half) * 2 + k // 2) * 2
-        return jnp.where(parity == 0, one, zero)
-
-    def flip(array, zero, one):
-        return send(array, [(i, i ^ (zero if i & 2 else one)) for i in range(32)])
+        one = (((k % 2) * 2 + k // 2) * 2 + half) * 2 + 1
+        zero = (((k % 2) * 2 + half) * 2 + k // 2) * 2
+        return jnp.where(parity == 1, one, zero)
+
+    def flip(array, one, zero):
+        return send(array, [(i, i ^ (one if i & 2 else zero)) for i in range(32)])
 
     parts = [run * share // sum(STREAMS) for share in STREAMS]
     count = len(parts)
@@ -264,9 +264,13 @@
         return wide(pick(own[t], index), pick(arrived[t], index))
 
     again = [flip(half_of(t, 1 - second), 8, 4) for t in range(count)]
-    planes = [wide(half_of(t, second), again[t]) for t in range(count)]
-    planes[0], velocity, master_weight = lax.optimization_barrier((planes[0], velocity, master_weight))
-    both = [wide(pick(plane, high), flip(pick(plane, 1 - high), 16, 16)).astype(BF16) for plane in planes]
+
+    def plane(t, index):
+        return wide(pick(own[t], second, index), pick(arrived[t], second, index), pick(again[t], index))
+
+    away = [plane(t, 1 - high).astype(BF16) for t in range(count)]
+    away[0], velocity, master_weight = lax.optimization_barrier((away[0], velocity, master_weight))
+    both = [wide(plane(t, high), flip(away[t], 16, 16)).astype(BF16) for t in range(count)]
     out = ()
     for t, array in enumerate(both):
         out = update_call(t, array, flip(array, 1, 1), velocity, master_weight, out)

time: 32.1 us -> 32.1 us (level)
  no operation moved by 1% of the time
where the time goes in v8:
time: 32.1 us; the launch traced here: 31.9 us
  starting transfers between devices  17.3 us (54%)
  Pallas kernels  8.27 us (26%)
  waiting for transfers between devices  5.29 us (16%)
  between operations  0.74 us (2%)
  other arithmetic  0.37 us (1%)
    ppermute x10, starting transfers between devices, send(): return lax.ppermute(array.astype(BF16), (NODE, LOCAL), pairs)  17.3 us
    pallas_call x3, Pallas kernels, term_call(): pl.pallas_call(kernel, out_shape=tuple(outs), in_specs=in_specs, out_spec...  6.76 us
    ppermute x10, waiting for transfers between devices, send(): return lax.ppermute(array.astype(BF16), (NODE, LOCAL), pairs)  5.29 us
    pallas_call x2, Pallas kernels, update_call(): pl.pallas_call(functools.partial(update_kernel, part, rows), out_shape=(j...  1.5 us
  transfers between devices with their start and end apart: 10, of which 7 were waited for; matrix products, arithmetic and copies ran while one was open for 1% of the time, Pallas kernels for 16%

profile of v8, /device:TPU:0, one launch (start us, length us, event | category | flops | bytes accessed | tf_op | source)
XLA Modules:
  0.0 31.9 jit_solution(11739464722611539129)
XLA Ops:
  0.6 2.5 %far_sent.1 = (bf16[256,512]{1,0:T(8,128)(2,1)S(1)}, bf16[256,512]{1,0:T(8,128)(2,1)S(1)}, bf16[392,1024]{1,0:T(8,128)(2,1)S(1)}, bf16[512,512]{1,0:T(8,128)(2,1...) custom-call(s32[1]{0:T(128)} %bitcast.parity_ref, s32[1]{0:T(128)} %bitcast.1.half_ref, s32[1]{0:T(128)} %bitcast.2.next_ref, ...), custom_call_target="tpu_custom_call" | custom-call | flops 411041792 | bytes 1851392 | tf_op jit(solution)/shard_map/far_sent/pallas_call | solution.py:152
  3.2 0.5 %collective-permute-start = (bf16[512,512]{1,0:T(8,128)(2,1)S(1)}, bf16[512,512]{1,0:T(8,128)(2,1)S(1)}, u32[]{:S(2)}, u32[]{:S(2)}) collective-permute-start(bf16[512,512]{1,0:T(8,128)(2,1)S(1)} %pad_maximum_fusion), channel_id=1, source_target_pairs={{0,2},{1,3},{2,0},{3,1},{4,6},{5,7},{6,4},{7,5},{8,10},{9,11},{10,... | collective-permute-start | bytes 1572872 | tf_op jit(solution)/shard_map/ppermute | solution.py:208
  3.8 0.1 collective-permute-start.1
  3.8 1.1 %own_sent.1 = (bf16[256,512]{1,0:T(8,128)(2,1)S(1)}, bf16[256,512]{1,0:T(8,128)(2,1)S(1)}) custom-call(bf16[392,1024]{1,0:T(8,128)(2,1)S(1)} %get-tuple-element.21.loan_ref, bf16[512,512]{1,0:T(8,128)(2,1)S(1)} %get-tuple-element.22.w_ref, f32[1,512]{1,0:T(1,128)S(1)} %get-tuple-element.23.gain_ref, bf16[392,512]{1,0:T(8,128)(2,1)S(1)} %get-tuple-element.24.u_ref), custom_call_target="tpu_custom_call" | custom-call | flops 411041792 | bytes 1851392 | tf_op jit(solution)/shard_map/own_sent/pallas_call | solution.py:152
  5.0 0.3 %collective-permute-done = bf16[512,512]{1,0:T(8,128)(2,1)S(1)} collective-permute-done((bf16[512,512]{1,0:T(8,128)(2,1)S(1)}, bf16[512,512]{1,0:T(8,128)(2,1)S(1)}, u32[]{:S(2)}, u32[]{:S(2)}) %collective-permute-start) | collective-permute-done | bytes 524320 | tf_op jit(solution)/shard_map/ppermute | solution.py:208
  5.3 0.1 add_convert_fusion
  5.4 3.0 %collective-permute-start.6 = (bf16[256,512]{1,0:T(8,128)(2,1)S(1)}, bf16[256,512]{1,0:T(8,128)(2,1)S(1)}, u32[]{:S(2)}, u32[]{:S(2)}) collective-permute-start(bf16[256,512]{1,0:T(8,128)(2,1)S(1)} %get-tuple-element.34), channel_id=1, source_target_pairs={{0,8},{1,9},{2,6},{3,7},{4,12},{5,13},{6,2},{7,3},{8,0},{9,1},{10,... | collective-permute-start | bytes 786440 | tf_op jit(solution)/shard_map/ppermute | solution.py:208
  8.4 0.1 collective-permute-start.2
  8.5 0.0 collective-permute-done.1.refs_4_
  8.5 3.1 %kept.1 = (bf16[256,512]{1,0:T(8,128)(2,1)S(1)}, bf16[256,512]{1,0:T(8,128)(2,1)S(1)}) custom-call(s32[1]{0:T(128)} %bitcast.4.parity_ref, s32[1]{0:T(128)} %bitcast.5.half_ref.next_ref, s32[1]{0:T(128)} %bitcast.5.half_ref.next_ref, bf16[392,512]{1,0:T(8,128)(2,1)} %refs_0_.3, bf16[512,2048]{1,0:T(8,128)(2,1)} %refs_1_.3, f32[1,2048]{1,0:T(1,128)} %bitcast.47, ...), custom_call_target="tpu_custom_call" | custom-call | flops 822083584 | bytes 2654208 | tf_op jit(solution)/shard_map/kept/pallas_call | solution.py:152
  11.7 0.0 copy-start
  11.7 0.0 copy-start.1
  11.7 1.1 %collective-permute-done.6 = bf16[256,512]{1,0:T(8,128)(2,1)S(1)} collective-permute-done((bf16[256,512]{1,0:T(8,128)(2,1)S(1)}, bf16[256,512]{1,0:T(8,128)(2,1)S(1)}, u32[]{:S(2)}, u32[]{:S(2)}) %collective-permute-start.6) | collective-permute-done | bytes 262176 | tf_op jit(solution)/shard_map/ppermute | solution.py:208
  12.8 2.0 %collective-permute-start.7 = (bf16[2,64,512]{2,1,0:T(8,128)(2,1)S(1)}, bf16[2,64,512]{2,1,0:T(8,128)(2,1)S(1)}, u32[]{:S(2)}, u32[]{:S(2)}) collective-permute-start(bf16[2,64,512]{2,1,0:T(8,128)(2,1)S(1)} %fusion.1), channel_id=1, source_target_pairs={{0,4},{1,5},{2,10},{3,11},{4,0},{5,1},{6,14},{7,15},{8,12},{9,13},... | collective-permute-start | bytes 393224 | tf_op jit(solution)/shard_map/ppermute | solution.py:208
  14.9 1.2 %collective-permute-done.2 = bf16[256,512]{1,0:T(8,128)(2,1)S(1)} collective-permute-done((bf16[256,512]{1,0:T(8,128)(2,1)S(1)}, bf16[256,512]{1,0:T(8,128)(2,1)S(1)}, u32[]{:S(2)}, u32[]{:S(2)}) %collective-permute-start.2) | collective-permute-done | bytes 262176 | tf_op jit(solution)/shard_map/ppermute | solution.py:208
  16.1 2.3 %collective-permute-start.3 = (bf16[2,64,512]{2,1,0:T(8,128)(2,1)S(1)}, bf16[2,64,512]{2,1,0:T(8,128)(2,1)S(1)}, u32[]{:S(2)}, u32[]{:S(2)}) collective-permute-start(bf16[2,64,512]{2,1,0:T(8,128)(2,1)S(1)} %fusion), channel_id=1, source_target_pairs={{0,4},{1,5},{2,10},{3,11},{4,0},{5,1},{6,14},{7,15},{8,12},{9,13},... | collective-permute-start | bytes 393224 | tf_op jit(solution)/shard_map/ppermute | solution.py:208
  18.4 0.0 collective-permute-done.7
  18.5 2.7 %collective-permute-start.8 = (bf16[64,512]{1,0:T(8,128)(2,1)S(1)}, bf16[64,512]{1,0:T(8,128)(2,1)S(1)}, u32[]{:S(2)}, u32[]{:S(2)}) collective-permute-start(bf16[64,512]{1,0:T(8,128)(2,1)S(1)} %fusion.4), channel_id=1, source_target_pairs={{0,16},{1,17},{2,18},{3,19},{4,20},{5,21},{6,22},{7,23},{8,24},{9,... | collective-permute-start | bytes 196616 | tf_op jit(solution)/shard_map/ppermute | solution.py:208
  21.1 0.3 collective-permute-done.3
  21.4 3.2 %collective-permute-start.4 = (bf16[64,512]{1,0:T(8,128)(2,1)S(1)}, bf16[64,512]{1,0:T(8,128)(2,1)S(1)}, u32[]{:S(2)}, u32[]{:S(2)}) collective-permute-start(bf16[64,512]{1,0:T(8,128)(2,1)S(1)} %fusion.5), channel_id=1, source_target_pairs={{0,16},{1,17},{2,18},{3,19},{4,20},{5,21},{6,22},{7,23},{8,24},{9,... | collective-permute-start | bytes 196616 | tf_op jit(solution)/shard_map/ppermute | solution.py:208
  24.6 0.0 collective-permute-done.8
  24.6 1.6 %collective-permute-start.9 = (bf16[64,512]{1,0:T(8,128)(2,1)S(1)}, bf16[64,512]{1,0:T(8,128)(2,1)S(1)}, u32[]{:S(2)}, u32[]{:S(2)}) collective-permute-start(bf16[64,512]{1,0:T(8,128)(2,1)S(1)} %fusion.3.grad_ref), channel_id=1, source_target_pairs={{0,1},{1,0},{2,3},{3,2},{4,5},{5,4},{6,7},{7,6},{8,9},{9,8},{10,11... | collective-permute-start | bytes 196616 | tf_op jit(solution)/shard_map/ppermute | solution.py:208
  26.2 0.6 %collective-permute-done.4 = bf16[64,512]{1,0:T(8,128)(2,1)S(1)} collective-permute-done((bf16[64,512]{1,0:T(8,128)(2,1)S(1)}, bf16[64,512]{1,0:T(8,128)(2,1)S(1)}, u32[]{:S(2)}, u32[]{:S(2)}) %collective-permute-start.4) | collective-permute-done | bytes 65568 | tf_op jit(solution)/shard_map/ppermute | solution.py:208
  26.9 1.9 %collective-permute-start.5 = (bf16[64,512]{1,0:T(8,128)(2,1)S(1)}, bf16[64,512]{1,0:T(8,128)(2,1)S(1)}, u32[]{:S(2)}, u32[]{:S(2)}) collective-permute-start(bf16[64,512]{1,0:T(8,128)(2,1)S(1)} %fusion.7.grad_ref), channel_id=1, source_target_pairs={{0,1},{1,0},{2,3},{3,2},{4,5},{5,4},{6,7},{7,6},{8,9},{9,8},{10,11... | collective-permute-start | bytes 196616 | tf_op jit(solution)/shard_map/ppermute | solution.py:208
  28.7 0.8 %collective-permute-done.9.rest_ref = bf16[64,512]{1,0:T(8,128)(2,1)S(1)} collective-permute-done((bf16[64,512]{1,0:T(8,128)(2,1)S(1)}, bf16[64,512]{1,0:T(8,128)(2,1)S(1)}, u32[]{:S(2)}, u32[]{:S(2)}) %collective-permute-start.9) | collective-permute-done | bytes 65568 | tf_op jit(solution)/shard_map/ppermute | solution.py:208
  29.6 0.0 copy-done
  29.6 0.0 copy-done.1
  29.6 0.8 %update.2 = (f32[128,512]{1,0:T(8,128)}, f32[128,512]{1,0:T(8,128)}) custom-call(bf16[64,512]{1,0:T(8,128)(2,1)S(1)} %fusion.3.grad_ref, bf16[64,512]{1,0:T(8,128)(2,1)S(1)} %collective-permute-done.9.rest_ref, f32[128,512]{1,0:T(8,128)S(1)} %copy-done, f32[128,512]{1,0:T(8,128)S(1)} %copy-done.1), custom_call_target="tpu_custom_call" | custom-call | tf_op jit(solution)/shard_map/update/pallas_call | solution.py:188
  30.3 0.9 %collective-permute-done.5.rest_ref = bf16[64,512]{1,0:T(8,128)(2,1)S(1)} collective-permute-done((bf16[64,512]{1,0:T(8,128)(2,1)S(1)}, bf16[64,512]{1,0:T(8,128)(2,1)S(1)}, u32[]{:S(2)}, u32[]{:S(2)}) %collective-permute-start.5) | collective-permute-done | bytes 65568 | tf_op jit(solution)/shard_map/ppermute | solution.py:208
  31.2 0.8 %update.3 = (f32[128,512]{1,0:T(8,128)}, f32[128,512]{1,0:T(8,128)}) custom-call(bf16[64,512]{1,0:T(8,128)(2,1)S(1)} %fusion.7.grad_ref, bf16[64,512]{1,0:T(8,128)(2,1)S(1)} %collective-permute-done.5.rest_ref, f32[128,512]{1,0:T(8,128)S(1)} %copy-done, f32[128,512]{1,0:T(8,128)S(1)} %copy-done.1, ...), custom_call_target="tpu_custom_call", output_to_operand_aliasing={{0}: (4, {}), {1}: (5, {})} | custom-call | tf_op jit(solution)/shard_map/update/pallas_call | solution.py:188
  (7 shorter events, 0.2 us)
Async XLA Ops:
  3.2 2.1 %collective-permute-start = (bf16[512,512]{1,0:T(8,128)(2,1)S(1)}, bf16[512,512]{1,0:T(8,128)(2,1)S(1)}, u32[]{:S(2)}, u32[]{:S(2)}) collective-permute-start(bf16[512,512]{1,0:T(8,128)(2,1)S(1)} %pad_maximum_fusion), channel_id=1, source_target_pairs={{0,2},{1,3},{2,0},{3,1},{4,6},{5,7},{6,4},{7,5},{8,10},{9,11},{10,... | collective-permute-start | bytes 1572872 | tf_op jit(solution)/shard_map/ppermute | solution.py:208
  3.8 4.8 %collective-permute-start.1 = (bf16[392,1024]{1,0:T(8,128)(2,1)S(1)}, bf16[392,1024]{1,0:T(8,128)(2,1)S(1)}, u32[]{:S(2)}, u32[]{:S(2)}) collective-permute-start(bf16[392,1024]{1,0:T(8,128)(2,1)S(1)} %get-tuple-element.21.loan_ref), channel_id=1, source_target_pairs={{0,2},{1,3},{2,0},{3,1},{4,6},{5,7},{6,4},{7,5},{8,10},{9,11},{10,... | collective-permute-start | bytes 2408456 | tf_op jit(solution)/shard_map/ppermute | solution.py:208
  5.4 7.4 %collective-permute-start.6 = (bf16[256,512]{1,0:T(8,128)(2,1)S(1)}, bf16[256,512]{1,0:T(8,128)(2,1)S(1)}, u32[]{:S(2)}, u32[]{:S(2)}) collective-permute-start(bf16[256,512]{1,0:T(8,128)(2,1)S(1)} %get-tuple-element.34), channel_id=1, source_target_pairs={{0,8},{1,9},{2,6},{3,7},{4,12},{5,13},{6,2},{7,3},{8,0},{9,1},{10,... | collective-permute-start | bytes 786440 | tf_op jit(solution)/shard_map/ppermute | solution.py:208
  8.4 7.6 %collective-permute-start.2 = (bf16[256,512]{1,0:T(8,128)(2,1)S(1)}, bf16[256,512]{1,0:T(8,128)(2,1)S(1)}, u32[]{:S(2)}, u32[]{:S(2)}) collective-permute-start(bf16[256,512]{1,0:T(8,128)(2,1)S(1)} %get-tuple-element.32), channel_id=1, source_target_pairs={{0,8},{1,9},{2,6},{3,7},{4,12},{5,13},{6,2},{7,3},{8,0},{9,1},{10,... | collective-permute-start | bytes 786440 | tf_op jit(solution)/shard_map/ppermute | solution.py:208
  11.7 17.9 %copy-start = (f32[128,512]{1,0:T(8,128)S(1)}, f32[128,512]{1,0:T(8,128)}, u32[]{:S(2)}) copy-start(f32[128,512]{1,0:T(8,128)} %velocity_ref.1) | copy-start | bytes 786436
  11.7 17.9 %copy-start.1 = (f32[128,512]{1,0:T(8,128)S(1)}, f32[128,512]{1,0:T(8,128)}, u32[]{:S(2)}) copy-start(f32[128,512]{1,0:T(8,128)} %weight_ref.1) | copy-start | bytes 786436
  12.8 5.6 %collective-permute-start.7 = (bf16[2,64,512]{2,1,0:T(8,128)(2,1)S(1)}, bf16[2,64,512]{2,1,0:T(8,128)(2,1)S(1)}, u32[]{:S(2)}, u32[]{:S(2)}) collective-permute-start(bf16[2,64,512]{2,1,0:T(8,128)(2,1)S(1)} %fusion.1), channel_id=1, source_target_pairs={{0,4},{1,5},{2,10},{3,11},{4,0},{5,1},{6,14},{7,15},{8,12},{9,13},... | collective-permute-start | bytes 393224 | tf_op jit(solution)/shard_map/ppermute | solution.py:208
  16.1 5.3 %collective-permute-start.3 = (bf16[2,64,512]{2,1,0:T(8,128)(2,1)S(1)}, bf16[2,64,512]{2,1,0:T(8,128)(2,1)S(1)}, u32[]{:S(2)}, u32[]{:S(2)}) collective-permute-start(bf16[2,64,512]{2,1,0:T(8,128)(2,1)S(1)} %fusion), channel_id=1, source_target_pairs={{0,4},{1,5},{2,10},{3,11},{4,0},{5,1},{6,14},{7,15},{8,12},{9,13},... | collective-permute-start | bytes 393224 | tf_op jit(solution)/shard_map/ppermute | solution.py:208
  18.5 6.1 %collective-permute-start.8 = (bf16[64,512]{1,0:T(8,128)(2,1)S(1)}, bf16[64,512]{1,0:T(8,128)(2,1)S(1)}, u32[]{:S(2)}, u32[]{:S(2)}) collective-permute-start(bf16[64,512]{1,0:T(8,128)(2,1)S(1)} %fusion.4), channel_id=1, source_target_pairs={{0,16},{1,17},{2,18},{3,19},{4,20},{5,21},{6,22},{7,23},{8,24},{9,... | collective-permute-start | bytes 196616 | tf_op jit(solution)/shard_map/ppermute | solution.py:208
  21.4 5.4 %collective-permute-start.4 = (bf16[64,512]{1,0:T(8,128)(2,1)S(1)}, bf16[64,512]{1,0:T(8,128)(2,1)S(1)}, u32[]{:S(2)}, u32[]{:S(2)}) collective-permute-start(bf16[64,512]{1,0:T(8,128)(2,1)S(1)} %fusion.5), channel_id=1, source_target_pairs={{0,16},{1,17},{2,18},{3,19},{4,20},{5,21},{6,22},{7,23},{8,24},{9,... | collective-permute-start | bytes 196616 | tf_op jit(solution)/shard_map/ppermute | solution.py:208
  24.6 5.0 %collective-permute-start.9 = (bf16[64,512]{1,0:T(8,128)(2,1)S(1)}, bf16[64,512]{1,0:T(8,128)(2,1)S(1)}, u32[]{:S(2)}, u32[]{:S(2)}) collective-permute-start(bf16[64,512]{1,0:T(8,128)(2,1)S(1)} %fusion.3.grad_ref), channel_id=1, source_target_pairs={{0,1},{1,0},{2,3},{3,2},{4,5},{5,4},{6,7},{7,6},{8,9},{9,8},{10,11... | collective-permute-start | bytes 196616 | tf_op jit(solution)/shard_map/ppermute | solution.py:208
  26.9 4.3 %collective-permute-start.5 = (bf16[64,512]{1,0:T(8,128)(2,1)S(1)}, bf16[64,512]{1,0:T(8,128)(2,1)S(1)}, u32[]{:S(2)}, u32[]{:S(2)}) collective-permute-start(bf16[64,512]{1,0:T(8,128)(2,1)S(1)} %fusion.7.grad_ref), channel_id=1, source_target_pairs={{0,1},{1,0},{2,3},{3,2},{4,5},{5,4},{6,7},{7,6},{8,9},{9,8},{10,11... | collective-permute-start | bytes 196616 | tf_op jit(solution)/shard_map/ppermute | solution.py:208
